TPU v7x, 32 devices: a whole 2x2x4 slice. The times are simulated.
32 devices in a mesh: seq: 8 (over y, x, core), head: 4 (over z).
Axes of the slice: x: 2, y: 2, z: 4, core: 2. Of those that a mesh axis runs over, the one named last changes fastest.
Arguments:
- queries: bfloat16 [9216, 5120], P(('seq', 'head')), may hold values from -120 to 120
- key_vectors: bfloat16 [9216, 5120], P(('seq', 'head')), may hold values from -20 to 20
- value_vectors: bfloat16 [9216, 5120], P(('seq', 'head')), may hold values from -6 to 6
- reach_time: int32 [24], P('seq'), may hold values from 0 to 1
- reach_width: int32 [24], P('seq'), may hold values from 0 to 2
- keep_mask: int32 [9216, 40], P('seq', 'head'), may hold values 0 or 1
Outputs:
- attended: bfloat16 [9216, 5120], P(('seq', 'head'))
All inputs are finite; a program needn't handle non-finite values. No bound on the sum of `keep_mask` on one device may be relied on, other than what follows from the above.
Results may differ from a plain program's by a relative error of at most 0.0046.
Values may be sent and summed in bfloat16 or wider, within the bound.
No kernel may reach another device: no remote copies, remote signals or barrier semaphores. Data moves between devices by JAX's collectives and lax.ppermute only.
A program may use at most 128 MiB of HBM per device.

v0:
```python
import functools
import math

import jax
import jax.numpy as jnp
from jax import lax
from jax.experimental import pallas as pl
from jax.experimental.pallas import tpu as pltpu
from jax.sharding import PartitionSpec as P

LANES = 128
LARGEST_CHUNK = 4
ANY = pl.BlockSpec(memory_space=pl.ANY)
VMEM_LIMIT = 60 * 2**20


def tile_mask(reach_t, reach_w, slab_index, slab_count):
    tile_count = reach_t.shape[0]
    places = jnp.arange(tile_count, dtype=jnp.int32)
    columns = jnp.arange(3 * tile_count, dtype=jnp.int32)
    offsets = columns // tile_count - 1
    key_place = columns % tile_count
    inside = (slab_index + offsets >= 0) & (slab_index + offsets < slab_count)
    near_time = jnp.abs(offsets)[None, :] <= reach_t[:, None]
    near_width = jnp.abs(key_place[None, :] - places[:, None]) <= reach_w[:, None]
    return near_time & near_width & inside[None, :]


def staged(pairs, stages, sems):
    arriving, leaving = [], []
    for i, (source, target) in enumerate(pairs):
        arriving.append(pltpu.make_async_copy(source, stages[i], sems.at[0, i]))
        leaving.append(pltpu.make_async_copy(stages[i], target, sems.at[1, i]))
    for copy in arriving:
        copy.start()
    for first, second in zip(arriving, leaving):
        first.wait()
        second.start()
    for copy in leaving:
        copy.wait()


def stage_shapes(shapes):
    return [pltpu.VMEM(shape, jnp.bfloat16) for shape in shapes] + [
        pltpu.SemaphoreType.DMA((2, len(shapes)))
    ]


def pack(arrays, after, groups, group_width, start, width):
    rows = arrays[0].shape[0]

    def kernel(*refs):
        sources, out = refs[: len(arrays)], refs[len(arrays) + len(after)]
        stages, sems = refs[len(arrays) + len(after) + 1 : -1], refs[-1]
        pairs = []
        for group in range(groups):
            columns = pl.ds(group * group_width + start, width)
            for i, source in enumerate(sources):
                pairs.append((source.at[:, columns], out.at[group, :, pl.ds(i * width, width)]))
        staged(pairs, stages, sems)

    return pl.pallas_call(
        kernel,
        in_specs=[ANY] * (len(arrays) + len(after)),
        out_specs=ANY,
        out_shape=jax.ShapeDtypeStruct((groups, rows, len(arrays) * width), jnp.bfloat16),
        scratch_shapes=stage_shapes([(rows, width)] * (len(arrays) * groups)),
        cost_estimate=pl.CostEstimate(
            flops=0,
            bytes_accessed=4 * len(arrays) * groups * rows * width,
            transcendentals=0,
        ),
        compiler_params=pltpu.CompilerParams(vmem_limit_bytes=VMEM_LIMIT),
        name="pack",
    )(*arrays, *after)


def pack_turned(array, after, groups, group_width, start, width):
    rows = array.shape[0]

    def kernel(*refs):
        outs = refs[1 + len(after) : 1 + len(after) + groups]
        stages, sems = refs[1 + len(after) + groups : -1], refs[-1]
        me = lax.axis_index("head")
        pairs = []
        for shift in range(groups):
            group = lax.rem(me + shift, groups)
            column = pl.multiple_of(group * group_width + start, LANES)
            pairs.append((refs[0].at[:, pl.ds(column, width)], outs[shift]))
        staged(pairs, stages, sems)

    return pl.pallas_call(
        kernel,
        in_specs=[ANY] * (1 + len(after)),
        out_specs=[ANY] * groups,
        out_shape=[jax.ShapeDtypeStruct((rows, width), jnp.bfloat16)] * groups,
        scratch_shapes=stage_shapes([(rows, width)] * groups),
        cost_estimate=pl.CostEstimate(
            flops=0, bytes_accessed=4 * groups * rows * width, transcendentals=0
        ),
        compiler_params=pltpu.CompilerParams(vmem_limit_bytes=VMEM_LIMIT),
        name="pack_turned",
    )(array, *after)


def gate(array, after):
    def kernel(*refs):
        del refs

    return pl.pallas_call(
        kernel,
        in_specs=[ANY] * (1 + len(after)),
        out_specs=ANY,
        out_shape=jax.ShapeDtypeStruct(array.shape, array.dtype),
        input_output_aliases={0: 0},
        compiler_params=pltpu.CompilerParams(vmem_limit_bytes=VMEM_LIMIT),
        name="gate",
    )(array, *after)


def place(chunks, group_width, total_width, target=None):
    groups = len(chunks[0][1])
    rows = chunks[0][1][0].shape[0]
    blocks = [block for _, parts in chunks for block in parts]
    extra = [] if target is None else [target]

    def kernel(*refs):
        out = refs[len(blocks) + len(extra)]
        stages, sems = refs[len(blocks) + len(extra) + 1 : -1], refs[-1]
        me = lax.axis_index("head")
        pairs = []
        for i, (start, parts) in enumerate(chunks):
            for shift, part in enumerate(parts):
                group = lax.rem(me + shift, groups)
                column = pl.multiple_of(group * group_width + start, LANES)
                pairs.append((refs[i * groups + shift], out.at[:, pl.ds(column, part.shape[1])]))
        staged(pairs, stages, sems)

    return pl.pallas_call(
        kernel,
        in_specs=[ANY] * (len(blocks) + len(extra)),
        out_specs=ANY,
        out_shape=jax.ShapeDtypeStruct((rows, total_width), jnp.bfloat16),
        scratch_shapes=stage_shapes([block.shape for block in blocks]),
        input_output_aliases={len(blocks): 0} if extra else {},
        cost_estimate=pl.CostEstimate(
            flops=0,
            bytes_accessed=4 * rows * sum(block.shape[1] for block in blocks),
            transcendentals=0,
        ),
        compiler_params=pltpu.CompilerParams(vmem_limit_bytes=VMEM_LIMIT),
        name="place",
    )(*blocks, *extra)


def lane_fold(op, wide):
    folded = wide[:, :LANES]
    for start in range(LANES, wide.shape[1], LANES):
        folded = op(folded, wide[:, start : start + LANES])
    return folded


def attend_kernel(groups, heads, first_head, tile_count, in_pieces, *refs):
    plan_ref, own_ref, prev_ref, next_ref, keep_ref = refs[:5]
    pieces = refs[5 : 5 + groups] if in_pieces else ()
    outs = refs[-6 - groups : -6]
    q_ref, out_ref, scores_ref, top_ref, total_ref, sum_ref = refs[-6:]
    slab_rows, width = out_ref.shape
    local_rows = slab_rows // groups
    head_size = width // heads
    tile_rows = slab_rows // tile_count
    scale = math.log2(math.e) / math.sqrt(head_size)
    slabs = ((0, prev_ref), (1, own_ref), (2, next_ref))
    me = lax.axis_index("head")

    def owner_rows(shift):
        owner = lax.rem(me + groups - shift, groups)
        return pl.ds(pl.multiple_of(owner * local_rows, 16), local_rows)

    def tile(index):
        return pl.ds(pl.multiple_of(index * tile_rows, tile_rows), tile_rows)

    def lanes(index):
        return pl.ds(index * head_size, head_size)

    for shift, piece in enumerate(pieces):
        q_ref[owner_rows(shift), :] = piece[...]
    query_ref, first_query = (q_ref, 0) if pieces else (own_ref, 2 * heads)

    def one_tile(i, carry):
        top_ref[...] = jnp.full_like(top_ref, -jnp.inf)
        total_ref[...] = jnp.zeros_like(total_ref)
        sum_ref[...] = jnp.zeros_like(sum_ref)

        for slab, pair_ref in slabs:

            def score(place, carry, slab=slab, pair_ref=pair_ref):
                column = slab * tile_count + place

                @pl.when(plan_ref[i * 3 * tile_count + column] > 0)
                def _():
                    for h in range(heads):
                        found = lax.dot_general(
                            query_ref[tile(i), lanes(first_query + h)],
                            pair_ref[tile(place), lanes(h)],
                            (((1,), (1,)), ((), ())),
                            preferred_element_type=jnp.float32,
                        )
                        scores_ref[h, column] = found
                        top_ref[h] = jnp.maximum(top_ref[h], lane_fold(jnp.maximum, found))

                return carry

            lax.fori_loop(0, tile_count, score, 0)

        for h in range(heads):
            highest = jnp.max(top_ref[h], axis=1, keepdims=True) * scale
            top_ref[h] = jnp.broadcast_to(highest, top_ref.shape[1:])

        for slab, pair_ref in slabs:

            def weigh(place, carry, slab=slab, pair_ref=pair_ref):
                column = slab * tile_count + place

                @pl.when(plan_ref[i * 3 * tile_count + column] > 0)
                def _():
                    for h in range(heads):
                        highest = jnp.concatenate([top_ref[h]] * (tile_rows // LANES), axis=1)
                        weights = jnp.exp2(scores_ref[h, column] * scale - highest)
                        total_ref[h] += lane_fold(jnp.add, weights)
                        sum_ref[h] += jnp.dot(
                            weights.astype(jnp.bfloat16),
                            pair_ref[tile(place), lanes(heads + h)],
                            preferred_element_type=jnp.float32,
                        )

                return carry

            lax.fori_loop(0, tile_count, weigh, 0)

        keep = keep_ref[tile(i), :].astype(jnp.float32)
        numbers = lax.broadcasted_iota(jnp.int32, keep.shape, 1)
        for h in range(heads):
            totals = jnp.sum(total_ref[h], axis=1, keepdims=True)
            mine = jnp.where(numbers == first_head + h, keep, 0.0)
            factor = jnp.sum(mine, axis=1, keepdims=True) * (10.0 / 9.0)
            out_ref[tile(i), lanes(h)] = (sum_ref[h] * (factor / totals)).astype(out_ref.dtype)
        return carry

    lax.fori_loop(0, tile_count, one_tile, 0)

    for shift in range(groups):
        outs[shift][...] = out_ref[owner_rows(shift), :]


def attend(
    plan, own, prev, behind, keep_mask, pieces, after, groups, first_head, heads, tile_count
):
    slab_rows, width = prev.shape[0], prev.shape[1] // 2
    local_rows = slab_rows // groups
    tile_rows = slab_rows // tile_count
    head_size = width // heads
    pairs = heads * slab_rows * 3 * slab_rows
    wholes = [
        pl.BlockSpec(array.shape, lambda s, plan: (0, 0))
        for array in (own, prev, behind, keep_mask, *pieces)
    ]
    accumulator = pltpu.VMEM((heads, tile_rows, LANES), jnp.float32)
    return pl.pallas_call(
        functools.partial(attend_kernel, groups, heads, first_head, tile_count, bool(pieces)),
        grid_spec=pltpu.PrefetchScalarGridSpec(
            num_scalar_prefetch=1,
            grid=(1,),
            in_specs=wholes + [ANY] * len(after),
            out_specs=[pl.BlockSpec((local_rows, width), lambda s, plan: (0, 0))] * groups,
            scratch_shapes=[
                pltpu.VMEM((slab_rows, width), jnp.bfloat16),
                pltpu.VMEM((slab_rows, width), jnp.bfloat16),
                pltpu.VMEM((heads, 3 * tile_count, tile_rows, tile_rows), jnp.float32),
                accumulator,
                accumulator,
                pltpu.VMEM((heads, tile_rows, head_size), jnp.float32),
            ],
        ),
        out_shape=[jax.ShapeDtypeStruct((local_rows, width), jnp.bfloat16)] * groups,
        compiler_params=pltpu.CompilerParams(vmem_limit_bytes=VMEM_LIMIT),
        cost_estimate=pl.CostEstimate(
            flops=16 * pairs * head_size,
            bytes_accessed=16 * slab_rows * width,
            transcendentals=pairs,
        ),
        name="attend",
    )(plan, own, prev, behind, keep_mask, *pieces, *after)


def on_device(queries, key_vectors, value_vectors, reach_time, reach_width, keep_mask):
    groups = lax.axis_size("head")
    slab_count = lax.axis_size("seq")
    total_width = queries.shape[1]
    group_heads = keep_mask.shape[1]
    group_width = total_width // groups
    head_size = group_width // group_heads
    tile_count = reach_time.shape[0]
    allowed = tile_mask(reach_time, reach_width, lax.axis_index("seq"), slab_count)
    plan = allowed.astype(jnp.int32).reshape(-1)
    onward = [(i, i + 1) for i in range(slab_count - 1)]
    backward = [(i + 1, i) for i in range(slab_count - 1)]

    def turn(array, shift):
        return lax.ppermute(array, "head", [(i, (i + shift) % groups) for i in range(groups)])

    sizes, left = [], group_heads
    while left:
        sizes.append(min(len(sizes) + 1, LARGEST_CHUNK, left))
        left -= sizes[-1]
    sizes.sort(reverse=True)
    count = len(sizes)
    firsts = [sum(sizes[:i]) for i in range(count)]

    def packed(i, after):
        arrays = (key_vectors, value_vectors, queries)[: 2 + (i + 1 == count)]
        start, width = firsts[i] * head_size, sizes[i] * head_size
        return pack(arrays, after, groups, group_width, start, width)

    def asked(i, after):
        start, width = firsts[i] * head_size, sizes[i] * head_size
        blocks = pack_turned(queries, after, groups, group_width, start, width)
        return [blocks[0]] + [turn(blocks[shift], shift) for shift in range(1, groups)]

    def arrive(i, after):
        own = lax.all_to_all(sent[i], "head", split_axis=0, concat_axis=0, tiled=True)
        own = gate(own, after) if after else own
        own = own.reshape(-1, own.shape[2])
        pairs = own[:, : 2 * sizes[i] * head_size]
        return own, lax.ppermute(pairs, "seq", onward), lax.ppermute(pairs, "seq", backward)

    sent, there, asks, done, early = [packed(0, [])], [], [], [], None
    there.append(arrive(0, []))
    if count > 1:
        asks.append(asked(0, sent))
        sent.append(gate(packed(1, sent), there[0][:1]))
    for i, heads in enumerate(sizes):
        if i + 1 < count:
            there.append(arrive(i + 1, [part[1][0] for part in done[-1:]]))
        if i == 0 and count > 2:
            asks.append(asked(1, there[0][1:]))
        if i + 2 < count:
            behind = there[i + 1][:1] + tuple(asks[1][:1] if i == 0 else [])
            sent.append(gate(packed(i + 2, there[i][:1]), behind))
        if i and i + 2 < count:
            asks.append(asked(i + 1, sent[i + 2 :] + done[i - 1][1][1:]))
        hold = [part[0] for part in there[i + 1 :] + asks[i + 1 :]] + sent[i + 2 :]
        hold += [part[1][0] for part in done[-1:]]
        if i + 1 == count and count > 2:
            early = place(done[:-1], group_width, total_width)
            hold.append(early)
        pieces = asks[i] if i + 1 < count else []
        outs = attend(
            plan, *there[i], keep_mask, pieces, hold, groups, firsts[i], heads, tile_count
        )
        back = [outs[0]] + [turn(outs[shift], groups - shift) for shift in range(1, groups)]
        done.append((firsts[i] * head_size, back))
    return place(done[-2:] if count > 2 else done, group_width, total_width, early)


def solution(mesh):
    return jax.shard_map(
        on_device,
        mesh=mesh,
        in_specs=(
            P(("seq", "head"), None),
            P(("seq", "head"), None),
            P(("seq", "head"), None),
            P("seq"),
            P("seq"),
            P("seq", "head"),
        ),
        out_specs=P(("seq", "head"), None),
        check_vma=False,
    )
```

profile of v0, /device:TPU:4, one launch (start us, length us, event | category | flops | bytes accessed | tf_op | source)
XLA Modules:
  0.0 328.1 jit_solution(16118320026825402426)
XLA Ops:
  0.0 2.5 pack.4.refs_2_.refs_1_
  2.5 4.9 %all-to-all-start = ((bf16[4,288,1024]{2,1,0:T(8,128)(2,1)}), bf16[4,288,1024]{2,1,0:T(8,128)(2,1)S(1)}, u32[]{:S(2)}, u32[]{:S(2)}) async-start(bf16[4,288,1024]{2,1,0:T(8,128)(2,1)} %pack.4.refs_2_.refs_1_), calls=%async_computation | async-start | bytes 4718592 | tf_op jit(solution)/shard_map/all_to_all | solution.py:331
  7.4 2.4 pack.6.refs_0_
  9.8 51.4 %all-to-all-done = bf16[4,288,1024]{2,1,0:T(8,128)(2,1)S(1)} async-done(((bf16[4,288,1024]{2,1,0:T(8,128)(2,1)}), bf16[4,288,1024]{2,1,0:T(8,128)(2,1)S(1)}, u32[]{:S(2)}, u32[]{:S(2)}) %all-to-all-start) | async-done | bytes 2359328 | tf_op jit(solution)/shard_map/all_to_all | solution.py:331
  62.6 4.6 %all-to-all-start.1 = ((bf16[4,288,768]{2,1,0:T(8,128)(2,1)}), bf16[4,288,768]{2,1,0:T(8,128)(2,1)}, u32[]{:S(2)}, u32[]{:S(2)}) async-start(bf16[4,288,768]{2,1,0:T(8,128)(2,1)} %gate.5), calls=%async_computation.1 | async-start | bytes 3538944 | tf_op jit(solution)/shard_map/all_to_all | solution.py:331
  67.2 2.1 collective-permute-start
  69.3 4.5 %collective-permute-start.1 = (bf16[1152,1024]{1,0:T(8,128)(2,1)S(1)}, bf16[1152,1024]{1,0:T(8,128)(2,1)}, u32[]{:S(2)}, u32[]{:S(2)}) collective-permute-start(bf16[1152,1024]{1,0:T(8,128)(2,1)S(1)} %bitcast.8), channel_id=1, source_target_pairs={{4,0},{8,4},{12,8},{16,12},{20,16},{24,20},{28,24},{5,1},{9,5},{13... | collective-permute-start | bytes 7077896 | tf_op jit(solution)/shard_map/ppermute | solution.py:335
  73.9 2.1 pack_turned.4
  77.9 2.4 collective-permute-start.3
  83.5 2.2 pack.5.refs_0_
  85.7 35.3 %collective-permute-done.refs_1_.refs_2_ = bf16[1152,1024]{1,0:T(8,128)(2,1)} collective-permute-done((bf16[1152,1024]{1,0:T(8,128)(2,1)S(1)}, bf16[1152,1024]{1,0:T(8,128)(2,1)}, u32[]{:S(2)}, u32[]{:S(2)}) %collective-permute-start) | collective-permute-done | bytes 2359328 | tf_op jit(solution)/shard_map/ppermute | solution.py:335
  125.8 5.0 %collective-permute-start.14 = (bf16[1152,768]{1,0:T(8,128)(2,1)}, bf16[1152,768]{1,0:T(8,128)(2,1)}, u32[]{:S(2)}, u32[]{:S(2)}) collective-permute-start(bf16[1152,768]{1,0:T(8,128)(2,1)} %bitcast.1.refs_1_.refs_9_.refs_3_), channel_id=1, source_target_pairs={{4,0},{8,4},{12,8},{16,12},{20,16},{24,20},{28,24},{5,1},{9,5},{13... | collective-permute-start | bytes 5308424 | tf_op jit(solution)/shard_map/ppermute | solution.py:335
  130.8 4.8 %all-to-all-start.2 = ((bf16[4,288,512]{2,1,0:T(8,128)(2,1)}), bf16[4,288,512]{2,1,0:T(8,128)(2,1)S(1)}, u32[]{:S(2)}, u32[]{:S(2)}) async-start(bf16[4,288,512]{2,1,0:T(8,128)(2,1)} %gate.6.refs_11_), calls=%async_computation.2 | async-start | bytes 2359296 | tf_op jit(solution)/shard_map/all_to_all | solution.py:331
  136.6 24.2 %attend.4 = (bf16[288,512]{1,0:T(8,128)(2,1)}, bf16[288,512]{1,0:T(8,128)(2,1)}, bf16[288,512]{1,0:T(8,128)(2,1)}, bf16[288,512]{1,0:T(8,128)(2,1)}) custom-call(s32[27]{0:T(128)} %reshape.58.refs_0_, bf16[1152,1024]{1,0:T(8,128)(2,1)} %bitcast.6, bf16[1152,1024]{1,0:T(8,128)(2,1)} %collective-permute-done.refs_1_.refs_2_, ...), custom_call_target="tpu_custom_call" | custom-call | flops 32614907904 | bytes 9437184 | tf_op jit(solution)/shard_map/attend/pallas_call | solution.py:269
  160.8 3.8 %collective-permute-start.7 = (bf16[288,512]{1,0:T(8,128)(2,1)}, bf16[288,512]{1,0:T(8,128)(2,1)S(1)}, u32[]{:S(2)}, u32[]{:S(2)}) collective-permute-start(bf16[288,512]{1,0:T(8,128)(2,1)} %get-tuple-element.39), channel_id=1, source_target_pairs={{0,3},{1,0},{2,1},{3,2},{4,7},{5,4},{6,5},{7,6},{8,11},{9,8},{10,9... | collective-permute-start | bytes 884744 | tf_op jit(solution)/shard_map/ppermute | solution.py:310
  165.8 6.7 %collective-permute-done.7.refs_2_.refs_1_ = bf16[288,512]{1,0:T(8,128)(2,1)S(1)} collective-permute-done((bf16[288,512]{1,0:T(8,128)(2,1)}, bf16[288,512]{1,0:T(8,128)(2,1)S(1)}, u32[]{:S(2)}, u32[]{:S(2)}) %collective-permute-start.7) | collective-permute-done | bytes 294944 | tf_op jit(solution)/shard_map/ppermute | solution.py:310
  172.4 19.5 %collective-permute-start.15 = (bf16[288,384]{1,0:T(8,128)(2,1)S(1)}, bf16[288,384]{1,0:T(8,128)(2,1)}, u32[]{:S(2)}, u32[]{:S(2)}) collective-permute-start(bf16[288,384]{1,0:T(8,128)(2,1)S(1)} %copy-done.24), channel_id=1, source_target_pairs={{0,1},{1,2},{2,3},{3,0},{4,5},{5,6},{6,7},{7,4},{8,9},{9,10},{10,1... | collective-permute-start | bytes 663560 | tf_op jit(solution)/shard_map/ppermute | solution.py:310
  191.9 3.1 collective-permute-done.8.refs_3_.refs_2_
  195.1 2.3 pack.7.refs_0_
  198.5 5.4 %all-to-all-start.3 = ((bf16[4,288,384]{2,1,0:T(8,128)(2,1)}), bf16[4,288,384]{2,1,0:T(8,128)(2,1)S(1)}, u32[]{:S(2)}, u32[]{:S(2)}) async-start(bf16[4,288,384]{2,1,0:T(8,128)(2,1)} %gate.8.refs_1_.refs_11_), calls=%async_computation.3 | async-start | bytes 1769472 | tf_op jit(solution)/shard_map/all_to_all | solution.py:331
  207.8 5.0 %collective-permute-start.6 = (bf16[1152,512]{1,0:T(8,128)(2,1)S(1)}, bf16[1152,512]{1,0:T(8,128)(2,1)}, u32[]{:S(2)}, u32[]{:S(2)}) collective-permute-start(bf16[1152,512]{1,0:T(8,128)(2,1)S(1)} %bitcast.13), channel_id=1, source_target_pairs={{4,0},{8,4},{12,8},{16,12},{20,16},{24,20},{28,24},{5,1},{9,5},{13... | collective-permute-start | bytes 3538952 | tf_op jit(solution)/shard_map/ppermute | solution.py:335
  212.9 19.9 %attend.5 = (bf16[288,384]{1,0:T(8,128)(2,1)}, bf16[288,384]{1,0:T(8,128)(2,1)}, bf16[288,384]{1,0:T(8,128)(2,1)}, bf16[288,384]{1,0:T(8,128)(2,1)}) custom-call(s32[27]{0:T(128)} %reshape.58.refs_0_, bf16[1152,768]{1,0:T(8,128)(2,1)} %bitcast.1.refs_1_.refs_9_.refs_3_, bf16[1152,768]{1,0:T(8,128)(2,1)} %collective-permute-done.13.refs_2_, ...), custom_call_target="tpu_custom_call" | custom-call | flops 24461180928 | bytes 7077888 | tf_op jit(solution)/shard_map/attend/pallas_call | solution.py:269
  232.8 11.4 %collective-permute-start.23 = (bf16[288,384]{1,0:T(8,128)(2,1)}, bf16[288,384]{1,0:T(8,128)(2,1)S(1)}, u32[]{:S(2)}, u32[]{:S(2)}) collective-permute-start(bf16[288,384]{1,0:T(8,128)(2,1)} %get-tuple-element.54), channel_id=1, source_target_pairs={{0,3},{1,0},{2,1},{3,2},{4,7},{5,4},{6,5},{7,6},{8,11},{9,8},{10,9... | collective-permute-start | bytes 663560 | tf_op jit(solution)/shard_map/ppermute | solution.py:310
  244.7 5.6 %collective-permute-done.23.refs_5_ = bf16[288,384]{1,0:T(8,128)(2,1)S(1)} collective-permute-done((bf16[288,384]{1,0:T(8,128)(2,1)}, bf16[288,384]{1,0:T(8,128)(2,1)S(1)}, u32[]{:S(2)}, u32[]{:S(2)}) %collective-permute-start.23) | collective-permute-done | bytes 221216 | tf_op jit(solution)/shard_map/ppermute | solution.py:310
  250.3 19.0 %collective-permute-done.24.refs_6_ = bf16[288,384]{1,0:T(8,128)(2,1)S(1)} collective-permute-done((bf16[288,384]{1,0:T(8,128)(2,1)}, bf16[288,384]{1,0:T(8,128)(2,1)S(1)}, u32[]{:S(2)}, u32[]{:S(2)}) %collective-permute-start.24) | collective-permute-done | bytes 221216 | tf_op jit(solution)/shard_map/ppermute | solution.py:310
  270.1 2.4 place.2.refs_6_.refs_8_
  277.3 3.9 %collective-permute-start.22 = (bf16[1152,256]{1,0:T(8,128)(2,1)S(1)}, bf16[1152,256]{1,0:T(8,128)(2,1)}, u32[]{:S(2)}, u32[]{:S(2)}) collective-permute-start(bf16[1152,256]{1,0:T(8,128)(2,1)S(1)} %slice.4), channel_id=1, source_target_pairs={{4,0},{8,4},{12,8},{16,12},{20,16},{24,20},{28,24},{5,1},{9,5},{13... | collective-permute-start | bytes 1769480 | tf_op jit(solution)/shard_map/ppermute | solution.py:335
  282.3 15.8 %attend.6 = (bf16[288,256]{1,0:T(8,128)(2,1)}, bf16[288,256]{1,0:T(8,128)(2,1)}, bf16[288,256]{1,0:T(8,128)(2,1)}, bf16[288,256]{1,0:T(8,128)(2,1)}) custom-call(s32[27]{0:T(128)} %reshape.58.refs_0_, bf16[1152,512]{1,0:T(8,128)(2,1)} %bitcast.11, bf16[1152,512]{1,0:T(8,128)(2,1)} %copy-done.20, bf16[1152,512]{1,0:T(8,128)(2,1)} %collective-permute-done.6.refs_3_, ...), custom_call_target="tpu_custom_call" | custom-call | flops 16307453952 | bytes 4718592 | tf_op jit(solution)/shard_map/attend/pallas_call | solution.py:269
  298.0 3.6 %collective-permute-start.18 = (bf16[288,256]{1,0:T(8,128)(2,1)}, bf16[288,256]{1,0:T(8,128)(2,1)S(1)}, u32[]{:S(2)}, u32[]{:S(2)}) collective-permute-start(bf16[288,256]{1,0:T(8,128)(2,1)} %get-tuple-element.51), channel_id=1, source_target_pairs={{0,3},{1,0},{2,1},{3,2},{4,7},{5,4},{6,5},{7,6},{8,11},{9,8},{10,9... | collective-permute-start | bytes 442376 | tf_op jit(solution)/shard_map/ppermute | solution.py:310
  302.9 12.4 %attend.7 = (bf16[288,128]{1,0:T(8,128)(2,1)}, bf16[288,128]{1,0:T(8,128)(2,1)}, bf16[288,128]{1,0:T(8,128)(2,1)}, bf16[288,128]{1,0:T(8,128)(2,1)}) custom-call(s32[27]{0:T(128)} %reshape.58.refs_0_, bf16[1152,384]{1,0:T(8,128)(2,1)} %bitcast.16, bf16[1152,256]{1,0:T(8,128)(2,1)} %collective-permute-done.21.refs_2_, ...), custom_call_target="tpu_custom_call" | custom-call | flops 8153726976 | bytes 2359296 | tf_op jit(solution)/shard_map/attend/pallas_call | solution.py:269
  315.3 2.6 collective-permute-start.26
  320.4 3.1 collective-permute-done.27.refs_6_
  (108 shorter events, 33.8 us)
Async XLA Ops:
  2.5 58.7 %all-to-all-start = ((bf16[4,288,1024]{2,1,0:T(8,128)(2,1)}), bf16[4,288,1024]{2,1,0:T(8,128)(2,1)S(1)}, u32[]{:S(2)}, u32[]{:S(2)}) async-start(bf16[4,288,1024]{2,1,0:T(8,128)(2,1)} %pack.4.refs_2_.refs_1_), calls=%async_computation | async-start | bytes 4718592 | tf_op jit(solution)/shard_map/all_to_all | solution.py:331
  62.6 61.2 %all-to-all-start.1 = ((bf16[4,288,768]{2,1,0:T(8,128)(2,1)}), bf16[4,288,768]{2,1,0:T(8,128)(2,1)}, u32[]{:S(2)}, u32[]{:S(2)}) async-start(bf16[4,288,768]{2,1,0:T(8,128)(2,1)} %gate.5), calls=%async_computation.1 | async-start | bytes 3538944 | tf_op jit(solution)/shard_map/all_to_all | solution.py:331
  67.2 53.8 %collective-permute-start = (bf16[1152,1024]{1,0:T(8,128)(2,1)S(1)}, bf16[1152,1024]{1,0:T(8,128)(2,1)}, u32[]{:S(2)}, u32[]{:S(2)}) collective-permute-start(bf16[1152,1024]{1,0:T(8,128)(2,1)S(1)} %bitcast.7), channel_id=1, source_target_pairs={{0,4},{4,8},{8,12},{12,16},{16,20},{20,24},{24,28},{1,5},{5,9},{9,... | collective-permute-start | bytes 7077896 | tf_op jit(solution)/shard_map/ppermute | solution.py:335
  69.3 52.5 %collective-permute-start.1 = (bf16[1152,1024]{1,0:T(8,128)(2,1)S(1)}, bf16[1152,1024]{1,0:T(8,128)(2,1)}, u32[]{:S(2)}, u32[]{:S(2)}) collective-permute-start(bf16[1152,1024]{1,0:T(8,128)(2,1)S(1)} %bitcast.8), channel_id=1, source_target_pairs={{4,0},{8,4},{12,8},{16,12},{20,16},{24,20},{28,24},{5,1},{9,5},{13... | collective-permute-start | bytes 7077896 | tf_op jit(solution)/shard_map/ppermute | solution.py:335
  75.9 59.7 %collective-permute-start.2 = (bf16[288,512]{1,0:T(8,128)(2,1)}, bf16[288,512]{1,0:T(8,128)(2,1)S(1)}, u32[]{:S(2)}, u32[]{:S(2)}) collective-permute-start(bf16[288,512]{1,0:T(8,128)(2,1)} %get-tuple-element.35), channel_id=1, source_target_pairs={{0,1},{1,2},{2,3},{3,0},{4,5},{5,6},{6,7},{7,4},{8,9},{9,10},{10,1... | collective-permute-start | bytes 884744 | tf_op jit(solution)/shard_map/ppermute | solution.py:310
  77.9 57.8 %collective-permute-start.3 = (bf16[288,512]{1,0:T(8,128)(2,1)}, bf16[288,512]{1,0:T(8,128)(2,1)S(1)}, u32[]{:S(2)}, u32[]{:S(2)}) collective-permute-start(bf16[288,512]{1,0:T(8,128)(2,1)} %get-tuple-element.36), channel_id=1, source_target_pairs={{0,2},{1,3},{2,0},{3,1},{4,6},{5,7},{6,4},{7,5},{8,10},{9,11},{10,... | collective-permute-start | bytes 884744 | tf_op jit(solution)/shard_map/ppermute | solution.py:310
  80.3 55.4 %collective-permute-start.4 = (bf16[288,512]{1,0:T(8,128)(2,1)}, bf16[288,512]{1,0:T(8,128)(2,1)S(1)}, u32[]{:S(2)}, u32[]{:S(2)}) collective-permute-start(bf16[288,512]{1,0:T(8,128)(2,1)} %get-tuple-element.37), channel_id=1, source_target_pairs={{0,3},{1,0},{2,1},{3,2},{4,7},{5,4},{6,5},{7,6},{8,11},{9,8},{10,9... | collective-permute-start | bytes 884744 | tf_op jit(solution)/shard_map/ppermute | solution.py:310
  123.9 89.0 %collective-permute-start.13 = (bf16[1152,768]{1,0:T(8,128)(2,1)}, bf16[1152,768]{1,0:T(8,128)(2,1)}, u32[]{:S(2)}, u32[]{:S(2)}) collective-permute-start(bf16[1152,768]{1,0:T(8,128)(2,1)} %bitcast.1.refs_1_.refs_9_.refs_3_), channel_id=1, source_target_pairs={{0,4},{4,8},{8,12},{12,16},{16,20},{20,24},{24,28},{1,5},{5,9},{9,... | collective-permute-start | bytes 5308424 | tf_op jit(solution)/shard_map/ppermute | solution.py:335
  125.8 87.1 %collective-permute-start.14 = (bf16[1152,768]{1,0:T(8,128)(2,1)}, bf16[1152,768]{1,0:T(8,128)(2,1)}, u32[]{:S(2)}, u32[]{:S(2)}) collective-permute-start(bf16[1152,768]{1,0:T(8,128)(2,1)} %bitcast.1.refs_1_.refs_9_.refs_3_), channel_id=1, source_target_pairs={{4,0},{8,4},{12,8},{16,12},{20,16},{24,20},{28,24},{5,1},{9,5},{13... | collective-permute-start | bytes 5308424 | tf_op jit(solution)/shard_map/ppermute | solution.py:335
  130.8 66.6 %all-to-all-start.2 = ((bf16[4,288,512]{2,1,0:T(8,128)(2,1)}), bf16[4,288,512]{2,1,0:T(8,128)(2,1)S(1)}, u32[]{:S(2)}, u32[]{:S(2)}) async-start(bf16[4,288,512]{2,1,0:T(8,128)(2,1)} %gate.6.refs_11_), calls=%async_computation.2 | async-start | bytes 2359296 | tf_op jit(solution)/shard_map/all_to_all | solution.py:331
  160.8 11.6 %collective-permute-start.7 = (bf16[288,512]{1,0:T(8,128)(2,1)}, bf16[288,512]{1,0:T(8,128)(2,1)S(1)}, u32[]{:S(2)}, u32[]{:S(2)}) collective-permute-start(bf16[288,512]{1,0:T(8,128)(2,1)} %get-tuple-element.39), channel_id=1, source_target_pairs={{0,3},{1,0},{2,1},{3,2},{4,7},{5,4},{6,5},{7,6},{8,11},{9,8},{10,9... | collective-permute-start | bytes 884744 | tf_op jit(solution)/shard_map/ppermute | solution.py:310
  164.6 30.4 %collective-permute-start.8 = (bf16[288,512]{1,0:T(8,128)(2,1)}, bf16[288,512]{1,0:T(8,128)(2,1)S(1)}, u32[]{:S(2)}, u32[]{:S(2)}) collective-permute-start(bf16[288,512]{1,0:T(8,128)(2,1)} %get-tuple-element.40), channel_id=1, source_target_pairs={{0,2},{1,3},{2,0},{3,1},{4,6},{5,7},{6,4},{7,5},{8,10},{9,11},{10,... | collective-permute-start | bytes 884744 | tf_op jit(solution)/shard_map/ppermute | solution.py:310
  164.6 30.4 %collective-permute-start.9 = (bf16[288,512]{1,0:T(8,128)(2,1)}, bf16[288,512]{1,0:T(8,128)(2,1)S(1)}, u32[]{:S(2)}, u32[]{:S(2)}) collective-permute-start(bf16[288,512]{1,0:T(8,128)(2,1)} %get-tuple-element.41), channel_id=1, source_target_pairs={{0,1},{1,2},{2,3},{3,0},{4,5},{5,6},{6,7},{7,4},{8,9},{9,10},{10,1... | collective-permute-start | bytes 884744 | tf_op jit(solution)/shard_map/ppermute | solution.py:310
  172.4 33.4 %collective-permute-start.15 = (bf16[288,384]{1,0:T(8,128)(2,1)S(1)}, bf16[288,384]{1,0:T(8,128)(2,1)}, u32[]{:S(2)}, u32[]{:S(2)}) collective-permute-start(bf16[288,384]{1,0:T(8,128)(2,1)S(1)} %copy-done.24), channel_id=1, source_target_pairs={{0,1},{1,2},{2,3},{3,0},{4,5},{5,6},{6,7},{7,4},{8,9},{9,10},{10,1... | collective-permute-start | bytes 663560 | tf_op jit(solution)/shard_map/ppermute | solution.py:310
  195.0 12.8 %collective-permute-start.16 = (bf16[288,384]{1,0:T(8,128)(2,1)}, bf16[288,384]{1,0:T(8,128)(2,1)}, u32[]{:S(2)}, u32[]{:S(2)}) collective-permute-start(bf16[288,384]{1,0:T(8,128)(2,1)} %get-tuple-element.47), channel_id=1, source_target_pairs={{0,2},{1,3},{2,0},{3,1},{4,6},{5,7},{6,4},{7,5},{8,10},{9,11},{10,... | collective-permute-start | bytes 663560 | tf_op jit(solution)/shard_map/ppermute | solution.py:310
  195.0 17.8 %collective-permute-start.17 = (bf16[288,384]{1,0:T(8,128)(2,1)}, bf16[288,384]{1,0:T(8,128)(2,1)}, u32[]{:S(2)}, u32[]{:S(2)}) collective-permute-start(bf16[288,384]{1,0:T(8,128)(2,1)} %get-tuple-element.48), channel_id=1, source_target_pairs={{0,3},{1,0},{2,1},{3,2},{4,7},{5,4},{6,5},{7,6},{8,11},{9,8},{10,9... | collective-permute-start | bytes 663560 | tf_op jit(solution)/shard_map/ppermute | solution.py:310
  198.5 74.1 %all-to-all-start.3 = ((bf16[4,288,384]{2,1,0:T(8,128)(2,1)}), bf16[4,288,384]{2,1,0:T(8,128)(2,1)S(1)}, u32[]{:S(2)}, u32[]{:S(2)}) async-start(bf16[4,288,384]{2,1,0:T(8,128)(2,1)} %gate.8.refs_1_.refs_11_), calls=%async_computation.3 | async-start | bytes 1769472 | tf_op jit(solution)/shard_map/all_to_all | solution.py:331
  205.9 75.3 %collective-permute-start.5 = (bf16[1152,512]{1,0:T(8,128)(2,1)S(1)}, bf16[1152,512]{1,0:T(8,128)(2,1)S(1)}, u32[]{:S(2)}, u32[]{:S(2)}) collective-permute-start(bf16[1152,512]{1,0:T(8,128)(2,1)S(1)} %bitcast.12), channel_id=1, source_target_pairs={{0,4},{4,8},{8,12},{12,16},{16,20},{20,24},{24,28},{1,5},{5,9},{9,... | collective-permute-start | bytes 3538952 | tf_op jit(solution)/shard_map/ppermute | solution.py:335
  207.8 73.4 %collective-permute-start.6 = (bf16[1152,512]{1,0:T(8,128)(2,1)S(1)}, bf16[1152,512]{1,0:T(8,128)(2,1)}, u32[]{:S(2)}, u32[]{:S(2)}) collective-permute-start(bf16[1152,512]{1,0:T(8,128)(2,1)S(1)} %bitcast.13), channel_id=1, source_target_pairs={{4,0},{8,4},{12,8},{16,12},{20,16},{24,20},{28,24},{5,1},{9,5},{13... | collective-permute-start | bytes 3538952 | tf_op jit(solution)/shard_map/ppermute | solution.py:335
  232.8 17.6 %collective-permute-start.23 = (bf16[288,384]{1,0:T(8,128)(2,1)}, bf16[288,384]{1,0:T(8,128)(2,1)S(1)}, u32[]{:S(2)}, u32[]{:S(2)}) collective-permute-start(bf16[288,384]{1,0:T(8,128)(2,1)} %get-tuple-element.54), channel_id=1, source_target_pairs={{0,3},{1,0},{2,1},{3,2},{4,7},{5,4},{6,5},{7,6},{8,11},{9,8},{10,9... | collective-permute-start | bytes 663560 | tf_op jit(solution)/shard_map/ppermute | solution.py:310
  244.2 25.2 %collective-permute-start.24 = (bf16[288,384]{1,0:T(8,128)(2,1)}, bf16[288,384]{1,0:T(8,128)(2,1)S(1)}, u32[]{:S(2)}, u32[]{:S(2)}) collective-permute-start(bf16[288,384]{1,0:T(8,128)(2,1)} %get-tuple-element.55), channel_id=1, source_target_pairs={{0,2},{1,3},{2,0},{3,1},{4,6},{5,7},{6,4},{7,5},{8,10},{9,11},{10,... | collective-permute-start | bytes 663560 | tf_op jit(solution)/shard_map/ppermute | solution.py:310
  244.2 25.2 %collective-permute-start.25 = (bf16[288,384]{1,0:T(8,128)(2,1)}, bf16[288,384]{1,0:T(8,128)(2,1)S(1)}, u32[]{:S(2)}, u32[]{:S(2)}) collective-permute-start(bf16[288,384]{1,0:T(8,128)(2,1)} %get-tuple-element.56), channel_id=1, source_target_pairs={{0,1},{1,2},{2,3},{3,0},{4,5},{5,6},{6,7},{7,4},{8,9},{9,10},{10,1... | collective-permute-start | bytes 663560 | tf_op jit(solution)/shard_map/ppermute | solution.py:310
  250.3 24.2 %collective-permute-start.10 = (bf16[288,256]{1,0:T(8,128)(2,1)}, bf16[288,256]{1,0:T(8,128)(2,1)}, u32[]{:S(2)}, u32[]{:S(2)}) collective-permute-start(bf16[288,256]{1,0:T(8,128)(2,1)} %get-tuple-element.43), channel_id=1, source_target_pairs={{0,1},{1,2},{2,3},{3,0},{4,5},{5,6},{6,7},{7,4},{8,9},{9,10},{10,1... | collective-permute-start | bytes 442376 | tf_op jit(solution)/shard_map/ppermute | solution.py:310
  269.3 8.0 %collective-permute-start.11 = (bf16[288,256]{1,0:T(8,128)(2,1)}, bf16[288,256]{1,0:T(8,128)(2,1)}, u32[]{:S(2)}, u32[]{:S(2)}) collective-permute-start(bf16[288,256]{1,0:T(8,128)(2,1)} %get-tuple-element.44), channel_id=1, source_target_pairs={{0,2},{1,3},{2,0},{3,1},{4,6},{5,7},{6,4},{7,5},{8,10},{9,11},{10,... | collective-permute-start | bytes 442376 | tf_op jit(solution)/shard_map/ppermute | solution.py:310
  269.3 11.9 %collective-permute-start.12 = (bf16[288,256]{1,0:T(8,128)(2,1)}, bf16[288,256]{1,0:T(8,128)(2,1)}, u32[]{:S(2)}, u32[]{:S(2)}) collective-permute-start(bf16[288,256]{1,0:T(8,128)(2,1)} %get-tuple-element.45), channel_id=1, source_target_pairs={{0,3},{1,0},{2,1},{3,2},{4,7},{5,4},{6,5},{7,6},{8,11},{9,8},{10,9... | collective-permute-start | bytes 442376 | tf_op jit(solution)/shard_map/ppermute | solution.py:310
  274.6 28.3 %collective-permute-start.21 = (bf16[1152,256]{1,0:T(8,128)(2,1)S(1)}, bf16[1152,256]{1,0:T(8,128)(2,1)}, u32[]{:S(2)}, u32[]{:S(2)}) collective-permute-start(bf16[1152,256]{1,0:T(8,128)(2,1)S(1)} %slice.4), channel_id=1, source_target_pairs={{0,4},{4,8},{8,12},{12,16},{16,20},{20,24},{24,28},{1,5},{5,9},{9,... | collective-permute-start | bytes 1769480 | tf_op jit(solution)/shard_map/ppermute | solution.py:335
  277.3 25.6 %collective-permute-start.22 = (bf16[1152,256]{1,0:T(8,128)(2,1)S(1)}, bf16[1152,256]{1,0:T(8,128)(2,1)}, u32[]{:S(2)}, u32[]{:S(2)}) collective-permute-start(bf16[1152,256]{1,0:T(8,128)(2,1)S(1)} %slice.4), channel_id=1, source_target_pairs={{4,0},{8,4},{12,8},{16,12},{20,16},{24,20},{28,24},{5,1},{9,5},{13... | collective-permute-start | bytes 1769480 | tf_op jit(solution)/shard_map/ppermute | solution.py:335
  298.0 20.9 %collective-permute-start.18 = (bf16[288,256]{1,0:T(8,128)(2,1)}, bf16[288,256]{1,0:T(8,128)(2,1)S(1)}, u32[]{:S(2)}, u32[]{:S(2)}) collective-permute-start(bf16[288,256]{1,0:T(8,128)(2,1)} %get-tuple-element.51), channel_id=1, source_target_pairs={{0,3},{1,0},{2,1},{3,2},{4,7},{5,4},{6,5},{7,6},{8,11},{9,8},{10,9... | collective-permute-start | bytes 442376 | tf_op jit(solution)/shard_map/ppermute | solution.py:310
  301.6 17.3 %collective-permute-start.19 = (bf16[288,256]{1,0:T(8,128)(2,1)}, bf16[288,256]{1,0:T(8,128)(2,1)S(1)}, u32[]{:S(2)}, u32[]{:S(2)}) collective-permute-start(bf16[288,256]{1,0:T(8,128)(2,1)} %get-tuple-element.52), channel_id=1, source_target_pairs={{0,2},{1,3},{2,0},{3,1},{4,6},{5,7},{6,4},{7,5},{8,10},{9,11},{10,... | collective-permute-start | bytes 442376 | tf_op jit(solution)/shard_map/ppermute | solution.py:310
  301.6 17.3 %collective-permute-start.20 = (bf16[288,256]{1,0:T(8,128)(2,1)}, bf16[288,256]{1,0:T(8,128)(2,1)S(1)}, u32[]{:S(2)}, u32[]{:S(2)}) collective-permute-start(bf16[288,256]{1,0:T(8,128)(2,1)} %get-tuple-element.53), channel_id=1, source_target_pairs={{0,1},{1,2},{2,3},{3,0},{4,5},{5,6},{6,7},{7,4},{8,9},{9,10},{10,1... | collective-permute-start | bytes 442376 | tf_op jit(solution)/shard_map/ppermute | solution.py:310
  317.8 5.6 %collective-permute-start.27 = (bf16[288,128]{1,0:T(8,128)(2,1)}, bf16[288,128]{1,0:T(8,128)(2,1)S(1)}, u32[]{:S(2)}, u32[]{:S(2)}) collective-permute-start(bf16[288,128]{1,0:T(8,128)(2,1)} %get-tuple-element.59), channel_id=1, source_target_pairs={{0,2},{1,3},{2,0},{3,1},{4,6},{5,7},{6,4},{7,5},{8,10},{9,11},{10,... | collective-permute-start | bytes 221192 | tf_op jit(solution)/shard_map/ppermute | solution.py:310
  319.0 6.4 %collective-permute-start.28 = (bf16[288,128]{1,0:T(8,128)(2,1)}, bf16[288,128]{1,0:T(8,128)(2,1)S(1)}, u32[]{:S(2)}, u32[]{:S(2)}) collective-permute-start(bf16[288,128]{1,0:T(8,128)(2,1)} %get-tuple-element.60), channel_id=1, source_target_pairs={{0,1},{1,2},{2,3},{3,0},{4,5},{5,6},{6,7},{7,4},{8,9},{9,10},{10,1... | collective-permute-start | bytes 221192 | tf_op jit(solution)/shard_map/ppermute | solution.py:310
  (26 other events, 175.5 us)
where the time goes:
time: 329 us; the launch traced here: 328 us
  waiting for transfers between devices  129 us (39%)
  starting transfers between devices  97 us (29%)
  Pallas kernels  92 us (28%)
  local copies, waits for them, and re-layouts  9.35 us (3%)
    pallas_call x4, Pallas kernels, attend(): pl.pallas_call(functools.partial(attend_kernel, groups, heads, first_head...  72.2 us
    all_to_all x4, waiting for transfers between devices, arrive(): lax.all_to_all(sent[i], 'head', split_axis=0, concat_axis=0, tiled=True)  51.4 us
    ppermute x21, starting transfers between devices, turn(): lax.ppermute(array, 'head', [(i, (i + shift) % groups) for i in range(gro...  50.9 us
    ppermute x21, waiting for transfers between devices, turn(): lax.ppermute(array, 'head', [(i, (i + shift) % groups) for i in range(gro...  41.5 us
    ppermute x4, waiting for transfers between devices, arrive(): lax.ppermute(pairs, 'seq', onward)  35.3 us
    all_to_all x4, starting transfers between devices, arrive(): lax.all_to_all(sent[i], 'head', split_axis=0, concat_axis=0, tiled=True)  19.7 us
    ppermute x4, starting transfers between devices, arrive(): lax.ppermute(pairs, 'seq', backward)  18.5 us
    pallas_call x4, Pallas kernels, pack(): pl.pallas_call(kernel, in_specs=[ANY] * (len(arrays) + len(after)), out_s...  9.35 us
  transfers between devices with their start and end apart: 33, of which 11 were waited for; matrix products, arithmetic and copies ran while one was open for 1% of the time, Pallas kernels for 27%

commit v1 on v0

--- a/solution.py
+++ b/solution.py
@@ -9,7 +9,7 @@
 from jax.sharding import PartitionSpec as P
 
 LANES = 128
-LARGEST_CHUNK = 4
+CHUNK_HEADS = 3
 ANY = pl.BlockSpec(memory_space=pl.ANY)
 VMEM_LIMIT = 60 * 2**20
 
@@ -309,11 +309,8 @@
     def turn(array, shift):
         return lax.ppermute(array, "head", [(i, (i + shift) % groups) for i in range(groups)])
 
-    sizes, left = [], group_heads
-    while left:
-        sizes.append(min(len(sizes) + 1, LARGEST_CHUNK, left))
-        left -= sizes[-1]
-    sizes.sort(reverse=True)
+    parts = -(-(group_heads - 1) // CHUNK_HEADS)
+    sizes = [(group_heads - 1 + i) // parts for i in reversed(range(parts))] + [1]
     count = len(sizes)
     firsts = [sum(sizes[:i]) for i in range(count)]
 
@@ -339,18 +336,20 @@
     if count > 1:
         asks.append(asked(0, sent))
         sent.append(gate(packed(1, sent), there[0][:1]))
+    if count > 2:
+        asks.append(asked(1, there[0][:1]))
     for i, heads in enumerate(sizes):
         if i + 1 < count:
             there.append(arrive(i + 1, [part[1][0] for part in done[-1:]]))
-        if i == 0 and count > 2:
-            asks.append(asked(1, there[0][1:]))
         if i + 2 < count:
-            behind = there[i + 1][:1] + tuple(asks[1][:1] if i == 0 else [])
-            sent.append(gate(packed(i + 2, there[i][:1]), behind))
-        if i and i + 2 < count:
-            asks.append(asked(i + 1, sent[i + 2 :] + done[i - 1][1][1:]))
-        hold = [part[0] for part in there[i + 1 :] + asks[i + 1 :]] + sent[i + 2 :]
+            sent.append(gate(packed(i + 2, there[i][:1]), there[i + 1][:1]))
+            if i:
+                asks.append(asked(i + 1, done[i - 1][1][1:] + sent[i + 2 :]))
+        hold = [part[0] for part in there[i + 1 :]] + sent[i + 2 :]
         hold += [part[1][0] for part in done[-1:]]
+        hold += [block for part in done[-2:-1] for block in part[1][1:]]
+        if i == 0:
+            hold += [part[0] for part in asks[1:]]
         if i + 1 == count and count > 2:
             early = place(done[:-1], group_width, total_width)
             hold.append(early)

time: 329 us -> 310 us (0.942)
  the two profiles are of different devices: /device:TPU:4 before, /device:TPU:1 now
where the time goes in v1:
time: 310 us; the launch traced here: 316 us
  Pallas kernels  128 us (41%)
  waiting for transfers between devices  88 us (28%)
  starting transfers between devices  87.9 us (28%)
  local copies, waits for them, and re-layouts  10.9 us (4%)
    pallas_call x4, Pallas kernels, attend(): pl.pallas_call(functools.partial(attend_kernel, groups, heads, first_head...  108 us
    all_to_all x4, waiting for transfers between devices, arrive(): lax.all_to_all(sent[i], 'head', split_axis=0, concat_axis=0, tiled=True)  74.2 us
    ppermute x21, starting transfers between devices, turn(): lax.ppermute(array, 'head', [(i, (i + shift) % groups) for i in range(gro...  39.1 us
    ppermute x4, starting transfers between devices, arrive(): lax.ppermute(pairs, 'seq', onward)  24.1 us
    all_to_all x4, starting transfers between devices, arrive(): lax.all_to_all(sent[i], 'head', split_axis=0, concat_axis=0, tiled=True)  16.6 us
    ppermute x21, waiting for transfers between devices, turn(): lax.ppermute(array, 'head', [(i, (i + shift) % groups) for i in range(gro...  13.8 us
    pallas_call x4, Pallas kernels, pack(): pl.pallas_call(kernel, in_specs=[ANY] * (len(arrays) + len(after)), out_s...  9.36 us
    unnamed x47, local copies, waits for them, and re-layouts  9.19 us
  transfers between devices with their start and end apart: 33, of which 8 were waited for; matrix products, arithmetic and copies ran while one was open for 1% of the time, Pallas kernels for 39%

profile of v1, /device:TPU:1, one launch (start us, length us, event | category | flops | bytes accessed | tf_op | source)
XLA Modules:
  0.0 315.6 jit_solution(3212032833027090470)
XLA Ops:
  0.0 2.4 pack.4.refs_2_.refs_1_
  2.4 5.4 %all-to-all-start = ((bf16[4,288,768]{2,1,0:T(8,128)(2,1)}), bf16[4,288,768]{2,1,0:T(8,128)(2,1)S(1)}, u32[]{:S(2)}, u32[]{:S(2)}) async-start(bf16[4,288,768]{2,1,0:T(8,128)(2,1)} %pack.4.refs_2_.refs_1_), calls=%async_computation | async-start | bytes 3538944 | tf_op jit(solution)/shard_map/all_to_all | solution.py:328
  7.8 2.4 pack.6.refs_0_
  10.3 38.2 %all-to-all-done = bf16[4,288,768]{2,1,0:T(8,128)(2,1)S(1)} async-done(((bf16[4,288,768]{2,1,0:T(8,128)(2,1)}), bf16[4,288,768]{2,1,0:T(8,128)(2,1)S(1)}, u32[]{:S(2)}, u32[]{:S(2)}) %all-to-all-start) | async-done | bytes 1769504 | tf_op jit(solution)/shard_map/all_to_all | solution.py:328
  49.7 3.7 %all-to-all-start.1 = ((bf16[4,288,768]{2,1,0:T(8,128)(2,1)}), bf16[4,288,768]{2,1,0:T(8,128)(2,1)S(1)}, u32[]{:S(2)}, u32[]{:S(2)}) async-start(bf16[4,288,768]{2,1,0:T(8,128)(2,1)} %gate.5), calls=%async_computation.1 | async-start | bytes 3538944 | tf_op jit(solution)/shard_map/all_to_all | solution.py:328
  53.5 4.5 %collective-permute-start = (bf16[1152,768]{1,0:T(8,128)(2,1)S(1)}, bf16[1152,768]{1,0:T(8,128)(2,1)}, u32[]{:S(2)}, u32[]{:S(2)}) collective-permute-start(bf16[1152,768]{1,0:T(8,128)(2,1)S(1)} %bitcast.8), channel_id=1, source_target_pairs={{0,4},{4,8},{8,12},{12,16},{16,20},{20,24},{24,28},{1,5},{5,9},{9,... | collective-permute-start | bytes 5308424 | tf_op jit(solution)/shard_map/ppermute | solution.py:332
  59.9 2.1 pack_turned.3
  63.7 2.1 collective-permute-start.3
  66.9 2.4 pack.5.refs_0_
  69.3 34.2 %all-to-all-done.1 = bf16[4,288,768]{2,1,0:T(8,128)(2,1)S(1)} async-done(((bf16[4,288,768]{2,1,0:T(8,128)(2,1)}), bf16[4,288,768]{2,1,0:T(8,128)(2,1)S(1)}, u32[]{:S(2)}, u32[]{:S(2)}) %all-to-all-start.1) | async-done | bytes 1769504 | tf_op jit(solution)/shard_map/all_to_all | solution.py:328
  104.8 3.7 %all-to-all-start.2 = ((bf16[4,288,768]{2,1,0:T(8,128)(2,1)}), bf16[4,288,768]{2,1,0:T(8,128)(2,1)S(1)}, u32[]{:S(2)}, u32[]{:S(2)}) async-start(bf16[4,288,768]{2,1,0:T(8,128)(2,1)} %gate.6.refs_10_), calls=%async_computation.2 | async-start | bytes 3538944 | tf_op jit(solution)/shard_map/all_to_all | solution.py:328
  114.8 2.1 collective-permute-start.16
  118.0 6.7 %collective-permute-start.13 = (bf16[1152,768]{1,0:T(8,128)(2,1)}, bf16[1152,768]{1,0:T(8,128)(2,1)}, u32[]{:S(2)}, u32[]{:S(2)}) collective-permute-start(bf16[1152,768]{1,0:T(8,128)(2,1)} %bitcast.16), channel_id=1, source_target_pairs={{0,4},{4,8},{8,12},{12,16},{16,20},{20,24},{24,28},{1,5},{5,9},{9,... | collective-permute-start | bytes 5308424 | tf_op jit(solution)/shard_map/ppermute | solution.py:332
  126.7 29.9 %attend.4 = (bf16[288,384]{1,0:T(8,128)(2,1)}, bf16[288,384]{1,0:T(8,128)(2,1)}, bf16[288,384]{1,0:T(8,128)(2,1)}, bf16[288,384]{1,0:T(8,128)(2,1)}) custom-call(s32[27]{0:T(128)} %reshape.58.refs_0_, bf16[1152,768]{1,0:T(8,128)(2,1)} %bitcast.7, bf16[1152,768]{1,0:T(8,128)(2,1)} %collective-permute-done.refs_2_, ...), custom_call_target="tpu_custom_call" | custom-call | flops 24461180928 | bytes 7077888 | tf_op jit(solution)/shard_map/attend/pallas_call | solution.py:269
  156.6 2.1 pack.7.refs_0_
  161.7 3.7 %all-to-all-start.3 = ((bf16[4,288,384]{2,1,0:T(8,128)(2,1)}), bf16[4,288,384]{2,1,0:T(8,128)(2,1)S(1)}, u32[]{:S(2)}, u32[]{:S(2)}) async-start(bf16[4,288,384]{2,1,0:T(8,128)(2,1)} %gate.8.refs_4_.refs_10_), calls=%async_computation.3 | async-start | bytes 1769472 | tf_op jit(solution)/shard_map/all_to_all | solution.py:328
  165.4 3.3 %collective-permute-start.7 = (bf16[288,384]{1,0:T(8,128)(2,1)S(1)}, bf16[288,384]{1,0:T(8,128)(2,1)S(1)}, u32[]{:S(2)}, u32[]{:S(2)}) collective-permute-start(bf16[288,384]{1,0:T(8,128)(2,1)S(1)} %copy-done.22), channel_id=1, source_target_pairs={{0,3},{1,0},{2,1},{3,2},{4,7},{5,4},{6,5},{7,6},{8,11},{9,8},{10,9... | collective-permute-start | bytes 663560 | tf_op jit(solution)/shard_map/ppermute | solution.py:310
  168.6 2.2 collective-permute-start.9
  170.8 9.4 %collective-permute-start.5 = (bf16[1152,768]{1,0:T(8,128)(2,1)S(1)}, bf16[1152,768]{1,0:T(8,128)(2,1)}, u32[]{:S(2)}, u32[]{:S(2)}) collective-permute-start(bf16[1152,768]{1,0:T(8,128)(2,1)S(1)} %bitcast.13), channel_id=1, source_target_pairs={{0,4},{4,8},{8,12},{12,16},{16,20},{20,24},{24,28},{1,5},{5,9},{9,... | collective-permute-start | bytes 5308424 | tf_op jit(solution)/shard_map/ppermute | solution.py:332
  182.2 29.9 %attend.5 = (bf16[288,384]{1,0:T(8,128)(2,1)}, bf16[288,384]{1,0:T(8,128)(2,1)}, bf16[288,384]{1,0:T(8,128)(2,1)}, bf16[288,384]{1,0:T(8,128)(2,1)}) custom-call(s32[27]{0:T(128)} %reshape.58.refs_0_, bf16[1152,768]{1,0:T(8,128)(2,1)} %bitcast.20, bf16[1152,768]{1,0:T(8,128)(2,1)} %collective-permute-done.13.refs_2_, ...), custom_call_target="tpu_custom_call" | custom-call | flops 24461180928 | bytes 7077888 | tf_op jit(solution)/shard_map/attend/pallas_call | solution.py:269
  215.8 6.1 %collective-permute-done.23.refs_5_.refs_6_ = bf16[288,384]{1,0:T(8,128)(2,1)S(1)} collective-permute-done((bf16[288,384]{1,0:T(8,128)(2,1)}, bf16[288,384]{1,0:T(8,128)(2,1)S(1)}, u32[]{:S(2)}, u32[]{:S(2)}) %collective-permute-start.23) | collective-permute-done | bytes 221216 | tf_op jit(solution)/shard_map/ppermute | solution.py:310
  221.9 11.0 %collective-permute-start.10 = (bf16[288,384]{1,0:T(8,128)(2,1)}, bf16[288,384]{1,0:T(8,128)(2,1)}, u32[]{:S(2)}, u32[]{:S(2)}) collective-permute-start(bf16[288,384]{1,0:T(8,128)(2,1)} %get-tuple-element.43), channel_id=1, source_target_pairs={{0,1},{1,2},{2,3},{3,0},{4,5},{5,6},{6,7},{7,4},{8,9},{9,10},{10,1... | collective-permute-start | bytes 663560 | tf_op jit(solution)/shard_map/ppermute | solution.py:310
  232.8 2.1 collective-permute-done.24.refs_6_.refs_7_
  235.7 2.4 place.2.refs_9_.refs_8_
  240.1 3.5 %collective-permute-start.21 = (bf16[1152,256]{1,0:T(8,128)(2,1)S(1)}, bf16[1152,256]{1,0:T(8,128)(2,1)S(1)}, u32[]{:S(2)}, u32[]{:S(2)}) collective-permute-start(bf16[1152,256]{1,0:T(8,128)(2,1)S(1)} %slice.4), channel_id=1, source_target_pairs={{0,4},{4,8},{8,12},{12,16},{16,20},{20,24},{24,28},{1,5},{5,9},{9,... | collective-permute-start | bytes 1769480 | tf_op jit(solution)/shard_map/ppermute | solution.py:332
  243.7 2.4 collective-permute-start.22
  246.1 29.9 %attend.6 = (bf16[288,384]{1,0:T(8,128)(2,1)}, bf16[288,384]{1,0:T(8,128)(2,1)}, bf16[288,384]{1,0:T(8,128)(2,1)}, bf16[288,384]{1,0:T(8,128)(2,1)}) custom-call(s32[27]{0:T(128)} %reshape.58.refs_0_, bf16[1152,768]{1,0:T(8,128)(2,1)} %bitcast.12, bf16[1152,768]{1,0:T(8,128)(2,1)} %collective-permute-done.5.refs_2_, ...), custom_call_target="tpu_custom_call" | custom-call | flops 24461180928 | bytes 7077888 | tf_op jit(solution)/shard_map/attend/pallas_call | solution.py:269
  276.0 6.4 %collective-permute-start.18 = (bf16[288,384]{1,0:T(8,128)(2,1)}, bf16[288,384]{1,0:T(8,128)(2,1)S(1)}, u32[]{:S(2)}, u32[]{:S(2)}) collective-permute-start(bf16[288,384]{1,0:T(8,128)(2,1)} %get-tuple-element.51), channel_id=1, source_target_pairs={{0,3},{1,0},{2,1},{3,2},{4,7},{5,4},{6,5},{7,6},{8,11},{9,8},{10,9... | collective-permute-start | bytes 663560 | tf_op jit(solution)/shard_map/ppermute | solution.py:310
  283.8 18.3 %attend.7 = (bf16[288,128]{1,0:T(8,128)(2,1)}, bf16[288,128]{1,0:T(8,128)(2,1)}, bf16[288,128]{1,0:T(8,128)(2,1)}, bf16[288,128]{1,0:T(8,128)(2,1)}) custom-call(s32[27]{0:T(128)} %reshape.58.refs_0_, bf16[1152,384]{1,0:T(8,128)(2,1)} %bitcast.23, bf16[1152,256]{1,0:T(8,128)(2,1)} %copy-done.20, bf16[1152,256]{1,0:T(8,128)(2,1)} %copy-done.21, ...), custom_call_target="tpu_custom_call" | custom-call | flops 8153726976 | bytes 2359296 | tf_op jit(solution)/shard_map/attend/pallas_call | solution.py:269
  302.1 3.0 collective-permute-start.26
  309.4 3.0 collective-permute-done.28.refs_7_
  313.2 2.2 place.3
  (104 shorter events, 34.4 us)
Async XLA Ops:
  2.4 46.1 %all-to-all-start = ((bf16[4,288,768]{2,1,0:T(8,128)(2,1)}), bf16[4,288,768]{2,1,0:T(8,128)(2,1)S(1)}, u32[]{:S(2)}, u32[]{:S(2)}) async-start(bf16[4,288,768]{2,1,0:T(8,128)(2,1)} %pack.4.refs_2_.refs_1_), calls=%async_computation | async-start | bytes 3538944 | tf_op jit(solution)/shard_map/all_to_all | solution.py:328
  49.7 53.8 %all-to-all-start.1 = ((bf16[4,288,768]{2,1,0:T(8,128)(2,1)}), bf16[4,288,768]{2,1,0:T(8,128)(2,1)S(1)}, u32[]{:S(2)}, u32[]{:S(2)}) async-start(bf16[4,288,768]{2,1,0:T(8,128)(2,1)} %gate.5), calls=%async_computation.1 | async-start | bytes 3538944 | tf_op jit(solution)/shard_map/all_to_all | solution.py:328
  53.5 64.6 %collective-permute-start = (bf16[1152,768]{1,0:T(8,128)(2,1)S(1)}, bf16[1152,768]{1,0:T(8,128)(2,1)}, u32[]{:S(2)}, u32[]{:S(2)}) collective-permute-start(bf16[1152,768]{1,0:T(8,128)(2,1)S(1)} %bitcast.8), channel_id=1, source_target_pairs={{0,4},{4,8},{8,12},{12,16},{16,20},{20,24},{24,28},{1,5},{5,9},{9,... | collective-permute-start | bytes 5308424 | tf_op jit(solution)/shard_map/ppermute | solution.py:332
  57.9 66.8 %collective-permute-start.1 = (bf16[1152,768]{1,0:T(8,128)(2,1)S(1)}, bf16[1152,768]{1,0:T(8,128)(2,1)}, u32[]{:S(2)}, u32[]{:S(2)}) collective-permute-start(bf16[1152,768]{1,0:T(8,128)(2,1)S(1)} %bitcast.9), channel_id=1, source_target_pairs={{4,0},{8,4},{12,8},{16,12},{20,16},{24,20},{28,24},{5,1},{9,5},{13... | collective-permute-start | bytes 5308424 | tf_op jit(solution)/shard_map/ppermute | solution.py:332
  61.9 51.3 %collective-permute-start.2 = (bf16[288,384]{1,0:T(8,128)(2,1)}, bf16[288,384]{1,0:T(8,128)(2,1)}, u32[]{:S(2)}, u32[]{:S(2)}) collective-permute-start(bf16[288,384]{1,0:T(8,128)(2,1)} %get-tuple-element.34), channel_id=1, source_target_pairs={{0,1},{1,2},{2,3},{3,0},{4,5},{5,6},{6,7},{7,4},{8,9},{9,10},{10,1... | collective-permute-start | bytes 663560 | tf_op jit(solution)/shard_map/ppermute | solution.py:310
  63.7 51.1 %collective-permute-start.3 = (bf16[288,384]{1,0:T(8,128)(2,1)}, bf16[288,384]{1,0:T(8,128)(2,1)}, u32[]{:S(2)}, u32[]{:S(2)}) collective-permute-start(bf16[288,384]{1,0:T(8,128)(2,1)} %get-tuple-element.35), channel_id=1, source_target_pairs={{0,2},{1,3},{2,0},{3,1},{4,6},{5,7},{6,4},{7,5},{8,10},{9,11},{10,... | collective-permute-start | bytes 663560 | tf_op jit(solution)/shard_map/ppermute | solution.py:310
  65.8 51.1 %collective-permute-start.4 = (bf16[288,384]{1,0:T(8,128)(2,1)}, bf16[288,384]{1,0:T(8,128)(2,1)}, u32[]{:S(2)}, u32[]{:S(2)}) collective-permute-start(bf16[288,384]{1,0:T(8,128)(2,1)} %get-tuple-element.36), channel_id=1, source_target_pairs={{0,3},{1,0},{2,1},{3,2},{4,7},{5,4},{6,5},{7,6},{8,11},{9,8},{10,9... | collective-permute-start | bytes 663560 | tf_op jit(solution)/shard_map/ppermute | solution.py:310
  104.8 55.6 %all-to-all-start.2 = ((bf16[4,288,768]{2,1,0:T(8,128)(2,1)}), bf16[4,288,768]{2,1,0:T(8,128)(2,1)S(1)}, u32[]{:S(2)}, u32[]{:S(2)}) async-start(bf16[4,288,768]{2,1,0:T(8,128)(2,1)} %gate.6.refs_10_), calls=%async_computation.2 | async-start | bytes 3538944 | tf_op jit(solution)/shard_map/all_to_all | solution.py:328
  113.3 52.1 %collective-permute-start.15 = (bf16[288,384]{1,0:T(8,128)(2,1)}, bf16[288,384]{1,0:T(8,128)(2,1)}, u32[]{:S(2)}, u32[]{:S(2)}) collective-permute-start(bf16[288,384]{1,0:T(8,128)(2,1)} %get-tuple-element.46), channel_id=1, source_target_pairs={{0,1},{1,2},{2,3},{3,0},{4,5},{5,6},{6,7},{7,4},{8,9},{9,10},{10,1... | collective-permute-start | bytes 663560 | tf_op jit(solution)/shard_map/ppermute | solution.py:310
  114.8 53.9 %collective-permute-start.16 = (bf16[288,384]{1,0:T(8,128)(2,1)}, bf16[288,384]{1,0:T(8,128)(2,1)}, u32[]{:S(2)}, u32[]{:S(2)}) collective-permute-start(bf16[288,384]{1,0:T(8,128)(2,1)} %get-tuple-element.47), channel_id=1, source_target_pairs={{0,2},{1,3},{2,0},{3,1},{4,6},{5,7},{6,4},{7,5},{8,10},{9,11},{10,... | collective-permute-start | bytes 663560 | tf_op jit(solution)/shard_map/ppermute | solution.py:310
  116.8 51.8 %collective-permute-start.17 = (bf16[288,384]{1,0:T(8,128)(2,1)}, bf16[288,384]{1,0:T(8,128)(2,1)}, u32[]{:S(2)}, u32[]{:S(2)}) collective-permute-start(bf16[288,384]{1,0:T(8,128)(2,1)} %get-tuple-element.48), channel_id=1, source_target_pairs={{0,3},{1,0},{2,1},{3,2},{4,7},{5,4},{6,5},{7,6},{8,11},{9,8},{10,9... | collective-permute-start | bytes 663560 | tf_op jit(solution)/shard_map/ppermute | solution.py:310
  118.0 52.8 %collective-permute-start.13 = (bf16[1152,768]{1,0:T(8,128)(2,1)}, bf16[1152,768]{1,0:T(8,128)(2,1)}, u32[]{:S(2)}, u32[]{:S(2)}) collective-permute-start(bf16[1152,768]{1,0:T(8,128)(2,1)} %bitcast.16), channel_id=1, source_target_pairs={{0,4},{4,8},{8,12},{12,16},{16,20},{20,24},{24,28},{1,5},{5,9},{9,... | collective-permute-start | bytes 5308424 | tf_op jit(solution)/shard_map/ppermute | solution.py:332
  124.8 55.5 %collective-permute-start.14 = (bf16[1152,768]{1,0:T(8,128)(2,1)}, bf16[1152,768]{1,0:T(8,128)(2,1)}, u32[]{:S(2)}, u32[]{:S(2)}) collective-permute-start(bf16[1152,768]{1,0:T(8,128)(2,1)} %bitcast.17), channel_id=1, source_target_pairs={{4,0},{8,4},{12,8},{16,12},{20,16},{24,20},{28,24},{5,1},{9,5},{13... | collective-permute-start | bytes 5308424 | tf_op jit(solution)/shard_map/ppermute | solution.py:332
  161.7 76.4 %all-to-all-start.3 = ((bf16[4,288,384]{2,1,0:T(8,128)(2,1)}), bf16[4,288,384]{2,1,0:T(8,128)(2,1)S(1)}, u32[]{:S(2)}, u32[]{:S(2)}) async-start(bf16[4,288,384]{2,1,0:T(8,128)(2,1)} %gate.8.refs_4_.refs_10_), calls=%async_computation.3 | async-start | bytes 1769472 | tf_op jit(solution)/shard_map/all_to_all | solution.py:328
  165.4 46.7 %collective-permute-start.7 = (bf16[288,384]{1,0:T(8,128)(2,1)S(1)}, bf16[288,384]{1,0:T(8,128)(2,1)S(1)}, u32[]{:S(2)}, u32[]{:S(2)}) collective-permute-start(bf16[288,384]{1,0:T(8,128)(2,1)S(1)} %copy-done.22), channel_id=1, source_target_pairs={{0,3},{1,0},{2,1},{3,2},{4,7},{5,4},{6,5},{7,6},{8,11},{9,8},{10,9... | collective-permute-start | bytes 663560 | tf_op jit(solution)/shard_map/ppermute | solution.py:310
  168.6 43.5 %collective-permute-start.8 = (bf16[288,384]{1,0:T(8,128)(2,1)}, bf16[288,384]{1,0:T(8,128)(2,1)S(1)}, u32[]{:S(2)}, u32[]{:S(2)}) collective-permute-start(bf16[288,384]{1,0:T(8,128)(2,1)} %get-tuple-element.40), channel_id=1, source_target_pairs={{0,2},{1,3},{2,0},{3,1},{4,6},{5,7},{6,4},{7,5},{8,10},{9,11},{10,... | collective-permute-start | bytes 663560 | tf_op jit(solution)/shard_map/ppermute | solution.py:310
  168.6 44.4 %collective-permute-start.9 = (bf16[288,384]{1,0:T(8,128)(2,1)}, bf16[288,384]{1,0:T(8,128)(2,1)S(1)}, u32[]{:S(2)}, u32[]{:S(2)}) collective-permute-start(bf16[288,384]{1,0:T(8,128)(2,1)} %get-tuple-element.41), channel_id=1, source_target_pairs={{0,1},{1,2},{2,3},{3,0},{4,5},{5,6},{6,7},{7,4},{8,9},{9,10},{10,1... | collective-permute-start | bytes 663560 | tf_op jit(solution)/shard_map/ppermute | solution.py:310
  170.8 75.3 %collective-permute-start.5 = (bf16[1152,768]{1,0:T(8,128)(2,1)S(1)}, bf16[1152,768]{1,0:T(8,128)(2,1)}, u32[]{:S(2)}, u32[]{:S(2)}) collective-permute-start(bf16[1152,768]{1,0:T(8,128)(2,1)S(1)} %bitcast.13), channel_id=1, source_target_pairs={{0,4},{4,8},{8,12},{12,16},{16,20},{20,24},{24,28},{1,5},{5,9},{9,... | collective-permute-start | bytes 5308424 | tf_op jit(solution)/shard_map/ppermute | solution.py:332
  180.3 65.9 %collective-permute-start.6 = (bf16[1152,768]{1,0:T(8,128)(2,1)S(1)}, bf16[1152,768]{1,0:T(8,128)(2,1)}, u32[]{:S(2)}, u32[]{:S(2)}) collective-permute-start(bf16[1152,768]{1,0:T(8,128)(2,1)S(1)} %bitcast.14), channel_id=1, source_target_pairs={{4,0},{8,4},{12,8},{16,12},{20,16},{24,20},{28,24},{5,1},{9,5},{13... | collective-permute-start | bytes 5308424 | tf_op jit(solution)/shard_map/ppermute | solution.py:332
  212.1 9.8 %collective-permute-start.23 = (bf16[288,384]{1,0:T(8,128)(2,1)}, bf16[288,384]{1,0:T(8,128)(2,1)S(1)}, u32[]{:S(2)}, u32[]{:S(2)}) collective-permute-start(bf16[288,384]{1,0:T(8,128)(2,1)} %get-tuple-element.54), channel_id=1, source_target_pairs={{0,3},{1,0},{2,1},{3,2},{4,7},{5,4},{6,5},{7,6},{8,11},{9,8},{10,9... | collective-permute-start | bytes 663560 | tf_op jit(solution)/shard_map/ppermute | solution.py:310
  212.1 22.8 %collective-permute-start.24 = (bf16[288,384]{1,0:T(8,128)(2,1)}, bf16[288,384]{1,0:T(8,128)(2,1)S(1)}, u32[]{:S(2)}, u32[]{:S(2)}) collective-permute-start(bf16[288,384]{1,0:T(8,128)(2,1)} %get-tuple-element.55), channel_id=1, source_target_pairs={{0,2},{1,3},{2,0},{3,1},{4,6},{5,7},{6,4},{7,5},{8,10},{9,11},{10,... | collective-permute-start | bytes 663560 | tf_op jit(solution)/shard_map/ppermute | solution.py:310
  213.0 21.9 %collective-permute-start.25 = (bf16[288,384]{1,0:T(8,128)(2,1)}, bf16[288,384]{1,0:T(8,128)(2,1)S(1)}, u32[]{:S(2)}, u32[]{:S(2)}) collective-permute-start(bf16[288,384]{1,0:T(8,128)(2,1)} %get-tuple-element.56), channel_id=1, source_target_pairs={{0,1},{1,2},{2,3},{3,0},{4,5},{5,6},{6,7},{7,4},{8,9},{9,10},{10,1... | collective-permute-start | bytes 663560 | tf_op jit(solution)/shard_map/ppermute | solution.py:310
  221.9 18.3 %collective-permute-start.10 = (bf16[288,384]{1,0:T(8,128)(2,1)}, bf16[288,384]{1,0:T(8,128)(2,1)}, u32[]{:S(2)}, u32[]{:S(2)}) collective-permute-start(bf16[288,384]{1,0:T(8,128)(2,1)} %get-tuple-element.43), channel_id=1, source_target_pairs={{0,1},{1,2},{2,3},{3,0},{4,5},{5,6},{6,7},{7,4},{8,9},{9,10},{10,1... | collective-permute-start | bytes 663560 | tf_op jit(solution)/shard_map/ppermute | solution.py:310
  234.9 8.7 %collective-permute-start.11 = (bf16[288,384]{1,0:T(8,128)(2,1)}, bf16[288,384]{1,0:T(8,128)(2,1)}, u32[]{:S(2)}, u32[]{:S(2)}) collective-permute-start(bf16[288,384]{1,0:T(8,128)(2,1)} %get-tuple-element.44), channel_id=1, source_target_pairs={{0,2},{1,3},{2,0},{3,1},{4,6},{5,7},{6,4},{7,5},{8,10},{9,11},{10,... | collective-permute-start | bytes 663560 | tf_op jit(solution)/shard_map/ppermute | solution.py:310
  234.9 11.2 %collective-permute-start.12 = (bf16[288,384]{1,0:T(8,128)(2,1)}, bf16[288,384]{1,0:T(8,128)(2,1)}, u32[]{:S(2)}, u32[]{:S(2)}) collective-permute-start(bf16[288,384]{1,0:T(8,128)(2,1)} %get-tuple-element.45), channel_id=1, source_target_pairs={{0,3},{1,0},{2,1},{3,2},{4,7},{5,4},{6,5},{7,6},{8,11},{9,8},{10,9... | collective-permute-start | bytes 663560 | tf_op jit(solution)/shard_map/ppermute | solution.py:310
  240.1 42.6 %collective-permute-start.21 = (bf16[1152,256]{1,0:T(8,128)(2,1)S(1)}, bf16[1152,256]{1,0:T(8,128)(2,1)S(1)}, u32[]{:S(2)}, u32[]{:S(2)}) collective-permute-start(bf16[1152,256]{1,0:T(8,128)(2,1)S(1)} %slice.4), channel_id=1, source_target_pairs={{0,4},{4,8},{8,12},{12,16},{16,20},{20,24},{24,28},{1,5},{5,9},{9,... | collective-permute-start | bytes 1769480 | tf_op jit(solution)/shard_map/ppermute | solution.py:332
  243.7 39.0 %collective-permute-start.22 = (bf16[1152,256]{1,0:T(8,128)(2,1)S(1)}, bf16[1152,256]{1,0:T(8,128)(2,1)S(1)}, u32[]{:S(2)}, u32[]{:S(2)}) collective-permute-start(bf16[1152,256]{1,0:T(8,128)(2,1)S(1)} %slice.4), channel_id=1, source_target_pairs={{4,0},{8,4},{12,8},{16,12},{20,16},{24,20},{28,24},{5,1},{9,5},{13... | collective-permute-start | bytes 1769480 | tf_op jit(solution)/shard_map/ppermute | solution.py:332
  276.0 36.3 %collective-permute-start.18 = (bf16[288,384]{1,0:T(8,128)(2,1)}, bf16[288,384]{1,0:T(8,128)(2,1)S(1)}, u32[]{:S(2)}, u32[]{:S(2)}) collective-permute-start(bf16[288,384]{1,0:T(8,128)(2,1)} %get-tuple-element.51), channel_id=1, source_target_pairs={{0,3},{1,0},{2,1},{3,2},{4,7},{5,4},{6,5},{7,6},{8,11},{9,8},{10,9... | collective-permute-start | bytes 663560 | tf_op jit(solution)/shard_map/ppermute | solution.py:310
  282.4 29.9 %collective-permute-start.19 = (bf16[288,384]{1,0:T(8,128)(2,1)}, bf16[288,384]{1,0:T(8,128)(2,1)S(1)}, u32[]{:S(2)}, u32[]{:S(2)}) collective-permute-start(bf16[288,384]{1,0:T(8,128)(2,1)} %get-tuple-element.52), channel_id=1, source_target_pairs={{0,2},{1,3},{2,0},{3,1},{4,6},{5,7},{6,4},{7,5},{8,10},{9,11},{10,... | collective-permute-start | bytes 663560 | tf_op jit(solution)/shard_map/ppermute | solution.py:310
  282.4 30.0 %collective-permute-start.20 = (bf16[288,384]{1,0:T(8,128)(2,1)}, bf16[288,384]{1,0:T(8,128)(2,1)S(1)}, u32[]{:S(2)}, u32[]{:S(2)}) collective-permute-start(bf16[288,384]{1,0:T(8,128)(2,1)} %get-tuple-element.53), channel_id=1, source_target_pairs={{0,1},{1,2},{2,3},{3,0},{4,5},{5,6},{6,7},{7,4},{8,9},{9,10},{10,1... | collective-permute-start | bytes 663560 | tf_op jit(solution)/shard_map/ppermute | solution.py:310
  302.1 4.7 %collective-permute-start.26 = (bf16[288,128]{1,0:T(8,128)(2,1)}, bf16[288,128]{1,0:T(8,128)(2,1)S(1)}, u32[]{:S(2)}, u32[]{:S(2)}) collective-permute-start(bf16[288,128]{1,0:T(8,128)(2,1)} %get-tuple-element.58), channel_id=1, source_target_pairs={{0,3},{1,0},{2,1},{3,2},{4,7},{5,4},{6,5},{7,6},{8,11},{9,8},{10,9... | collective-permute-start | bytes 221192 | tf_op jit(solution)/shard_map/ppermute | solution.py:310
  306.8 5.5 %collective-permute-start.28 = (bf16[288,128]{1,0:T(8,128)(2,1)}, bf16[288,128]{1,0:T(8,128)(2,1)S(1)}, u32[]{:S(2)}, u32[]{:S(2)}) collective-permute-start(bf16[288,128]{1,0:T(8,128)(2,1)} %get-tuple-element.60), channel_id=1, source_target_pairs={{0,1},{1,2},{2,3},{3,0},{4,5},{5,6},{6,7},{7,4},{8,9},{9,10},{10,1... | collective-permute-start | bytes 221192 | tf_op jit(solution)/shard_map/ppermute | solution.py:310
  (24 other events, 65.0 us)

commit v2 on v1

--- a/solution.py
+++ b/solution.py
@@ -14,16 +14,14 @@
 VMEM_LIMIT = 60 * 2**20
 
 
-def tile_mask(reach_t, reach_w, slab_index, slab_count):
+def reach_plan(reach_t, reach_w, slab_index, slab_count):
     tile_count = reach_t.shape[0]
     places = jnp.arange(tile_count, dtype=jnp.int32)
-    columns = jnp.arange(3 * tile_count, dtype=jnp.int32)
-    offsets = columns // tile_count - 1
-    key_place = columns % tile_count
-    inside = (slab_index + offsets >= 0) & (slab_index + offsets < slab_count)
-    near_time = jnp.abs(offsets)[None, :] <= reach_t[:, None]
-    near_width = jnp.abs(key_place[None, :] - places[:, None]) <= reach_w[:, None]
-    return near_time & near_width & inside[None, :]
+    before = jnp.minimum(jnp.minimum(reach_t, 1), slab_index)
+    behind = jnp.minimum(jnp.minimum(reach_t, 1), slab_count - 1 - slab_index)
+    low = jnp.maximum(places - reach_w, 0)
+    high = jnp.minimum(places + reach_w, tile_count - 1)
+    return jnp.stack([1 - before, before + 1 + behind, low, high - low + 1], axis=1).reshape(-1)
 
 
 def staged(pairs, stages, sems):
@@ -163,88 +161,97 @@
 def attend_kernel(groups, heads, first_head, tile_count, in_pieces, *refs):
     plan_ref, own_ref, prev_ref, next_ref, keep_ref = refs[:5]
     pieces = refs[5 : 5 + groups] if in_pieces else ()
-    outs = refs[-6 - groups : -6]
-    q_ref, out_ref, scores_ref, top_ref, total_ref, sum_ref = refs[-6:]
+    outs = refs[-8 - groups : -8]
+    pair_ref, q_ref, out_ref, scores_ref, top_ref, total_ref, sum_ref, sems = refs[-8:]
     slab_rows, width = out_ref.shape
     local_rows = slab_rows // groups
     head_size = width // heads
     tile_rows = slab_rows // tile_count
     scale = math.log2(math.e) / math.sqrt(head_size)
-    slabs = ((0, prev_ref), (1, own_ref), (2, next_ref))
     me = lax.axis_index("head")
 
     def owner_rows(shift):
         owner = lax.rem(me + groups - shift, groups)
         return pl.ds(pl.multiple_of(owner * local_rows, 16), local_rows)
 
-    def tile(index):
-        return pl.ds(pl.multiple_of(index * tile_rows, tile_rows), tile_rows)
-
     def lanes(index):
         return pl.ds(index * head_size, head_size)
 
-    for shift, piece in enumerate(pieces):
-        q_ref[owner_rows(shift), :] = piece[...]
-    query_ref, first_query = (q_ref, 0) if pieces else (own_ref, 2 * heads)
+    loads = [
+        (prev_ref, pair_ref.at[0]),
+        (own_ref.at[:, pl.ds(0, 2 * width)], pair_ref.at[1]),
+        (next_ref, pair_ref.at[2]),
+    ]
+    loads += [(piece, q_ref.at[owner_rows(i), :]) for i, piece in enumerate(pieces)]
+    if not pieces:
+        loads.append((own_ref.at[:, pl.ds(2 * width, width)], q_ref))
+    copies = [
+        pltpu.make_async_copy(source, target, sems.at[i])
+        for i, (source, target) in enumerate(loads)
+    ]
+    for copy in copies:
+        copy.start()
+    for copy in copies:
+        copy.wait()
 
     def one_tile(i, carry):
+        first_slab, slabs = plan_ref[4 * i], plan_ref[4 * i + 1]
+        first_place, places = plan_ref[4 * i + 2], plan_ref[4 * i + 3]
+        mine = pl.ds(pl.multiple_of(i * tile_rows, tile_rows), tile_rows)
+        start = pl.multiple_of(first_place * tile_rows, tile_rows)
         top_ref[...] = jnp.full_like(top_ref, -jnp.inf)
         total_ref[...] = jnp.zeros_like(total_ref)
         sum_ref[...] = jnp.zeros_like(sum_ref)
 
-        for slab, pair_ref in slabs:
-
-            def score(place, carry, slab=slab, pair_ref=pair_ref):
-                column = slab * tile_count + place
-
-                @pl.when(plan_ref[i * 3 * tile_count + column] > 0)
-                def _():
-                    for h in range(heads):
-                        found = lax.dot_general(
-                            query_ref[tile(i), lanes(first_query + h)],
-                            pair_ref[tile(place), lanes(h)],
-                            (((1,), (1,)), ((), ())),
-                            preferred_element_type=jnp.float32,
-                        )
-                        scores_ref[h, column] = found
-                        top_ref[h] = jnp.maximum(top_ref[h], lane_fold(jnp.maximum, found))
-
+        for count in range(1, tile_count + 1):
+            rows = count * tile_rows
+
+            def score(slab, carry, rows=rows):
+                for h in range(heads):
+                    found = lax.dot_general(
+                        q_ref[mine, lanes(h)],
+                        pair_ref[slab, pl.ds(start, rows), lanes(h)],
+                        (((1,), (1,)), ((), ())),
+                        preferred_element_type=jnp.float32,
+                    )
+                    scores_ref[h, slab, :, pl.ds(0, rows)] = found
+                    top_ref[h] = jnp.maximum(top_ref[h], lane_fold(jnp.maximum, found))
                 return carry
 
-            lax.fori_loop(0, tile_count, score, 0)
+            @pl.when(places == count)
+            def _(score=score):
+                lax.fori_loop(first_slab, first_slab + slabs, score, 0)
 
         for h in range(heads):
             highest = jnp.max(top_ref[h], axis=1, keepdims=True) * scale
             top_ref[h] = jnp.broadcast_to(highest, top_ref.shape[1:])
 
-        for slab, pair_ref in slabs:
-
-            def weigh(place, carry, slab=slab, pair_ref=pair_ref):
-                column = slab * tile_count + place
-
-                @pl.when(plan_ref[i * 3 * tile_count + column] > 0)
-                def _():
-                    for h in range(heads):
-                        highest = jnp.concatenate([top_ref[h]] * (tile_rows // LANES), axis=1)
-                        weights = jnp.exp2(scores_ref[h, column] * scale - highest)
-                        total_ref[h] += lane_fold(jnp.add, weights)
-                        sum_ref[h] += jnp.dot(
-                            weights.astype(jnp.bfloat16),
-                            pair_ref[tile(place), lanes(heads + h)],
-                            preferred_element_type=jnp.float32,
-                        )
-
+        for count in range(1, tile_count + 1):
+            rows = count * tile_rows
+
+            def weigh(slab, carry, rows=rows):
+                for h in range(heads):
+                    highest = jnp.concatenate([top_ref[h]] * (rows // LANES), axis=1)
+                    weights = jnp.exp2(scores_ref[h, slab, :, pl.ds(0, rows)] * scale - highest)
+                    total_ref[h] += lane_fold(jnp.add, weights)
+                    sum_ref[h] += jnp.dot(
+                        weights.astype(jnp.bfloat16),
+                        pair_ref[slab, pl.ds(start, rows), lanes(heads + h)],
+                        preferred_element_type=jnp.float32,
+                    )
                 return carry
 
-            lax.fori_loop(0, tile_count, weigh, 0)
-
-        keep = keep_ref[tile(i), :].astype(jnp.float32)
+            @pl.when(places == count)
+            def _(weigh=weigh):
+                lax.fori_loop(first_slab, first_slab + slabs, weigh, 0)
+
+        keep = keep_ref[mine, :].astype(jnp.float32)
         numbers = lax.broadcasted_iota(jnp.int32, keep.shape, 1)
         for h in range(heads):
             totals = jnp.sum(total_ref[h], axis=1, keepdims=True)
-            mine = jnp.where(numbers == first_head + h, keep, 0.0)
-            factor = jnp.sum(mine, axis=1, keepdims=True) * (10.0 / 9.0)
-            out_ref[tile(i), lanes(h)] = (sum_ref[h] * (factor / totals)).astype(out_ref.dtype)
+            kept = jnp.where(numbers == first_head + h, keep, 0.0)
+            factor = jnp.sum(kept, axis=1, keepdims=True) * (10.0 / 9.0)
+            out_ref[mine, lanes(h)] = (sum_ref[h] * (factor / totals)).astype(out_ref.dtype)
         return carry
 
     lax.fori_loop(0, tile_count, one_tile, 0)
@@ -261,31 +268,31 @@
     tile_rows = slab_rows // tile_count
     head_size = width // heads
     pairs = heads * slab_rows * 3 * slab_rows
-    wholes = [
-        pl.BlockSpec(array.shape, lambda s, plan: (0, 0))
-        for array in (own, prev, behind, keep_mask, *pieces)
-    ]
     accumulator = pltpu.VMEM((heads, tile_rows, LANES), jnp.float32)
     return pl.pallas_call(
         functools.partial(attend_kernel, groups, heads, first_head, tile_count, bool(pieces)),
         grid_spec=pltpu.PrefetchScalarGridSpec(
             num_scalar_prefetch=1,
             grid=(1,),
-            in_specs=wholes + [ANY] * len(after),
+            in_specs=[ANY] * 3
+            + [pl.BlockSpec(keep_mask.shape, lambda s, plan: (0, 0))]
+            + [ANY] * (len(pieces) + len(after)),
             out_specs=[pl.BlockSpec((local_rows, width), lambda s, plan: (0, 0))] * groups,
             scratch_shapes=[
+                pltpu.VMEM((3, slab_rows, 2 * width), jnp.bfloat16),
                 pltpu.VMEM((slab_rows, width), jnp.bfloat16),
                 pltpu.VMEM((slab_rows, width), jnp.bfloat16),
-                pltpu.VMEM((heads, 3 * tile_count, tile_rows, tile_rows), jnp.float32),
+                pltpu.VMEM((heads, 3, tile_rows, slab_rows), jnp.float32),
                 accumulator,
                 accumulator,
                 pltpu.VMEM((heads, tile_rows, head_size), jnp.float32),
+                pltpu.SemaphoreType.DMA((3 + max(len(pieces), 1),)),
             ],
         ),
         out_shape=[jax.ShapeDtypeStruct((local_rows, width), jnp.bfloat16)] * groups,
         compiler_params=pltpu.CompilerParams(vmem_limit_bytes=VMEM_LIMIT),
         cost_estimate=pl.CostEstimate(
-            flops=16 * pairs * head_size,
+            flops=12 * pairs * head_size,
             bytes_accessed=16 * slab_rows * width,
             transcendentals=pairs,
         ),
@@ -301,8 +308,7 @@
     group_width = total_width // groups
     head_size = group_width // group_heads
     tile_count = reach_time.shape[0]
-    allowed = tile_mask(reach_time, reach_width, lax.axis_index("seq"), slab_count)
-    plan = allowed.astype(jnp.int32).reshape(-1)
+    plan = reach_plan(reach_time, reach_width, lax.axis_index("seq"), slab_count)
     onward = [(i, i + 1) for i in range(slab_count - 1)]
     backward = [(i + 1, i) for i in range(slab_count - 1)]
 
@@ -313,9 +319,10 @@
     sizes = [(group_heads - 1 + i) // parts for i in reversed(range(parts))] + [1]
     count = len(sizes)
     firsts = [sum(sizes[:i]) for i in range(count)]
+    with_permutes = min(2, count - 1)
 
     def packed(i, after):
-        arrays = (key_vectors, value_vectors, queries)[: 2 + (i + 1 == count)]
+        arrays = (key_vectors, value_vectors, queries)[: 3 - (i < with_permutes)]
         start, width = firsts[i] * head_size, sizes[i] * head_size
         return pack(arrays, after, groups, group_width, start, width)
 
@@ -334,26 +341,22 @@
     sent, there, asks, done, early = [packed(0, [])], [], [], [], None
     there.append(arrive(0, []))
     if count > 1:
-        asks.append(asked(0, sent))
         sent.append(gate(packed(1, sent), there[0][:1]))
-    if count > 2:
-        asks.append(asked(1, there[0][:1]))
+    for i in range(with_permutes):
+        asks.append(asked(i, there[i - 1][:1] if i else sent[:1]))
     for i, heads in enumerate(sizes):
         if i + 1 < count:
             there.append(arrive(i + 1, [part[1][0] for part in done[-1:]]))
         if i + 2 < count:
             sent.append(gate(packed(i + 2, there[i][:1]), there[i + 1][:1]))
-            if i:
-                asks.append(asked(i + 1, done[i - 1][1][1:] + sent[i + 2 :]))
         hold = [part[0] for part in there[i + 1 :]] + sent[i + 2 :]
         hold += [part[1][0] for part in done[-1:]]
         hold += [block for part in done[-2:-1] for block in part[1][1:]]
-        if i == 0:
-            hold += [part[0] for part in asks[1:]]
+        hold += [part[0] for part in asks[i + 1 :]]
         if i + 1 == count and count > 2:
             early = place(done[:-1], group_width, total_width)
             hold.append(early)
-        pieces = asks[i] if i + 1 < count else []
+        pieces = asks[i] if i < with_permutes else []
         outs = attend(
             plan, *there[i], keep_mask, pieces, hold, groups, firsts[i], heads, tile_count
         )

time: 310 us -> 337 us (1.087)
  the two profiles are of different devices: /device:TPU:1 before, /device:TPU:2 now
where the time goes in v2:
time: 337 us; the launch traced here: 335 us
  waiting for transfers between devices  163 us (48%)
  Pallas kernels  86.6 us (26%)
  starting transfers between devices  70.9 us (21%)
  local copies, waits for them, and re-layouts  14 us (4%)
    ppermute x18, waiting for transfers between devices, turn(): lax.ppermute(array, 'head', [(i, (i + shift) % groups) for i in range(gro...  86.3 us
    all_to_all x4, waiting for transfers between devices, arrive(): lax.all_to_all(sent[i], 'head', split_axis=0, concat_axis=0, tiled=True)  76.6 us
    pallas_call x4, Pallas kernels, attend(): pl.pallas_call(functools.partial(attend_kernel, groups, heads, first_head...  68.1 us
    ppermute x18, starting transfers between devices, turn(): lax.ppermute(array, 'head', [(i, (i + shift) % groups) for i in range(gro...  34.3 us
    all_to_all x4, starting transfers between devices, arrive(): lax.all_to_all(sent[i], 'head', split_axis=0, concat_axis=0, tiled=True)  15.7 us
    ppermute x4, starting transfers between devices, arrive(): lax.ppermute(pairs, 'seq', backward)  13 us
    unnamed x55, local copies, waits for them, and re-layouts  10.6 us
    pallas_call x4, Pallas kernels, pack(): pl.pallas_call(kernel, in_specs=[ANY] * (len(arrays) + len(after)), out_s...  9.76 us
  transfers between devices with their start and end apart: 30, of which 9 were waited for; matrix products, arithmetic and copies ran while one was open for 1% of the time, Pallas kernels for 24%

profile of v2, /device:TPU:2, one launch (start us, length us, event | category | flops | bytes accessed | tf_op | source)
XLA Modules:
  0.0 335.0 jit_solution(14457371050127622839)
XLA Ops:
  0.0 2.4 pack.4.refs_2_.refs_1_
  2.4 4.9 %all-to-all-start = ((bf16[4,288,768]{2,1,0:T(8,128)(2,1)}), bf16[4,288,768]{2,1,0:T(8,128)(2,1)S(1)}, u32[]{:S(2)}, u32[]{:S(2)}) async-start(bf16[4,288,768]{2,1,0:T(8,128)(2,1)} %pack.4.refs_2_.refs_1_), calls=%async_computation | async-start | bytes 3538944 | tf_op jit(solution)/shard_map/all_to_all | solution.py:335
  7.3 2.4 pack.6.refs_0_
  9.7 38.8 %all-to-all-done = bf16[4,288,768]{2,1,0:T(8,128)(2,1)S(1)} async-done(((bf16[4,288,768]{2,1,0:T(8,128)(2,1)}), bf16[4,288,768]{2,1,0:T(8,128)(2,1)S(1)}, u32[]{:S(2)}, u32[]{:S(2)}) %all-to-all-start) | async-done | bytes 1769504 | tf_op jit(solution)/shard_map/all_to_all | solution.py:335
  49.7 3.6 %all-to-all-start.1 = ((bf16[4,288,768]{2,1,0:T(8,128)(2,1)}), bf16[4,288,768]{2,1,0:T(8,128)(2,1)S(1)}, u32[]{:S(2)}, u32[]{:S(2)}) async-start(bf16[4,288,768]{2,1,0:T(8,128)(2,1)} %gate.5), calls=%async_computation.1 | async-start | bytes 3538944 | tf_op jit(solution)/shard_map/all_to_all | solution.py:335
  53.3 2.8 pack.5.refs_0_
  56.1 37.9 %all-to-all-done.1 = bf16[4,288,768]{2,1,0:T(8,128)(2,1)S(1)} async-done(((bf16[4,288,768]{2,1,0:T(8,128)(2,1)}), bf16[4,288,768]{2,1,0:T(8,128)(2,1)S(1)}, u32[]{:S(2)}, u32[]{:S(2)}) %all-to-all-start.1) | async-done | bytes 1769504 | tf_op jit(solution)/shard_map/all_to_all | solution.py:335
  95.2 3.7 %all-to-all-start.2 = ((bf16[4,288,1152]{2,1,0:T(8,128)(2,1)}), bf16[4,288,1152]{2,1,0:T(8,128)(2,1)S(1)}, u32[]{:S(2)}, u32[]{:S(2)}) async-start(bf16[4,288,1152]{2,1,0:T(8,128)(2,1)} %gate.6.refs_10_), calls=%async_computation.2 | async-start | bytes 5308416 | tf_op jit(solution)/shard_map/all_to_all | solution.py:335
  98.9 2.1 collective-permute-start
  100.9 3.6 %collective-permute-start.1 = (bf16[1152,768]{1,0:T(8,128)(2,1)}, bf16[1152,768]{1,0:T(8,128)(2,1)}, u32[]{:S(2)}, u32[]{:S(2)}) collective-permute-start(bf16[1152,768]{1,0:T(8,128)(2,1)} %bitcast.19), channel_id=1, source_target_pairs={{4,0},{8,4},{12,8},{16,12},{20,16},{24,20},{28,24},{5,1},{9,5},{13... | collective-permute-start | bytes 5308424 | tf_op jit(solution)/shard_map/ppermute | solution.py:339
  104.6 2.1 pack_turned.2
  108.7 2.4 collective-permute-start.3
  112.5 39.4 %collective-permute-done.2.refs_6_ = bf16[288,384]{1,0:T(8,128)(2,1)S(1)} collective-permute-done((bf16[288,384]{1,0:T(8,128)(2,1)}, bf16[288,384]{1,0:T(8,128)(2,1)S(1)}, u32[]{:S(2)}, u32[]{:S(2)}) %collective-permute-start.2) | collective-permute-done | bytes 221216 | tf_op jit(solution)/shard_map/ppermute | solution.py:316
  153.9 19.9 %collective-permute-done.3.refs_7_ = bf16[288,384]{1,0:T(8,128)(2,1)S(1)} collective-permute-done((bf16[288,384]{1,0:T(8,128)(2,1)}, bf16[288,384]{1,0:T(8,128)(2,1)S(1)}, u32[]{:S(2)}, u32[]{:S(2)}) %collective-permute-start.3) | collective-permute-done | bytes 221216 | tf_op jit(solution)/shard_map/ppermute | solution.py:316
  180.3 5.2 %collective-permute-start.10 = (bf16[288,384]{1,0:T(8,128)(2,1)}, bf16[288,384]{1,0:T(8,128)(2,1)S(1)}, u32[]{:S(2)}, u32[]{:S(2)}) collective-permute-start(bf16[288,384]{1,0:T(8,128)(2,1)} %get-tuple-element.36), channel_id=1, source_target_pairs={{0,2},{1,3},{2,0},{3,1},{4,6},{5,7},{6,4},{7,5},{8,10},{9,11},{10,... | collective-permute-start | bytes 663560 | tf_op jit(solution)/shard_map/ppermute | solution.py:316
  187.5 19.2 %attend.4 = (bf16[288,384]{1,0:T(8,128)(2,1)}, bf16[288,384]{1,0:T(8,128)(2,1)}, bf16[288,384]{1,0:T(8,128)(2,1)}, bf16[288,384]{1,0:T(8,128)(2,1)}) custom-call(s32[12]{0:T(128)} %reshape.15.refs_0_, bf16[1152,768]{1,0:T(8,128)(2,1)} %bitcast.21, bf16[1152,768]{1,0:T(8,128)(2,1)} %collective-permute-done.refs_2_, ...), custom_call_target="tpu_custom_call" | custom-call | flops 18345885696 | bytes 7077888 | tf_op jit(solution)/shard_map/attend/pallas_call | solution.py:272
  206.7 2.2 pack.7.refs_0_
  212.0 3.6 %all-to-all-start.3 = ((bf16[4,288,384]{2,1,0:T(8,128)(2,1)}), bf16[4,288,384]{2,1,0:T(8,128)(2,1)S(1)}, u32[]{:S(2)}, u32[]{:S(2)}) async-start(bf16[4,288,384]{2,1,0:T(8,128)(2,1)} %gate.8.refs_10_), calls=%async_computation.3 | async-start | bytes 1769472 | tf_op jit(solution)/shard_map/all_to_all | solution.py:335
  215.6 3.8 %collective-permute-start.12 = (bf16[288,384]{1,0:T(8,128)(2,1)}, bf16[288,384]{1,0:T(8,128)(2,1)S(1)}, u32[]{:S(2)}, u32[]{:S(2)}) collective-permute-start(bf16[288,384]{1,0:T(8,128)(2,1)} %get-tuple-element.39), channel_id=1, source_target_pairs={{0,3},{1,0},{2,1},{3,2},{4,7},{5,4},{6,5},{7,6},{8,11},{9,8},{10,9... | collective-permute-start | bytes 663560 | tf_op jit(solution)/shard_map/ppermute | solution.py:316
  223.8 3.8 %collective-permute-start.6 = (bf16[1152,768]{1,0:T(8,128)(2,1)S(1)}, bf16[1152,768]{1,0:T(8,128)(2,1)}, u32[]{:S(2)}, u32[]{:S(2)}) collective-permute-start(bf16[1152,768]{1,0:T(8,128)(2,1)S(1)} %slice.8), channel_id=1, source_target_pairs={{4,0},{8,4},{12,8},{16,12},{20,16},{24,20},{28,24},{5,1},{9,5},{13... | collective-permute-start | bytes 5308424 | tf_op jit(solution)/shard_map/ppermute | solution.py:339
  227.7 19.2 %attend.5 = (bf16[288,384]{1,0:T(8,128)(2,1)}, bf16[288,384]{1,0:T(8,128)(2,1)}, bf16[288,384]{1,0:T(8,128)(2,1)}, bf16[288,384]{1,0:T(8,128)(2,1)}) custom-call(s32[12]{0:T(128)} %reshape.15.refs_0_, bf16[1152,768]{1,0:T(8,128)(2,1)} %bitcast.27, bf16[1152,768]{1,0:T(8,128)(2,1)} %collective-permute-done.7.refs_2_, ...), custom_call_target="tpu_custom_call" | custom-call | flops 18345885696 | bytes 7077888 | tf_op jit(solution)/shard_map/attend/pallas_call | solution.py:272
  246.9 2.7 collective-permute-start.20
  249.7 8.6 %collective-permute-done.13.refs_8_.refs_2_ = bf16[288,384]{1,0:T(8,128)(2,1)S(1)} collective-permute-done((bf16[288,384]{1,0:T(8,128)(2,1)}, bf16[288,384]{1,0:T(8,128)(2,1)S(1)}, u32[]{:S(2)}, u32[]{:S(2)}) %collective-permute-start.13) | collective-permute-done | bytes 221216 | tf_op jit(solution)/shard_map/ppermute | solution.py:316
  258.3 7.0 %collective-permute-start.22 = (bf16[288,384]{1,0:T(8,128)(2,1)}, bf16[288,384]{1,0:T(8,128)(2,1)S(1)}, u32[]{:S(2)}, u32[]{:S(2)}) collective-permute-start(bf16[288,384]{1,0:T(8,128)(2,1)} %get-tuple-element.48), channel_id=1, source_target_pairs={{0,1},{1,2},{2,3},{3,0},{4,5},{5,6},{6,7},{7,4},{8,9},{9,10},{10,1... | collective-permute-start | bytes 663560 | tf_op jit(solution)/shard_map/ppermute | solution.py:316
  265.3 8.4 %collective-permute-done.21.refs_6_.refs_7_ = bf16[288,384]{1,0:T(8,128)(2,1)S(1)} collective-permute-done((bf16[288,384]{1,0:T(8,128)(2,1)}, bf16[288,384]{1,0:T(8,128)(2,1)S(1)}, u32[]{:S(2)}, u32[]{:S(2)}) %collective-permute-start.21) | collective-permute-done | bytes 221216 | tf_op jit(solution)/shard_map/ppermute | solution.py:316
  274.5 2.4 place.2.refs_9_.refs_8_
  280.8 3.6 %collective-permute-start.19 = (bf16[1152,256]{1,0:T(8,128)(2,1)S(1)}, bf16[1152,256]{1,0:T(8,128)(2,1)S(1)}, u32[]{:S(2)}, u32[]{:S(2)}) collective-permute-start(bf16[1152,256]{1,0:T(8,128)(2,1)S(1)} %slice.9), channel_id=1, source_target_pairs={{4,0},{8,4},{12,8},{16,12},{20,16},{24,20},{28,24},{5,1},{9,5},{13... | collective-permute-start | bytes 1769480 | tf_op jit(solution)/shard_map/ppermute | solution.py:339
  284.5 19.3 %attend.6 = (bf16[288,384]{1,0:T(8,128)(2,1)}, bf16[288,384]{1,0:T(8,128)(2,1)}, bf16[288,384]{1,0:T(8,128)(2,1)}, bf16[288,384]{1,0:T(8,128)(2,1)}) custom-call(s32[12]{0:T(128)} %reshape.15.refs_0_, bf16[1152,1152]{1,0:T(8,128)(2,1)} %bitcast.15, bf16[1152,768]{1,0:T(8,128)(2,1)} %collective-permute-done.5.refs_2_, ...), custom_call_target="tpu_custom_call" | custom-call | flops 18345885696 | bytes 7077888 | tf_op jit(solution)/shard_map/attend/pallas_call | solution.py:272
  307.3 10.4 %attend.7 = (bf16[288,128]{1,0:T(8,128)(2,1)}, bf16[288,128]{1,0:T(8,128)(2,1)}, bf16[288,128]{1,0:T(8,128)(2,1)}, bf16[288,128]{1,0:T(8,128)(2,1)}) custom-call(s32[12]{0:T(128)} %reshape.15.refs_0_, bf16[1152,384]{1,0:T(8,128)(2,1)} %bitcast.30, bf16[1152,256]{1,0:T(8,128)(2,1)} %copy-done.19, bf16[1152,256]{1,0:T(8,128)(2,1)} %copy-done.20, ...), custom_call_target="tpu_custom_call" | custom-call | flops 6115295232 | bytes 2359296 | tf_op jit(solution)/shard_map/attend/pallas_call | solution.py:272
  320.4 5.0 %collective-permute-done.23.refs_5_ = bf16[288,128]{1,0:T(8,128)(2,1)S(1)} collective-permute-done((bf16[288,128]{1,0:T(8,128)(2,1)}, bf16[288,128]{1,0:T(8,128)(2,1)S(1)}, u32[]{:S(2)}, u32[]{:S(2)}) %collective-permute-start.23) | collective-permute-done | bytes 73760 | tf_op jit(solution)/shard_map/ppermute | solution.py:316
  327.1 4.7 %collective-permute-done.25.refs_7_ = bf16[288,128]{1,0:T(8,128)(2,1)S(1)} collective-permute-done((bf16[288,128]{1,0:T(8,128)(2,1)}, bf16[288,128]{1,0:T(8,128)(2,1)S(1)}, u32[]{:S(2)}, u32[]{:S(2)}) %collective-permute-start.25) | collective-permute-done | bytes 73760 | tf_op jit(solution)/shard_map/ppermute | solution.py:316
  332.7 2.2 place.3
  (106 shorter events, 37.2 us)
Async XLA Ops:
  2.4 46.1 %all-to-all-start = ((bf16[4,288,768]{2,1,0:T(8,128)(2,1)}), bf16[4,288,768]{2,1,0:T(8,128)(2,1)S(1)}, u32[]{:S(2)}, u32[]{:S(2)}) async-start(bf16[4,288,768]{2,1,0:T(8,128)(2,1)} %pack.4.refs_2_.refs_1_), calls=%async_computation | async-start | bytes 3538944 | tf_op jit(solution)/shard_map/all_to_all | solution.py:335
  49.7 44.2 %all-to-all-start.1 = ((bf16[4,288,768]{2,1,0:T(8,128)(2,1)}), bf16[4,288,768]{2,1,0:T(8,128)(2,1)S(1)}, u32[]{:S(2)}, u32[]{:S(2)}) async-start(bf16[4,288,768]{2,1,0:T(8,128)(2,1)} %gate.5), calls=%async_computation.1 | async-start | bytes 3538944 | tf_op jit(solution)/shard_map/all_to_all | solution.py:335
  95.2 113.7 %all-to-all-start.2 = ((bf16[4,288,1152]{2,1,0:T(8,128)(2,1)}), bf16[4,288,1152]{2,1,0:T(8,128)(2,1)S(1)}, u32[]{:S(2)}, u32[]{:S(2)}) async-start(bf16[4,288,1152]{2,1,0:T(8,128)(2,1)} %gate.6.refs_10_), calls=%async_computation.2 | async-start | bytes 5308416 | tf_op jit(solution)/shard_map/all_to_all | solution.py:335
  98.9 77.5 %copy-start.16 = (s32[1152,10]{0,1:T(8,128)S(1)}, s32[1152,10]{0,1:T(8,128)}, u32[]{:S(2)}) copy-start(s32[1152,10]{0,1:T(8,128)} %param.11) | copy-start | bytes 138244
  98.9 86.5 %collective-permute-start = (bf16[1152,768]{1,0:T(8,128)(2,1)}, bf16[1152,768]{1,0:T(8,128)(2,1)}, u32[]{:S(2)}, u32[]{:S(2)}) collective-permute-start(bf16[1152,768]{1,0:T(8,128)(2,1)} %bitcast.18), channel_id=1, source_target_pairs={{0,4},{4,8},{8,12},{12,16},{16,20},{20,24},{24,28},{1,5},{5,9},{9,... | collective-permute-start | bytes 5308424 | tf_op jit(solution)/shard_map/ppermute | solution.py:339
  100.9 85.0 %collective-permute-start.1 = (bf16[1152,768]{1,0:T(8,128)(2,1)}, bf16[1152,768]{1,0:T(8,128)(2,1)}, u32[]{:S(2)}, u32[]{:S(2)}) collective-permute-start(bf16[1152,768]{1,0:T(8,128)(2,1)} %bitcast.19), channel_id=1, source_target_pairs={{4,0},{8,4},{12,8},{16,12},{20,16},{24,20},{28,24},{5,1},{9,5},{13... | collective-permute-start | bytes 5308424 | tf_op jit(solution)/shard_map/ppermute | solution.py:339
  106.7 45.3 %collective-permute-start.2 = (bf16[288,384]{1,0:T(8,128)(2,1)}, bf16[288,384]{1,0:T(8,128)(2,1)S(1)}, u32[]{:S(2)}, u32[]{:S(2)}) collective-permute-start(bf16[288,384]{1,0:T(8,128)(2,1)} %get-tuple-element.30), channel_id=1, source_target_pairs={{0,1},{1,2},{2,3},{3,0},{4,5},{5,6},{6,7},{7,4},{8,9},{9,10},{10,1... | collective-permute-start | bytes 663560 | tf_op jit(solution)/shard_map/ppermute | solution.py:316
  108.7 65.1 %collective-permute-start.3 = (bf16[288,384]{1,0:T(8,128)(2,1)}, bf16[288,384]{1,0:T(8,128)(2,1)S(1)}, u32[]{:S(2)}, u32[]{:S(2)}) collective-permute-start(bf16[288,384]{1,0:T(8,128)(2,1)} %get-tuple-element.31), channel_id=1, source_target_pairs={{0,2},{1,3},{2,0},{3,1},{4,6},{5,7},{6,4},{7,5},{8,10},{9,11},{10,... | collective-permute-start | bytes 663560 | tf_op jit(solution)/shard_map/ppermute | solution.py:316
  111.0 68.5 %collective-permute-start.4 = (bf16[288,384]{1,0:T(8,128)(2,1)}, bf16[288,384]{1,0:T(8,128)(2,1)S(1)}, u32[]{:S(2)}, u32[]{:S(2)}) collective-permute-start(bf16[288,384]{1,0:T(8,128)(2,1)} %get-tuple-element.32), channel_id=1, source_target_pairs={{0,3},{1,0},{2,1},{3,2},{4,7},{5,4},{6,5},{7,6},{8,11},{9,8},{10,9... | collective-permute-start | bytes 663560 | tf_op jit(solution)/shard_map/ppermute | solution.py:316
  152.0 27.6 %copy-start.22 = (bf16[288,384]{1,0:T(8,128)(2,1)}, bf16[288,384]{1,0:T(8,128)(2,1)S(1)}, u32[]{:S(2)}) copy-start(bf16[288,384]{1,0:T(8,128)(2,1)S(1)} %collective-permute-done.2.refs_6_) | copy-start | bytes 663556
  152.0 70.0 %collective-permute-start.7 = (bf16[1152,768]{1,0:T(8,128)(2,1)}, bf16[1152,768]{1,0:T(8,128)(2,1)}, u32[]{:S(2)}, u32[]{:S(2)}) collective-permute-start(bf16[1152,768]{1,0:T(8,128)(2,1)} %bitcast.23), channel_id=1, source_target_pairs={{0,4},{4,8},{8,12},{12,16},{16,20},{20,24},{24,28},{1,5},{5,9},{9,... | collective-permute-start | bytes 5308424 | tf_op jit(solution)/shard_map/ppermute | solution.py:339
  173.7 50.1 %collective-permute-start.8 = (bf16[1152,768]{1,0:T(8,128)(2,1)}, bf16[1152,768]{1,0:T(8,128)(2,1)}, u32[]{:S(2)}, u32[]{:S(2)}) collective-permute-start(bf16[1152,768]{1,0:T(8,128)(2,1)} %bitcast.24), channel_id=1, source_target_pairs={{4,0},{8,4},{12,8},{16,12},{20,16},{24,20},{28,24},{5,1},{9,5},{13... | collective-permute-start | bytes 5308424 | tf_op jit(solution)/shard_map/ppermute | solution.py:339
  180.3 35.3 %collective-permute-start.10 = (bf16[288,384]{1,0:T(8,128)(2,1)}, bf16[288,384]{1,0:T(8,128)(2,1)S(1)}, u32[]{:S(2)}, u32[]{:S(2)}) collective-permute-start(bf16[288,384]{1,0:T(8,128)(2,1)} %get-tuple-element.36), channel_id=1, source_target_pairs={{0,2},{1,3},{2,0},{3,1},{4,6},{5,7},{6,4},{7,5},{8,10},{9,11},{10,... | collective-permute-start | bytes 663560 | tf_op jit(solution)/shard_map/ppermute | solution.py:316
  185.4 34.0 %collective-permute-start.11 = (bf16[288,384]{1,0:T(8,128)(2,1)}, bf16[288,384]{1,0:T(8,128)(2,1)S(1)}, u32[]{:S(2)}, u32[]{:S(2)}) collective-permute-start(bf16[288,384]{1,0:T(8,128)(2,1)} %get-tuple-element.37), channel_id=1, source_target_pairs={{0,3},{1,0},{2,1},{3,2},{4,7},{5,4},{6,5},{7,6},{8,11},{9,8},{10,9... | collective-permute-start | bytes 663560 | tf_op jit(solution)/shard_map/ppermute | solution.py:316
  186.0 34.1 %collective-permute-start.9 = (bf16[288,384]{1,0:T(8,128)(2,1)}, bf16[288,384]{1,0:T(8,128)(2,1)S(1)}, u32[]{:S(2)}, u32[]{:S(2)}) collective-permute-start(bf16[288,384]{1,0:T(8,128)(2,1)} %get-tuple-element.35), channel_id=1, source_target_pairs={{0,1},{1,2},{2,3},{3,0},{4,5},{5,6},{6,7},{7,4},{8,9},{9,10},{10,1... | collective-permute-start | bytes 663560 | tf_op jit(solution)/shard_map/ppermute | solution.py:316
  212.0 64.9 %all-to-all-start.3 = ((bf16[4,288,384]{2,1,0:T(8,128)(2,1)}), bf16[4,288,384]{2,1,0:T(8,128)(2,1)S(1)}, u32[]{:S(2)}, u32[]{:S(2)}) async-start(bf16[4,288,384]{2,1,0:T(8,128)(2,1)} %gate.8.refs_10_), calls=%async_computation.3 | async-start | bytes 1769472 | tf_op jit(solution)/shard_map/all_to_all | solution.py:335
  215.6 31.3 %collective-permute-start.12 = (bf16[288,384]{1,0:T(8,128)(2,1)}, bf16[288,384]{1,0:T(8,128)(2,1)S(1)}, u32[]{:S(2)}, u32[]{:S(2)}) collective-permute-start(bf16[288,384]{1,0:T(8,128)(2,1)} %get-tuple-element.39), channel_id=1, source_target_pairs={{0,3},{1,0},{2,1},{3,2},{4,7},{5,4},{6,5},{7,6},{8,11},{9,8},{10,9... | collective-permute-start | bytes 663560 | tf_op jit(solution)/shard_map/ppermute | solution.py:316
  220.1 38.2 %collective-permute-start.13 = (bf16[288,384]{1,0:T(8,128)(2,1)}, bf16[288,384]{1,0:T(8,128)(2,1)S(1)}, u32[]{:S(2)}, u32[]{:S(2)}) collective-permute-start(bf16[288,384]{1,0:T(8,128)(2,1)} %get-tuple-element.40), channel_id=1, source_target_pairs={{0,2},{1,3},{2,0},{3,1},{4,6},{5,7},{6,4},{7,5},{8,10},{9,11},{10,... | collective-permute-start | bytes 663560 | tf_op jit(solution)/shard_map/ppermute | solution.py:316
  220.8 37.5 %collective-permute-start.14 = (bf16[288,384]{1,0:T(8,128)(2,1)}, bf16[288,384]{1,0:T(8,128)(2,1)S(1)}, u32[]{:S(2)}, u32[]{:S(2)}) collective-permute-start(bf16[288,384]{1,0:T(8,128)(2,1)} %get-tuple-element.41), channel_id=1, source_target_pairs={{0,1},{1,2},{2,3},{3,0},{4,5},{5,6},{6,7},{7,4},{8,9},{9,10},{10,1... | collective-permute-start | bytes 663560 | tf_op jit(solution)/shard_map/ppermute | solution.py:316
  221.9 62.6 %collective-permute-start.5 = (bf16[1152,768]{1,0:T(8,128)(2,1)S(1)}, bf16[1152,768]{1,0:T(8,128)(2,1)}, u32[]{:S(2)}, u32[]{:S(2)}) collective-permute-start(bf16[1152,768]{1,0:T(8,128)(2,1)S(1)} %slice.8), channel_id=1, source_target_pairs={{0,4},{4,8},{8,12},{12,16},{16,20},{20,24},{24,28},{1,5},{5,9},{9,... | collective-permute-start | bytes 5308424 | tf_op jit(solution)/shard_map/ppermute | solution.py:339
  223.8 60.6 %collective-permute-start.6 = (bf16[1152,768]{1,0:T(8,128)(2,1)S(1)}, bf16[1152,768]{1,0:T(8,128)(2,1)}, u32[]{:S(2)}, u32[]{:S(2)}) collective-permute-start(bf16[1152,768]{1,0:T(8,128)(2,1)S(1)} %slice.8), channel_id=1, source_target_pairs={{4,0},{8,4},{12,8},{16,12},{20,16},{24,20},{28,24},{5,1},{9,5},{13... | collective-permute-start | bytes 5308424 | tf_op jit(solution)/shard_map/ppermute | solution.py:339
  246.9 18.4 %collective-permute-start.20 = (bf16[288,384]{1,0:T(8,128)(2,1)}, bf16[288,384]{1,0:T(8,128)(2,1)S(1)}, u32[]{:S(2)}, u32[]{:S(2)}) collective-permute-start(bf16[288,384]{1,0:T(8,128)(2,1)} %get-tuple-element.46), channel_id=1, source_target_pairs={{0,3},{1,0},{2,1},{3,2},{4,7},{5,4},{6,5},{7,6},{8,11},{9,8},{10,9... | collective-permute-start | bytes 663560 | tf_op jit(solution)/shard_map/ppermute | solution.py:316
  258.3 15.4 %collective-permute-start.21 = (bf16[288,384]{1,0:T(8,128)(2,1)}, bf16[288,384]{1,0:T(8,128)(2,1)S(1)}, u32[]{:S(2)}, u32[]{:S(2)}) collective-permute-start(bf16[288,384]{1,0:T(8,128)(2,1)} %get-tuple-element.47), channel_id=1, source_target_pairs={{0,2},{1,3},{2,0},{3,1},{4,6},{5,7},{6,4},{7,5},{8,10},{9,11},{10,... | collective-permute-start | bytes 663560 | tf_op jit(solution)/shard_map/ppermute | solution.py:316
  258.3 15.4 %collective-permute-start.22 = (bf16[288,384]{1,0:T(8,128)(2,1)}, bf16[288,384]{1,0:T(8,128)(2,1)S(1)}, u32[]{:S(2)}, u32[]{:S(2)}) collective-permute-start(bf16[288,384]{1,0:T(8,128)(2,1)} %get-tuple-element.48), channel_id=1, source_target_pairs={{0,1},{1,2},{2,3},{3,0},{4,5},{5,6},{6,7},{7,4},{8,9},{9,10},{10,1... | collective-permute-start | bytes 663560 | tf_op jit(solution)/shard_map/ppermute | solution.py:316
  278.9 27.4 %collective-permute-start.18 = (bf16[1152,256]{1,0:T(8,128)(2,1)S(1)}, bf16[1152,256]{1,0:T(8,128)(2,1)S(1)}, u32[]{:S(2)}, u32[]{:S(2)}) collective-permute-start(bf16[1152,256]{1,0:T(8,128)(2,1)S(1)} %slice.9), channel_id=1, source_target_pairs={{0,4},{4,8},{8,12},{12,16},{16,20},{20,24},{24,28},{1,5},{5,9},{9,... | collective-permute-start | bytes 1769480 | tf_op jit(solution)/shard_map/ppermute | solution.py:339
  280.8 25.5 %collective-permute-start.19 = (bf16[1152,256]{1,0:T(8,128)(2,1)S(1)}, bf16[1152,256]{1,0:T(8,128)(2,1)S(1)}, u32[]{:S(2)}, u32[]{:S(2)}) collective-permute-start(bf16[1152,256]{1,0:T(8,128)(2,1)S(1)} %slice.9), channel_id=1, source_target_pairs={{4,0},{8,4},{12,8},{16,12},{20,16},{24,20},{28,24},{5,1},{9,5},{13... | collective-permute-start | bytes 1769480 | tf_op jit(solution)/shard_map/ppermute | solution.py:339
  303.8 28.0 %collective-permute-start.15 = (bf16[288,384]{1,0:T(8,128)(2,1)}, bf16[288,384]{1,0:T(8,128)(2,1)S(1)}, u32[]{:S(2)}, u32[]{:S(2)}) collective-permute-start(bf16[288,384]{1,0:T(8,128)(2,1)} %get-tuple-element.43), channel_id=1, source_target_pairs={{0,3},{1,0},{2,1},{3,2},{4,7},{5,4},{6,5},{7,6},{8,11},{9,8},{10,9... | collective-permute-start | bytes 663560 | tf_op jit(solution)/shard_map/ppermute | solution.py:316
  304.0 27.9 %collective-permute-start.16 = (bf16[288,384]{1,0:T(8,128)(2,1)}, bf16[288,384]{1,0:T(8,128)(2,1)S(1)}, u32[]{:S(2)}, u32[]{:S(2)}) collective-permute-start(bf16[288,384]{1,0:T(8,128)(2,1)} %get-tuple-element.44), channel_id=1, source_target_pairs={{0,2},{1,3},{2,0},{3,1},{4,6},{5,7},{6,4},{7,5},{8,10},{9,11},{10,... | collective-permute-start | bytes 663560 | tf_op jit(solution)/shard_map/ppermute | solution.py:316
  304.3 27.5 %collective-permute-start.17 = (bf16[288,384]{1,0:T(8,128)(2,1)}, bf16[288,384]{1,0:T(8,128)(2,1)S(1)}, u32[]{:S(2)}, u32[]{:S(2)}) collective-permute-start(bf16[288,384]{1,0:T(8,128)(2,1)} %get-tuple-element.45), channel_id=1, source_target_pairs={{0,1},{1,2},{2,3},{3,0},{4,5},{5,6},{6,7},{7,4},{8,9},{9,10},{10,1... | collective-permute-start | bytes 663560 | tf_op jit(solution)/shard_map/ppermute | solution.py:316
  317.8 7.7 %collective-permute-start.23 = (bf16[288,128]{1,0:T(8,128)(2,1)}, bf16[288,128]{1,0:T(8,128)(2,1)S(1)}, u32[]{:S(2)}, u32[]{:S(2)}) collective-permute-start(bf16[288,128]{1,0:T(8,128)(2,1)} %get-tuple-element.50), channel_id=1, source_target_pairs={{0,3},{1,0},{2,1},{3,2},{4,7},{5,4},{6,5},{7,6},{8,11},{9,8},{10,9... | collective-permute-start | bytes 221192 | tf_op jit(solution)/shard_map/ppermute | solution.py:316
  319.8 7.3 %collective-permute-start.24 = (bf16[288,128]{1,0:T(8,128)(2,1)}, bf16[288,128]{1,0:T(8,128)(2,1)S(1)}, u32[]{:S(2)}, u32[]{:S(2)}) collective-permute-start(bf16[288,128]{1,0:T(8,128)(2,1)} %get-tuple-element.51), channel_id=1, source_target_pairs={{0,2},{1,3},{2,0},{3,1},{4,6},{5,7},{6,4},{7,5},{8,10},{9,11},{10,... | collective-permute-start | bytes 221192 | tf_op jit(solution)/shard_map/ppermute | solution.py:316
  325.5 6.4 %collective-permute-start.25 = (bf16[288,128]{1,0:T(8,128)(2,1)}, bf16[288,128]{1,0:T(8,128)(2,1)S(1)}, u32[]{:S(2)}, u32[]{:S(2)}) collective-permute-start(bf16[288,128]{1,0:T(8,128)(2,1)} %get-tuple-element.52), channel_id=1, source_target_pairs={{0,1},{1,2},{2,3},{3,0},{4,5},{5,6},{6,7},{7,4},{8,9},{9,10},{10,1... | collective-permute-start | bytes 221192 | tf_op jit(solution)/shard_map/ppermute | solution.py:316
  (25 other events, 135.7 us)

commit v3 on v2

--- a/solution.py
+++ b/solution.py
@@ -44,29 +44,31 @@
     ]
 
 
-def pack(arrays, after, groups, group_width, start, width):
-    rows = arrays[0].shape[0]
+def pack(parts, after, groups, group_width):
+    rows = parts[0][0].shape[0]
+    arrays = [array for array, _, _ in parts]
+    total = sum(width for _, _, width in parts)
 
     def kernel(*refs):
-        sources, out = refs[: len(arrays)], refs[len(arrays) + len(after)]
-        stages, sems = refs[len(arrays) + len(after) + 1 : -1], refs[-1]
+        out = refs[len(parts) + len(after)]
+        stages, sems = refs[len(parts) + len(after) + 1 : -1], refs[-1]
         pairs = []
         for group in range(groups):
-            columns = pl.ds(group * group_width + start, width)
-            for i, source in enumerate(sources):
-                pairs.append((source.at[:, columns], out.at[group, :, pl.ds(i * width, width)]))
+            filled = 0
+            for source, (_, start, width) in zip(refs, parts):
+                columns = pl.ds(group * group_width + start, width)
+                pairs.append((source.at[:, columns], out.at[group, :, pl.ds(filled, width)]))
+                filled += width
         staged(pairs, stages, sems)
 
     return pl.pallas_call(
         kernel,
-        in_specs=[ANY] * (len(arrays) + len(after)),
+        in_specs=[ANY] * (len(parts) + len(after)),
         out_specs=ANY,
-        out_shape=jax.ShapeDtypeStruct((groups, rows, len(arrays) * width), jnp.bfloat16),
-        scratch_shapes=stage_shapes([(rows, width)] * (len(arrays) * groups)),
+        out_shape=jax.ShapeDtypeStruct((groups, rows, total), jnp.bfloat16),
+        scratch_shapes=stage_shapes([(rows, width) for _, _, width in parts] * groups),
         cost_estimate=pl.CostEstimate(
-            flops=0,
-            bytes_accessed=4 * len(arrays) * groups * rows * width,
-            transcendentals=0,
+            flops=0, bytes_accessed=4 * groups * rows * total, transcendentals=0
         ),
         compiler_params=pltpu.CompilerParams(vmem_limit_bytes=VMEM_LIMIT),
         name="pack",
@@ -158,9 +160,9 @@
     return folded
 
 
-def attend_kernel(groups, heads, first_head, tile_count, in_pieces, *refs):
+def attend_kernel(groups, heads, first_head, tile_count, query_lane, *refs):
     plan_ref, own_ref, prev_ref, next_ref, keep_ref = refs[:5]
-    pieces = refs[5 : 5 + groups] if in_pieces else ()
+    asked = refs[5 : 5 + groups] if query_lane is None else refs[5:6]
     outs = refs[-8 - groups : -8]
     pair_ref, q_ref, out_ref, scores_ref, top_ref, total_ref, sum_ref, sems = refs[-8:]
     slab_rows, width = out_ref.shape
@@ -182,9 +184,10 @@
         (own_ref.at[:, pl.ds(0, 2 * width)], pair_ref.at[1]),
         (next_ref, pair_ref.at[2]),
     ]
-    loads += [(piece, q_ref.at[owner_rows(i), :]) for i, piece in enumerate(pieces)]
-    if not pieces:
-        loads.append((own_ref.at[:, pl.ds(2 * width, width)], q_ref))
+    if query_lane is None:
+        loads += [(piece, q_ref.at[owner_rows(i), :]) for i, piece in enumerate(asked)]
+    else:
+        loads.append((asked[0].at[:, pl.ds(query_lane, width)], q_ref))
     copies = [
         pltpu.make_async_copy(source, target, sems.at[i])
         for i, (source, target) in enumerate(loads)
@@ -261,7 +264,7 @@
 
 
 def attend(
-    plan, own, prev, behind, keep_mask, pieces, after, groups, first_head, heads, tile_count
+    plan, own, prev, behind, keep_mask, asked, lane, after, groups, first_head, heads, tile_count
 ):
     slab_rows, width = prev.shape[0], prev.shape[1] // 2
     local_rows = slab_rows // groups
@@ -270,13 +273,13 @@
     pairs = heads * slab_rows * 3 * slab_rows
     accumulator = pltpu.VMEM((heads, tile_rows, LANES), jnp.float32)
     return pl.pallas_call(
-        functools.partial(attend_kernel, groups, heads, first_head, tile_count, bool(pieces)),
+        functools.partial(attend_kernel, groups, heads, first_head, tile_count, lane),
         grid_spec=pltpu.PrefetchScalarGridSpec(
             num_scalar_prefetch=1,
             grid=(1,),
             in_specs=[ANY] * 3
             + [pl.BlockSpec(keep_mask.shape, lambda s, plan: (0, 0))]
-            + [ANY] * (len(pieces) + len(after)),
+            + [ANY] * (len(asked) + len(after)),
             out_specs=[pl.BlockSpec((local_rows, width), lambda s, plan: (0, 0))] * groups,
             scratch_shapes=[
                 pltpu.VMEM((3, slab_rows, 2 * width), jnp.bfloat16),
@@ -286,7 +289,7 @@
                 accumulator,
                 accumulator,
                 pltpu.VMEM((heads, tile_rows, head_size), jnp.float32),
-                pltpu.SemaphoreType.DMA((3 + max(len(pieces), 1),)),
+                pltpu.SemaphoreType.DMA((3 + len(asked),)),
             ],
         ),
         out_shape=[jax.ShapeDtypeStruct((local_rows, width), jnp.bfloat16)] * groups,
@@ -297,7 +300,7 @@
             transcendentals=pairs,
         ),
         name="attend",
-    )(plan, own, prev, behind, keep_mask, *pieces, *after)
+    )(plan, own, prev, behind, keep_mask, *asked, *after)
 
 
 def on_device(queries, key_vectors, value_vectors, reach_time, reach_width, keep_mask):
@@ -319,16 +322,19 @@
     sizes = [(group_heads - 1 + i) // parts for i in reversed(range(parts))] + [1]
     count = len(sizes)
     firsts = [sum(sizes[:i]) for i in range(count)]
-    with_permutes = min(2, count - 1)
+    by_permutes = max(count - 2, 0)
+
+    def columns(i):
+        return firsts[i] * head_size, sizes[i] * head_size
 
     def packed(i, after):
-        arrays = (key_vectors, value_vectors, queries)[: 3 - (i < with_permutes)]
-        start, width = firsts[i] * head_size, sizes[i] * head_size
-        return pack(arrays, after, groups, group_width, start, width)
+        parts = [(key_vectors, *columns(i)), (value_vectors, *columns(i))]
+        if i + 1 == count:
+            parts += [(queries, *columns(j)) for j in reversed(range(by_permutes, count))]
+        return pack(parts, after, groups, group_width)
 
     def asked(i, after):
-        start, width = firsts[i] * head_size, sizes[i] * head_size
-        blocks = pack_turned(queries, after, groups, group_width, start, width)
+        blocks = pack_turned(queries, after, groups, group_width, *columns(i))
         return [blocks[0]] + [turn(blocks[shift], shift) for shift in range(1, groups)]
 
     def arrive(i, after):
@@ -342,13 +348,14 @@
     there.append(arrive(0, []))
     if count > 1:
         sent.append(gate(packed(1, sent), there[0][:1]))
-    for i in range(with_permutes):
+    for i in range(by_permutes):
         asks.append(asked(i, there[i - 1][:1] if i else sent[:1]))
     for i, heads in enumerate(sizes):
         if i + 1 < count:
             there.append(arrive(i + 1, [part[1][0] for part in done[-1:]]))
         if i + 2 < count:
-            sent.append(gate(packed(i + 2, there[i][:1]), there[i + 1][:1]))
+            landed = [*there[i + 1][:1], *there[i][1:], *asks[i][1:]]
+            sent.append(gate(packed(i + 2, there[i][:1]), landed))
         hold = [part[0] for part in there[i + 1 :]] + sent[i + 2 :]
         hold += [part[1][0] for part in done[-1:]]
         hold += [block for part in done[-2:-1] for block in part[1][1:]]
@@ -356,9 +363,13 @@
         if i + 1 == count and count > 2:
             early = place(done[:-1], group_width, total_width)
             hold.append(early)
-        pieces = asks[i] if i < with_permutes else []
+        if i < by_permutes:
+            source, lane = asks[i], None
+        else:
+            source, lane = there[-1][:1], 2 * columns(count - 1)[1]
+            lane += sum(columns(j)[1] for j in range(i + 1, count))
         outs = attend(
-            plan, *there[i], keep_mask, pieces, hold, groups, firsts[i], heads, tile_count
+            plan, *there[i], keep_mask, source, lane, hold, groups, firsts[i], heads, tile_count
         )
         back = [outs[0]] + [turn(outs[shift], groups - shift) for shift in range(1, groups)]
         done.append((firsts[i] * head_size, back))

time: 337 us -> 317 us (0.941)
  waiting for transfers between devices: 163 us -> 146 us
  Pallas kernels: 86.6 us -> 76.5 us
  starting transfers between devices: 70.9 us -> 80 us
    all_to_all x4, waiting for transfers between devices: 76.6 us -> 54.6 us  [arrive(): lax.all_to_all(sent[i], 'head', split_axis=0, concat_axis=0, tiled=True)]
    pallas_call x4, Pallas kernels: 68.1 us -> 58.1 us  [attend(): pl.pallas_call(functools.partial(attend_kernel, groups, heads, first_head...]
    all_to_all x4, starting transfers between devices: 15.7 us -> 21 us  [arrive(): lax.all_to_all(sent[i], 'head', split_axis=0, concat_axis=0, tiled=True)]
    ppermute x18, waiting for transfers between devices: 86.3 us -> 91 us  [turn(): lax.ppermute(array, 'head', [(i, (i + shift) % groups) for i in range(gro...]
    unnamed x55 -> x43, local copies, waits for them, and re-layouts: 10.6 us -> 9.27 us
  transfers between devices with their start and end apart: 30 -> 30, of which waited for: 9 -> 10; matrix products, arithmetic and copies ran while one was open for 1% -> 1% of each run, Pallas kernels for 24% -> 23%
where the time goes in v3:
time: 317 us; the launch traced here: 314 us
  waiting for transfers between devices  146 us (46%)
  starting transfers between devices  80 us (25%)
  Pallas kernels  76.5 us (24%)
  local copies, waits for them, and re-layouts  11.1 us (4%)
    ppermute x18, waiting for transfers between devices, turn(): lax.ppermute(array, 'head', [(i, (i + shift) % groups) for i in range(gro...  91 us
    pallas_call x4, Pallas kernels, attend(): pl.pallas_call(functools.partial(attend_kernel, groups, heads, first_head...  58.1 us
    all_to_all x4, waiting for transfers between devices, arrive(): lax.all_to_all(sent[i], 'head', split_axis=0, concat_axis=0, tiled=True)  54.6 us
    ppermute x18, starting transfers between devices, turn(): lax.ppermute(array, 'head', [(i, (i + shift) % groups) for i in range(gro...  36.8 us
    all_to_all x4, starting transfers between devices, arrive(): lax.all_to_all(sent[i], 'head', split_axis=0, concat_axis=0, tiled=True)  21 us
    ppermute x4, starting transfers between devices, arrive(): lax.ppermute(pairs, 'seq', backward)  14.6 us
    pallas_call x4, Pallas kernels, pack(): pl.pallas_call(kernel, in_specs=[ANY] * (len(parts) + len(after)), out_sp...  9.77 us
    unnamed x43, local copies, waits for them, and re-layouts  9.27 us
  transfers between devices with their start and end apart: 30, of which 10 were waited for; matrix products, arithmetic and copies ran while one was open for 1% of the time, Pallas kernels for 23%

profile of v3, /device:TPU:2, one launch (start us, length us, event | category | flops | bytes accessed | tf_op | source)
XLA Modules:
  0.0 313.8 jit_solution(16058411161820978897)
XLA Ops:
  0.0 2.4 pack.4.refs_2_.refs_1_
  2.4 4.9 %all-to-all-start = ((bf16[4,288,768]{2,1,0:T(8,128)(2,1)}), bf16[4,288,768]{2,1,0:T(8,128)(2,1)S(1)}, u32[]{:S(2)}, u32[]{:S(2)}) async-start(bf16[4,288,768]{2,1,0:T(8,128)(2,1)} %pack.4.refs_2_.refs_1_), calls=%async_computation | async-start | bytes 3538944 | tf_op jit(solution)/shard_map/all_to_all | solution.py:341
  7.3 2.4 pack.6.refs_0_
  9.7 38.7 %all-to-all-done = bf16[4,288,768]{2,1,0:T(8,128)(2,1)S(1)} async-done(((bf16[4,288,768]{2,1,0:T(8,128)(2,1)}), bf16[4,288,768]{2,1,0:T(8,128)(2,1)S(1)}, u32[]{:S(2)}, u32[]{:S(2)}) %all-to-all-start) | async-done | bytes 1769504 | tf_op jit(solution)/shard_map/all_to_all | solution.py:341
  49.7 3.7 %all-to-all-start.1 = ((bf16[4,288,768]{2,1,0:T(8,128)(2,1)}), bf16[4,288,768]{2,1,0:T(8,128)(2,1)S(1)}, u32[]{:S(2)}, u32[]{:S(2)}) async-start(bf16[4,288,768]{2,1,0:T(8,128)(2,1)} %gate.5), calls=%async_computation.1 | async-start | bytes 3538944 | tf_op jit(solution)/shard_map/all_to_all | solution.py:341
  55.3 3.6 %collective-permute-start.1 = (bf16[1152,768]{1,0:T(8,128)(2,1)S(1)}, bf16[1152,768]{1,0:T(8,128)(2,1)}, u32[]{:S(2)}, u32[]{:S(2)}) collective-permute-start(bf16[1152,768]{1,0:T(8,128)(2,1)S(1)} %bitcast.17), channel_id=1, source_target_pairs={{4,0},{8,4},{12,8},{16,12},{20,16},{24,20},{28,24},{5,1},{9,5},{13... | collective-permute-start | bytes 5308424 | tf_op jit(solution)/shard_map/ppermute | solution.py:345
  63.0 2.4 collective-permute-start.3
  66.9 2.4 pack.5.refs_0_
  69.3 23.0 %collective-permute-done.2.refs_4_.refs_6_ = bf16[288,384]{1,0:T(8,128)(2,1)S(1)} collective-permute-done((bf16[288,384]{1,0:T(8,128)(2,1)}, bf16[288,384]{1,0:T(8,128)(2,1)S(1)}, u32[]{:S(2)}, u32[]{:S(2)}) %collective-permute-start.2) | collective-permute-done | bytes 221216 | tf_op jit(solution)/shard_map/ppermute | solution.py:319
  92.3 17.0 %collective-permute-done.3.refs_5_.refs_7_ = bf16[288,384]{1,0:T(8,128)(2,1)S(1)} collective-permute-done((bf16[288,384]{1,0:T(8,128)(2,1)}, bf16[288,384]{1,0:T(8,128)(2,1)S(1)}, u32[]{:S(2)}, u32[]{:S(2)}) %collective-permute-start.3) | collective-permute-done | bytes 221216 | tf_op jit(solution)/shard_map/ppermute | solution.py:319
  111.3 6.5 %all-to-all-start.2 = ((bf16[4,288,768]{2,1,0:T(8,128)(2,1)}), bf16[4,288,768]{2,1,0:T(8,128)(2,1)S(1)}, u32[]{:S(2)}, u32[]{:S(2)}) async-start(bf16[4,288,768]{2,1,0:T(8,128)(2,1)} %gate.6.refs_10_), calls=%async_computation.2 | async-start | bytes 3538944 | tf_op jit(solution)/shard_map/all_to_all | solution.py:341
  119.8 3.6 %collective-permute-start.8 = (bf16[1152,768]{1,0:T(8,128)(2,1)S(1)}, bf16[1152,768]{1,0:T(8,128)(2,1)}, u32[]{:S(2)}, u32[]{:S(2)}) collective-permute-start(bf16[1152,768]{1,0:T(8,128)(2,1)S(1)} %bitcast.28), channel_id=1, source_target_pairs={{4,0},{8,4},{12,8},{16,12},{20,16},{24,20},{28,24},{5,1},{9,5},{13... | collective-permute-start | bytes 5308424 | tf_op jit(solution)/shard_map/ppermute | solution.py:345
  128.1 3.0 collective-permute-start.10
  133.2 16.2 %attend.4 = (bf16[288,384]{1,0:T(8,128)(2,1)}, bf16[288,384]{1,0:T(8,128)(2,1)}, bf16[288,384]{1,0:T(8,128)(2,1)}, bf16[288,384]{1,0:T(8,128)(2,1)}) custom-call(s32[12]{0:T(128)} %reshape.15.refs_0_, bf16[1152,768]{1,0:T(8,128)(2,1)} %bitcast.15, bf16[1152,768]{1,0:T(8,128)(2,1)} %collective-permute-done.refs_2_, ...), custom_call_target="tpu_custom_call" | custom-call | flops 18345885696 | bytes 7077888 | tf_op jit(solution)/shard_map/attend/pallas_call | solution.py:275
  149.4 2.6 pack.7.refs_0_
  152.0 15.8 %all-to-all-done.2.refs_0_ = bf16[4,288,768]{2,1,0:T(8,128)(2,1)S(1)} async-done(((bf16[4,288,768]{2,1,0:T(8,128)(2,1)}), bf16[4,288,768]{2,1,0:T(8,128)(2,1)S(1)}, u32[]{:S(2)}, u32[]{:S(2)}) %all-to-all-start.2) | async-done | bytes 1769504 | tf_op jit(solution)/shard_map/all_to_all | solution.py:341
  169.1 3.5 %collective-permute-done.10.refs_5_.refs_7_ = bf16[288,384]{1,0:T(8,128)(2,1)} collective-permute-done((bf16[288,384]{1,0:T(8,128)(2,1)}, bf16[288,384]{1,0:T(8,128)(2,1)}, u32[]{:S(2)}, u32[]{:S(2)}) %collective-permute-start.10) | collective-permute-done | bytes 221216 | tf_op jit(solution)/shard_map/ppermute | solution.py:319
  172.7 5.9 %all-to-all-start.3 = ((bf16[4,288,768]{2,1,0:T(8,128)(2,1)}), bf16[4,288,768]{2,1,0:T(8,128)(2,1)S(1)}, u32[]{:S(2)}, u32[]{:S(2)}) async-start(bf16[4,288,768]{2,1,0:T(8,128)(2,1)} %gate.8.refs_10_), calls=%async_computation.3 | async-start | bytes 3538944 | tf_op jit(solution)/shard_map/all_to_all | solution.py:341
  178.6 3.8 %collective-permute-start.12 = (bf16[288,384]{1,0:T(8,128)(2,1)}, bf16[288,384]{1,0:T(8,128)(2,1)S(1)}, u32[]{:S(2)}, u32[]{:S(2)}) collective-permute-start(bf16[288,384]{1,0:T(8,128)(2,1)} %get-tuple-element.39), channel_id=1, source_target_pairs={{0,3},{1,0},{2,1},{3,2},{4,7},{5,4},{6,5},{7,6},{8,11},{9,8},{10,9... | collective-permute-start | bytes 663560 | tf_op jit(solution)/shard_map/ppermute | solution.py:319
  185.5 3.6 %collective-permute-start.6 = (bf16[1152,768]{1,0:T(8,128)(2,1)S(1)}, bf16[1152,768]{1,0:T(8,128)(2,1)}, u32[]{:S(2)}, u32[]{:S(2)}) collective-permute-start(bf16[1152,768]{1,0:T(8,128)(2,1)S(1)} %bitcast.22), channel_id=1, source_target_pairs={{4,0},{8,4},{12,8},{16,12},{20,16},{24,20},{28,24},{5,1},{9,5},{13... | collective-permute-start | bytes 5308424 | tf_op jit(solution)/shard_map/ppermute | solution.py:345
  189.1 16.2 %attend.5 = (bf16[288,384]{1,0:T(8,128)(2,1)}, bf16[288,384]{1,0:T(8,128)(2,1)}, bf16[288,384]{1,0:T(8,128)(2,1)}, bf16[288,384]{1,0:T(8,128)(2,1)}) custom-call(s32[12]{0:T(128)} %reshape.15.refs_0_, bf16[1152,768]{1,0:T(8,128)(2,1)} %bitcast.26, bf16[1152,768]{1,0:T(8,128)(2,1)} %collective-permute-done.7.refs_2_, ...), custom_call_target="tpu_custom_call" | custom-call | flops 18345885696 | bytes 7077888 | tf_op jit(solution)/shard_map/attend/pallas_call | solution.py:275
  205.3 8.0 %collective-permute-done.12.refs_8_.refs_1_ = bf16[288,384]{1,0:T(8,128)(2,1)S(1)} collective-permute-done((bf16[288,384]{1,0:T(8,128)(2,1)}, bf16[288,384]{1,0:T(8,128)(2,1)S(1)}, u32[]{:S(2)}, u32[]{:S(2)}) %collective-permute-start.12) | collective-permute-done | bytes 221216 | tf_op jit(solution)/shard_map/ppermute | solution.py:319
  213.3 4.2 %collective-permute-start.20 = (bf16[288,384]{1,0:T(8,128)(2,1)}, bf16[288,384]{1,0:T(8,128)(2,1)}, u32[]{:S(2)}, u32[]{:S(2)}) collective-permute-start(bf16[288,384]{1,0:T(8,128)(2,1)} %get-tuple-element.46), channel_id=1, source_target_pairs={{0,3},{1,0},{2,1},{3,2},{4,7},{5,4},{6,5},{7,6},{8,11},{9,8},{10,9... | collective-permute-start | bytes 663560 | tf_op jit(solution)/shard_map/ppermute | solution.py:319
  217.5 21.3 %collective-permute-done.13.refs_9_.refs_2_ = bf16[288,384]{1,0:T(8,128)(2,1)S(1)} collective-permute-done((bf16[288,384]{1,0:T(8,128)(2,1)}, bf16[288,384]{1,0:T(8,128)(2,1)S(1)}, u32[]{:S(2)}, u32[]{:S(2)}) %collective-permute-start.13) | collective-permute-done | bytes 221216 | tf_op jit(solution)/shard_map/ppermute | solution.py:319
  238.8 9.6 %collective-permute-start.22 = (bf16[288,384]{1,0:T(8,128)(2,1)}, bf16[288,384]{1,0:T(8,128)(2,1)}, u32[]{:S(2)}, u32[]{:S(2)}) collective-permute-start(bf16[288,384]{1,0:T(8,128)(2,1)} %get-tuple-element.48), channel_id=1, source_target_pairs={{0,1},{1,2},{2,3},{3,0},{4,5},{5,6},{6,7},{7,4},{8,9},{9,10},{10,1... | collective-permute-start | bytes 663560 | tf_op jit(solution)/shard_map/ppermute | solution.py:319
  248.5 8.4 %collective-permute-done.21.refs_6_.refs_8_ = bf16[288,384]{1,0:T(8,128)(2,1)} collective-permute-done((bf16[288,384]{1,0:T(8,128)(2,1)}, bf16[288,384]{1,0:T(8,128)(2,1)}, u32[]{:S(2)}, u32[]{:S(2)}) %collective-permute-start.21) | collective-permute-done | bytes 221216 | tf_op jit(solution)/shard_map/ppermute | solution.py:319
  256.8 2.4 place.2.refs_10_.refs_8_
  263.5 3.6 %collective-permute-start.19 = (bf16[1152,256]{1,0:T(8,128)(2,1)S(1)}, bf16[1152,256]{1,0:T(8,128)(2,1)S(1)}, u32[]{:S(2)}, u32[]{:S(2)}) collective-permute-start(bf16[1152,256]{1,0:T(8,128)(2,1)S(1)} %slice.4), channel_id=1, source_target_pairs={{4,0},{8,4},{12,8},{16,12},{20,16},{24,20},{28,24},{5,1},{9,5},{13... | collective-permute-start | bytes 1769480 | tf_op jit(solution)/shard_map/ppermute | solution.py:345
  267.1 16.2 %attend.6 = (bf16[288,384]{1,0:T(8,128)(2,1)}, bf16[288,384]{1,0:T(8,128)(2,1)}, bf16[288,384]{1,0:T(8,128)(2,1)}, bf16[288,384]{1,0:T(8,128)(2,1)}) custom-call(s32[12]{0:T(128)} %reshape.15.refs_0_, bf16[1152,768]{1,0:T(8,128)(2,1)} %bitcast.20, bf16[1152,768]{1,0:T(8,128)(2,1)} %collective-permute-done.5.refs_2_, ...), custom_call_target="tpu_custom_call" | custom-call | flops 18345885696 | bytes 7077888 | tf_op jit(solution)/shard_map/attend/pallas_call | solution.py:275
  287.9 9.5 %attend.7 = (bf16[288,128]{1,0:T(8,128)(2,1)}, bf16[288,128]{1,0:T(8,128)(2,1)}, bf16[288,128]{1,0:T(8,128)(2,1)}, bf16[288,128]{1,0:T(8,128)(2,1)}) custom-call(s32[12]{0:T(128)} %reshape.15.refs_0_, bf16[1152,768]{1,0:T(8,128)(2,1)} %bitcast.32, bf16[1152,256]{1,0:T(8,128)(2,1)} %copy-done.19, bf16[1152,256]{1,0:T(8,128)(2,1)} %copy-done.20, ...), custom_call_target="tpu_custom_call" | custom-call | flops 6115295232 | bytes 2359296 | tf_op jit(solution)/shard_map/attend/pallas_call | solution.py:275
  301.0 7.7 %collective-permute-done.16.refs_2_ = bf16[288,384]{1,0:T(8,128)(2,1)S(1)} collective-permute-done((bf16[288,384]{1,0:T(8,128)(2,1)}, bf16[288,384]{1,0:T(8,128)(2,1)S(1)}, u32[]{:S(2)}, u32[]{:S(2)}) %collective-permute-start.16) | collective-permute-done | bytes 221216 | tf_op jit(solution)/shard_map/ppermute | solution.py:319
  311.4 2.2 place.3
  (93 shorter events, 38.6 us)
Async XLA Ops:
  2.4 46.1 %all-to-all-start = ((bf16[4,288,768]{2,1,0:T(8,128)(2,1)}), bf16[4,288,768]{2,1,0:T(8,128)(2,1)S(1)}, u32[]{:S(2)}, u32[]{:S(2)}) async-start(bf16[4,288,768]{2,1,0:T(8,128)(2,1)} %pack.4.refs_2_.refs_1_), calls=%async_computation | async-start | bytes 3538944 | tf_op jit(solution)/shard_map/all_to_all | solution.py:341
  49.7 60.3 %all-to-all-start.1 = ((bf16[4,288,768]{2,1,0:T(8,128)(2,1)}), bf16[4,288,768]{2,1,0:T(8,128)(2,1)S(1)}, u32[]{:S(2)}, u32[]{:S(2)}) async-start(bf16[4,288,768]{2,1,0:T(8,128)(2,1)} %gate.5), calls=%async_computation.1 | async-start | bytes 3538944 | tf_op jit(solution)/shard_map/all_to_all | solution.py:341
  53.4 55.9 %collective-permute-start = (bf16[1152,768]{1,0:T(8,128)(2,1)S(1)}, bf16[1152,768]{1,0:T(8,128)(2,1)}, u32[]{:S(2)}, u32[]{:S(2)}) collective-permute-start(bf16[1152,768]{1,0:T(8,128)(2,1)S(1)} %bitcast.16), channel_id=1, source_target_pairs={{0,4},{4,8},{8,12},{12,16},{16,20},{20,24},{24,28},{1,5},{5,9},{9,... | collective-permute-start | bytes 5308424 | tf_op jit(solution)/shard_map/ppermute | solution.py:345
  55.3 54.7 %collective-permute-start.1 = (bf16[1152,768]{1,0:T(8,128)(2,1)S(1)}, bf16[1152,768]{1,0:T(8,128)(2,1)}, u32[]{:S(2)}, u32[]{:S(2)}) collective-permute-start(bf16[1152,768]{1,0:T(8,128)(2,1)S(1)} %bitcast.17), channel_id=1, source_target_pairs={{4,0},{8,4},{12,8},{16,12},{20,16},{24,20},{28,24},{5,1},{9,5},{13... | collective-permute-start | bytes 5308424 | tf_op jit(solution)/shard_map/ppermute | solution.py:345
  61.0 31.2 %collective-permute-start.2 = (bf16[288,384]{1,0:T(8,128)(2,1)}, bf16[288,384]{1,0:T(8,128)(2,1)S(1)}, u32[]{:S(2)}, u32[]{:S(2)}) collective-permute-start(bf16[288,384]{1,0:T(8,128)(2,1)} %get-tuple-element.29), channel_id=1, source_target_pairs={{0,1},{1,2},{2,3},{3,0},{4,5},{5,6},{6,7},{7,4},{8,9},{9,10},{10,1... | collective-permute-start | bytes 663560 | tf_op jit(solution)/shard_map/ppermute | solution.py:319
  63.0 46.3 %collective-permute-start.3 = (bf16[288,384]{1,0:T(8,128)(2,1)}, bf16[288,384]{1,0:T(8,128)(2,1)S(1)}, u32[]{:S(2)}, u32[]{:S(2)}) collective-permute-start(bf16[288,384]{1,0:T(8,128)(2,1)} %get-tuple-element.30), channel_id=1, source_target_pairs={{0,2},{1,3},{2,0},{3,1},{4,6},{5,7},{6,4},{7,5},{8,10},{9,11},{10,... | collective-permute-start | bytes 663560 | tf_op jit(solution)/shard_map/ppermute | solution.py:319
  65.4 43.9 %collective-permute-start.4 = (bf16[288,384]{1,0:T(8,128)(2,1)}, bf16[288,384]{1,0:T(8,128)(2,1)}, u32[]{:S(2)}, u32[]{:S(2)}) collective-permute-start(bf16[288,384]{1,0:T(8,128)(2,1)} %get-tuple-element.31), channel_id=1, source_target_pairs={{0,3},{1,0},{2,1},{3,2},{4,7},{5,4},{6,5},{7,6},{8,11},{9,8},{10,9... | collective-permute-start | bytes 663560 | tf_op jit(solution)/shard_map/ppermute | solution.py:319
  111.3 56.6 %all-to-all-start.2 = ((bf16[4,288,768]{2,1,0:T(8,128)(2,1)}), bf16[4,288,768]{2,1,0:T(8,128)(2,1)S(1)}, u32[]{:S(2)}, u32[]{:S(2)}) async-start(bf16[4,288,768]{2,1,0:T(8,128)(2,1)} %gate.6.refs_10_), calls=%async_computation.2 | async-start | bytes 3538944 | tf_op jit(solution)/shard_map/all_to_all | solution.py:341
  117.8 54.8 %collective-permute-start.7 = (bf16[1152,768]{1,0:T(8,128)(2,1)S(1)}, bf16[1152,768]{1,0:T(8,128)(2,1)}, u32[]{:S(2)}, u32[]{:S(2)}) collective-permute-start(bf16[1152,768]{1,0:T(8,128)(2,1)S(1)} %bitcast.27), channel_id=1, source_target_pairs={{0,4},{4,8},{8,12},{12,16},{16,20},{20,24},{24,28},{1,5},{5,9},{9,... | collective-permute-start | bytes 5308424 | tf_op jit(solution)/shard_map/ppermute | solution.py:345
  119.8 52.9 %collective-permute-start.8 = (bf16[1152,768]{1,0:T(8,128)(2,1)S(1)}, bf16[1152,768]{1,0:T(8,128)(2,1)}, u32[]{:S(2)}, u32[]{:S(2)}) collective-permute-start(bf16[1152,768]{1,0:T(8,128)(2,1)S(1)} %bitcast.28), channel_id=1, source_target_pairs={{4,0},{8,4},{12,8},{16,12},{20,16},{24,20},{28,24},{5,1},{9,5},{13... | collective-permute-start | bytes 5308424 | tf_op jit(solution)/shard_map/ppermute | solution.py:345
  128.1 44.5 %collective-permute-start.10 = (bf16[288,384]{1,0:T(8,128)(2,1)}, bf16[288,384]{1,0:T(8,128)(2,1)}, u32[]{:S(2)}, u32[]{:S(2)}) collective-permute-start(bf16[288,384]{1,0:T(8,128)(2,1)} %get-tuple-element.36), channel_id=1, source_target_pairs={{0,2},{1,3},{2,0},{3,1},{4,6},{5,7},{6,4},{7,5},{8,10},{9,11},{10,... | collective-permute-start | bytes 663560 | tf_op jit(solution)/shard_map/ppermute | solution.py:319
  131.1 41.5 %collective-permute-start.11 = (bf16[288,384]{1,0:T(8,128)(2,1)}, bf16[288,384]{1,0:T(8,128)(2,1)}, u32[]{:S(2)}, u32[]{:S(2)}) collective-permute-start(bf16[288,384]{1,0:T(8,128)(2,1)} %get-tuple-element.37), channel_id=1, source_target_pairs={{0,3},{1,0},{2,1},{3,2},{4,7},{5,4},{6,5},{7,6},{8,11},{9,8},{10,9... | collective-permute-start | bytes 663560 | tf_op jit(solution)/shard_map/ppermute | solution.py:319
  132.6 40.1 %collective-permute-start.9 = (bf16[288,384]{1,0:T(8,128)(2,1)}, bf16[288,384]{1,0:T(8,128)(2,1)}, u32[]{:S(2)}, u32[]{:S(2)}) collective-permute-start(bf16[288,384]{1,0:T(8,128)(2,1)} %get-tuple-element.35), channel_id=1, source_target_pairs={{0,1},{1,2},{2,3},{3,0},{4,5},{5,6},{6,7},{7,4},{8,9},{9,10},{10,1... | collective-permute-start | bytes 663560 | tf_op jit(solution)/shard_map/ppermute | solution.py:319
  172.7 86.5 %all-to-all-start.3 = ((bf16[4,288,768]{2,1,0:T(8,128)(2,1)}), bf16[4,288,768]{2,1,0:T(8,128)(2,1)S(1)}, u32[]{:S(2)}, u32[]{:S(2)}) async-start(bf16[4,288,768]{2,1,0:T(8,128)(2,1)} %gate.8.refs_10_), calls=%async_computation.3 | async-start | bytes 3538944 | tf_op jit(solution)/shard_map/all_to_all | solution.py:341
  178.6 34.7 %collective-permute-start.12 = (bf16[288,384]{1,0:T(8,128)(2,1)}, bf16[288,384]{1,0:T(8,128)(2,1)S(1)}, u32[]{:S(2)}, u32[]{:S(2)}) collective-permute-start(bf16[288,384]{1,0:T(8,128)(2,1)} %get-tuple-element.39), channel_id=1, source_target_pairs={{0,3},{1,0},{2,1},{3,2},{4,7},{5,4},{6,5},{7,6},{8,11},{9,8},{10,9... | collective-permute-start | bytes 663560 | tf_op jit(solution)/shard_map/ppermute | solution.py:319
  182.4 56.4 %collective-permute-start.13 = (bf16[288,384]{1,0:T(8,128)(2,1)}, bf16[288,384]{1,0:T(8,128)(2,1)S(1)}, u32[]{:S(2)}, u32[]{:S(2)}) collective-permute-start(bf16[288,384]{1,0:T(8,128)(2,1)} %get-tuple-element.40), channel_id=1, source_target_pairs={{0,2},{1,3},{2,0},{3,1},{4,6},{5,7},{6,4},{7,5},{8,10},{9,11},{10,... | collective-permute-start | bytes 663560 | tf_op jit(solution)/shard_map/ppermute | solution.py:319
  182.4 56.4 %collective-permute-start.14 = (bf16[288,384]{1,0:T(8,128)(2,1)}, bf16[288,384]{1,0:T(8,128)(2,1)}, u32[]{:S(2)}, u32[]{:S(2)}) collective-permute-start(bf16[288,384]{1,0:T(8,128)(2,1)} %get-tuple-element.41), channel_id=1, source_target_pairs={{0,1},{1,2},{2,3},{3,0},{4,5},{5,6},{6,7},{7,4},{8,9},{9,10},{10,1... | collective-permute-start | bytes 663560 | tf_op jit(solution)/shard_map/ppermute | solution.py:319
  183.6 83.6 %collective-permute-start.5 = (bf16[1152,768]{1,0:T(8,128)(2,1)S(1)}, bf16[1152,768]{1,0:T(8,128)(2,1)}, u32[]{:S(2)}, u32[]{:S(2)}) collective-permute-start(bf16[1152,768]{1,0:T(8,128)(2,1)S(1)} %bitcast.21), channel_id=1, source_target_pairs={{0,4},{4,8},{8,12},{12,16},{16,20},{20,24},{24,28},{1,5},{5,9},{9,... | collective-permute-start | bytes 5308424 | tf_op jit(solution)/shard_map/ppermute | solution.py:345
  185.5 81.6 %collective-permute-start.6 = (bf16[1152,768]{1,0:T(8,128)(2,1)S(1)}, bf16[1152,768]{1,0:T(8,128)(2,1)}, u32[]{:S(2)}, u32[]{:S(2)}) collective-permute-start(bf16[1152,768]{1,0:T(8,128)(2,1)S(1)} %bitcast.22), channel_id=1, source_target_pairs={{4,0},{8,4},{12,8},{16,12},{20,16},{24,20},{28,24},{5,1},{9,5},{13... | collective-permute-start | bytes 5308424 | tf_op jit(solution)/shard_map/ppermute | solution.py:345
  213.3 43.5 %copy-start.12 = (bf16[288,384]{1,0:T(8,128)(2,1)}, bf16[288,384]{1,0:T(8,128)(2,1)S(1)}, u32[]{:S(2)}) copy-start(bf16[288,384]{1,0:T(8,128)(2,1)S(1)} %collective-permute-done.12.refs_8_.refs_1_) | copy-start | bytes 663556
  213.3 35.2 %collective-permute-start.20 = (bf16[288,384]{1,0:T(8,128)(2,1)}, bf16[288,384]{1,0:T(8,128)(2,1)}, u32[]{:S(2)}, u32[]{:S(2)}) collective-permute-start(bf16[288,384]{1,0:T(8,128)(2,1)} %get-tuple-element.46), channel_id=1, source_target_pairs={{0,3},{1,0},{2,1},{3,2},{4,7},{5,4},{6,5},{7,6},{8,11},{9,8},{10,9... | collective-permute-start | bytes 663560 | tf_op jit(solution)/shard_map/ppermute | solution.py:319
  238.8 18.0 %copy-start.13 = (bf16[288,384]{1,0:T(8,128)(2,1)}, bf16[288,384]{1,0:T(8,128)(2,1)S(1)}, u32[]{:S(2)}) copy-start(bf16[288,384]{1,0:T(8,128)(2,1)S(1)} %collective-permute-done.13.refs_9_.refs_2_) | copy-start | bytes 663556
  238.8 18.0 %collective-permute-start.21 = (bf16[288,384]{1,0:T(8,128)(2,1)}, bf16[288,384]{1,0:T(8,128)(2,1)}, u32[]{:S(2)}, u32[]{:S(2)}) collective-permute-start(bf16[288,384]{1,0:T(8,128)(2,1)} %get-tuple-element.47), channel_id=1, source_target_pairs={{0,2},{1,3},{2,0},{3,1},{4,6},{5,7},{6,4},{7,5},{8,10},{9,11},{10,... | collective-permute-start | bytes 663560 | tf_op jit(solution)/shard_map/ppermute | solution.py:319
  238.8 18.0 %collective-permute-start.22 = (bf16[288,384]{1,0:T(8,128)(2,1)}, bf16[288,384]{1,0:T(8,128)(2,1)}, u32[]{:S(2)}, u32[]{:S(2)}) collective-permute-start(bf16[288,384]{1,0:T(8,128)(2,1)} %get-tuple-element.48), channel_id=1, source_target_pairs={{0,1},{1,2},{2,3},{3,0},{4,5},{5,6},{6,7},{7,4},{8,9},{9,10},{10,1... | collective-permute-start | bytes 663560 | tf_op jit(solution)/shard_map/ppermute | solution.py:319
  261.5 25.3 %collective-permute-start.18 = (bf16[1152,256]{1,0:T(8,128)(2,1)S(1)}, bf16[1152,256]{1,0:T(8,128)(2,1)S(1)}, u32[]{:S(2)}, u32[]{:S(2)}) collective-permute-start(bf16[1152,256]{1,0:T(8,128)(2,1)S(1)} %slice.4), channel_id=1, source_target_pairs={{0,4},{4,8},{8,12},{12,16},{16,20},{20,24},{24,28},{1,5},{5,9},{9,... | collective-permute-start | bytes 1769480 | tf_op jit(solution)/shard_map/ppermute | solution.py:345
  263.5 23.4 %collective-permute-start.19 = (bf16[1152,256]{1,0:T(8,128)(2,1)S(1)}, bf16[1152,256]{1,0:T(8,128)(2,1)S(1)}, u32[]{:S(2)}, u32[]{:S(2)}) collective-permute-start(bf16[1152,256]{1,0:T(8,128)(2,1)S(1)} %slice.4), channel_id=1, source_target_pairs={{4,0},{8,4},{12,8},{16,12},{20,16},{24,20},{28,24},{5,1},{9,5},{13... | collective-permute-start | bytes 1769480 | tf_op jit(solution)/shard_map/ppermute | solution.py:345
  283.4 17.0 %collective-permute-start.15 = (bf16[288,384]{1,0:T(8,128)(2,1)}, bf16[288,384]{1,0:T(8,128)(2,1)S(1)}, u32[]{:S(2)}, u32[]{:S(2)}) collective-permute-start(bf16[288,384]{1,0:T(8,128)(2,1)} %get-tuple-element.43), channel_id=1, source_target_pairs={{0,3},{1,0},{2,1},{3,2},{4,7},{5,4},{6,5},{7,6},{8,11},{9,8},{10,9... | collective-permute-start | bytes 663560 | tf_op jit(solution)/shard_map/ppermute | solution.py:319
  284.9 23.9 %collective-permute-start.16 = (bf16[288,384]{1,0:T(8,128)(2,1)}, bf16[288,384]{1,0:T(8,128)(2,1)S(1)}, u32[]{:S(2)}, u32[]{:S(2)}) collective-permute-start(bf16[288,384]{1,0:T(8,128)(2,1)} %get-tuple-element.44), channel_id=1, source_target_pairs={{0,2},{1,3},{2,0},{3,1},{4,6},{5,7},{6,4},{7,5},{8,10},{9,11},{10,... | collective-permute-start | bytes 663560 | tf_op jit(solution)/shard_map/ppermute | solution.py:319
  284.9 23.9 %collective-permute-start.17 = (bf16[288,384]{1,0:T(8,128)(2,1)}, bf16[288,384]{1,0:T(8,128)(2,1)S(1)}, u32[]{:S(2)}, u32[]{:S(2)}) collective-permute-start(bf16[288,384]{1,0:T(8,128)(2,1)} %get-tuple-element.45), channel_id=1, source_target_pairs={{0,1},{1,2},{2,3},{3,0},{4,5},{5,6},{6,7},{7,4},{8,9},{9,10},{10,1... | collective-permute-start | bytes 663560 | tf_op jit(solution)/shard_map/ppermute | solution.py:319
  297.4 11.4 %collective-permute-start.23 = (bf16[288,128]{1,0:T(8,128)(2,1)}, bf16[288,128]{1,0:T(8,128)(2,1)S(1)}, u32[]{:S(2)}, u32[]{:S(2)}) collective-permute-start(bf16[288,128]{1,0:T(8,128)(2,1)} %get-tuple-element.50), channel_id=1, source_target_pairs={{0,3},{1,0},{2,1},{3,2},{4,7},{5,4},{6,5},{7,6},{8,11},{9,8},{10,9... | collective-permute-start | bytes 221192 | tf_op jit(solution)/shard_map/ppermute | solution.py:319
  299.3 11.5 %collective-permute-start.24 = (bf16[288,128]{1,0:T(8,128)(2,1)}, bf16[288,128]{1,0:T(8,128)(2,1)S(1)}, u32[]{:S(2)}, u32[]{:S(2)}) collective-permute-start(bf16[288,128]{1,0:T(8,128)(2,1)} %get-tuple-element.51), channel_id=1, source_target_pairs={{0,2},{1,3},{2,0},{3,1},{4,6},{5,7},{6,4},{7,5},{8,10},{9,11},{10,... | collective-permute-start | bytes 221192 | tf_op jit(solution)/shard_map/ppermute | solution.py:319
  300.4 10.3 %collective-permute-start.25 = (bf16[288,128]{1,0:T(8,128)(2,1)}, bf16[288,128]{1,0:T(8,128)(2,1)S(1)}, u32[]{:S(2)}, u32[]{:S(2)}) collective-permute-start(bf16[288,128]{1,0:T(8,128)(2,1)} %get-tuple-element.52), channel_id=1, source_target_pairs={{0,1},{1,2},{2,3},{3,0},{4,5},{5,6},{6,7},{7,4},{8,9},{9,10},{10,1... | collective-permute-start | bytes 221192 | tf_op jit(solution)/shard_map/ppermute | solution.py:319
  (19 other events, 76.5 us)

commit v4 on v3

--- a/solution.py
+++ b/solution.py
@@ -337,6 +337,9 @@
         blocks = pack_turned(queries, after, groups, group_width, *columns(i))
         return [blocks[0]] + [turn(blocks[shift], shift) for shift in range(1, groups)]
 
+    def back_home(outs):
+        return [outs[0]] + [turn(outs[shift], groups - shift) for shift in range(1, groups)]
+
     def arrive(i, after):
         own = lax.all_to_all(sent[i], "head", split_axis=0, concat_axis=0, tiled=True)
         own = gate(own, after) if after else own
@@ -349,19 +352,20 @@
     if count > 1:
         sent.append(gate(packed(1, sent), there[0][:1]))
     for i in range(by_permutes):
-        asks.append(asked(i, there[i - 1][:1] if i else sent[:1]))
+        asks.append(asked(i, there[i - 1][1:] if i else sent[:1]))
     for i, heads in enumerate(sizes):
         if i + 1 < count:
             there.append(arrive(i + 1, [part[1][0] for part in done[-1:]]))
         if i + 2 < count:
-            landed = [*there[i + 1][:1], *there[i][1:], *asks[i][1:]]
+            landed = [*there[i + 1][:1], *there[i][1:]] + [part[0] for part in asks[i + 1 :]]
             sent.append(gate(packed(i + 2, there[i][:1]), landed))
         hold = [part[0] for part in there[i + 1 :]] + sent[i + 2 :]
         hold += [part[1][0] for part in done[-1:]]
-        hold += [block for part in done[-2:-1] for block in part[1][1:]]
         hold += [part[0] for part in asks[i + 1 :]]
+        if 0 < i == count - 2:
+            hold += done[0][1][1:]
         if i + 1 == count and count > 2:
-            early = place(done[:-1], group_width, total_width)
+            early = place(done[:1], group_width, total_width)
             hold.append(early)
         if i < by_permutes:
             source, lane = asks[i], None
@@ -371,9 +375,13 @@
         outs = attend(
             plan, *there[i], keep_mask, source, lane, hold, groups, firsts[i], heads, tile_count
         )
-        back = [outs[0]] + [turn(outs[shift], groups - shift) for shift in range(1, groups)]
-        done.append((firsts[i] * head_size, back))
-    return place(done[-2:] if count > 2 else done, group_width, total_width, early)
+        done.append((firsts[i] * head_size, back_home(outs) if i == 0 else outs))
+    final = []
+    for i, (start, outs) in enumerate(done):
+        if 0 < i < count - 2:
+            outs = [outs[0]] + [gate(block, there[-1][:1]) for block in outs[1:]]
+        final.append((start, back_home(outs) if i else outs))
+    return place(final[1:] if count > 2 else final, group_width, total_width, early)
 
 
 def solution(mesh):

time: 317 us -> 344 us (1.085)
  waiting for transfers between devices: 146 us -> 164 us
  starting transfers between devices: 80 us -> 96.4 us
    ppermute x4, waiting for transfers between devices: 0.01 us -> 17.9 us  [arrive(): lax.ppermute(pairs, 'seq', backward)]
    ppermute x18, starting transfers between devices: 36.8 us -> 52.7 us  [turn(): lax.ppermute(array, 'head', [(i, (i + shift) % groups) for i in range(gro...]
    all_to_all x4, waiting for transfers between devices: 54.6 us -> 38.7 us  [arrive(): lax.all_to_all(sent[i], 'head', split_axis=0, concat_axis=0, tiled=True)]
    ppermute x4, waiting for transfers between devices: 0.01 us -> 15.9 us  [arrive(): lax.ppermute(pairs, 'seq', onward)]
    unnamed x43 -> x53, local copies, waits for them, and re-layouts: 9.27 us -> 7.53 us
  transfers between devices with their start and end apart: 30 -> 30, of which waited for: 10 -> 10; matrix products, arithmetic and copies ran while one was open for 1% -> 1% of each run, Pallas kernels for 23% -> 20%
where the time goes in v4:
time: 344 us
  waiting for transfers between devices  164 us (48%)
  starting transfers between devices  96.4 us (28%)
  Pallas kernels  73.5 us (21%)
  local copies, waits for them, and re-layouts  9.4 us (3%)
    ppermute x18, waiting for transfers between devices, turn(): lax.ppermute(array, 'head', [(i, (i + shift) % groups) for i in range(gro...  91.6 us
    pallas_call x4, Pallas kernels, attend(): pl.pallas_call(functools.partial(attend_kernel, groups, heads, first_head...  54.8 us
    ppermute x18, starting transfers between devices, turn(): lax.ppermute(array, 'head', [(i, (i + shift) % groups) for i in range(gro...  52.7 us
    all_to_all x4, waiting for transfers between devices, arrive(): lax.all_to_all(sent[i], 'head', split_axis=0, concat_axis=0, tiled=True)  38.7 us
    all_to_all x4, starting transfers between devices, arrive(): lax.all_to_all(sent[i], 'head', split_axis=0, concat_axis=0, tiled=True)  21.2 us
    ppermute x4, waiting for transfers between devices, arrive(): lax.ppermute(pairs, 'seq', backward)  17.9 us
    ppermute x4, waiting for transfers between devices, arrive(): lax.ppermute(pairs, 'seq', onward)  15.9 us
    ppermute x4, starting transfers between devices, arrive(): lax.ppermute(pairs, 'seq', backward)  14.1 us
  transfers between devices with their start and end apart: 30, of which 10 were waited for; matrix products, arithmetic and copies ran while one was open for 1% of the time, Pallas kernels for 20%

profile of v4, /device:TPU:2, one launch (start us, length us, event | category | flops | bytes accessed | tf_op | source)
XLA Modules:
  0.0 344.0 jit_solution(12354492404023911065)
XLA Ops:
  0.0 2.4 pack.4.refs_2_.refs_1_
  2.4 4.9 %all-to-all-start = ((bf16[4,288,768]{2,1,0:T(8,128)(2,1)}), bf16[4,288,768]{2,1,0:T(8,128)(2,1)S(1)}, u32[]{:S(2)}, u32[]{:S(2)}) async-start(bf16[4,288,768]{2,1,0:T(8,128)(2,1)} %pack.4.refs_2_.refs_1_), calls=%async_computation | async-start | bytes 3538944 | tf_op jit(solution)/shard_map/all_to_all | solution.py:344
  7.3 2.5 pack.5.refs_0_
  9.8 38.7 %all-to-all-done = bf16[4,288,768]{2,1,0:T(8,128)(2,1)S(1)} async-done(((bf16[4,288,768]{2,1,0:T(8,128)(2,1)}), bf16[4,288,768]{2,1,0:T(8,128)(2,1)S(1)}, u32[]{:S(2)}, u32[]{:S(2)}) %all-to-all-start) | async-done | bytes 1769504 | tf_op jit(solution)/shard_map/all_to_all | solution.py:344
  49.7 3.7 %all-to-all-start.1 = ((bf16[4,288,768]{2,1,0:T(8,128)(2,1)}), bf16[4,288,768]{2,1,0:T(8,128)(2,1)S(1)}, u32[]{:S(2)}, u32[]{:S(2)}) async-start(bf16[4,288,768]{2,1,0:T(8,128)(2,1)} %gate.8), calls=%async_computation.1 | async-start | bytes 3538944 | tf_op jit(solution)/shard_map/all_to_all | solution.py:344
  55.3 3.6 %collective-permute-start.3 = (bf16[1152,768]{1,0:T(8,128)(2,1)S(1)}, bf16[1152,768]{1,0:T(8,128)(2,1)}, u32[]{:S(2)}, u32[]{:S(2)}) collective-permute-start(bf16[1152,768]{1,0:T(8,128)(2,1)S(1)} %bitcast.24), channel_id=1, source_target_pairs={{4,0},{8,4},{12,8},{16,12},{20,16},{24,20},{28,24},{5,1},{9,5},{13... | collective-permute-start | bytes 5308424 | tf_op jit(solution)/shard_map/ppermute | solution.py:348
  59.0 2.4 pack.6.refs_0_
  61.4 15.9 %collective-permute-done.2.refs_1_.refs_2_ = bf16[1152,768]{1,0:T(8,128)(2,1)} collective-permute-done((bf16[1152,768]{1,0:T(8,128)(2,1)S(1)}, bf16[1152,768]{1,0:T(8,128)(2,1)}, u32[]{:S(2)}, u32[]{:S(2)}) %collective-permute-start.2) | collective-permute-done | bytes 1769504 | tf_op jit(solution)/shard_map/ppermute | solution.py:348
  77.4 17.9 %collective-permute-done.3.refs_2_.refs_3_ = bf16[1152,768]{1,0:T(8,128)(2,1)} collective-permute-done((bf16[1152,768]{1,0:T(8,128)(2,1)S(1)}, bf16[1152,768]{1,0:T(8,128)(2,1)}, u32[]{:S(2)}, u32[]{:S(2)}) %collective-permute-start.3) | collective-permute-done | bytes 1769504 | tf_op jit(solution)/shard_map/ppermute | solution.py:348
  98.5 5.0 %all-to-all-start.2 = ((bf16[4,288,768]{2,1,0:T(8,128)(2,1)}), bf16[4,288,768]{2,1,0:T(8,128)(2,1)S(1)}, u32[]{:S(2)}, u32[]{:S(2)}) async-start(bf16[4,288,768]{2,1,0:T(8,128)(2,1)} %gate.9.refs_10_), calls=%async_computation.2 | async-start | bytes 3538944 | tf_op jit(solution)/shard_map/all_to_all | solution.py:344
  111.6 2.4 collective-permute-start
  114.0 3.2 collective-permute-start.1
  120.0 2.6 pack.7.refs_0_
  122.6 19.3 %collective-permute-done.7.refs_6_ = bf16[288,384]{1,0:T(8,128)(2,1)} collective-permute-done((bf16[288,384]{1,0:T(8,128)(2,1)}, bf16[288,384]{1,0:T(8,128)(2,1)}, u32[]{:S(2)}, u32[]{:S(2)}) %collective-permute-start.7) | collective-permute-done | bytes 221216 | tf_op jit(solution)/shard_map/ppermute | solution.py:319
  142.0 17.9 %collective-permute-done.8.refs_7_ = bf16[288,384]{1,0:T(8,128)(2,1)} collective-permute-done((bf16[288,384]{1,0:T(8,128)(2,1)}, bf16[288,384]{1,0:T(8,128)(2,1)}, u32[]{:S(2)}, u32[]{:S(2)}) %collective-permute-start.8) | collective-permute-done | bytes 221216 | tf_op jit(solution)/shard_map/ppermute | solution.py:319
  159.9 15.2 %attend.4 = (bf16[288,384]{1,0:T(8,128)(2,1)}, bf16[288,384]{1,0:T(8,128)(2,1)}, bf16[288,384]{1,0:T(8,128)(2,1)}, bf16[288,384]{1,0:T(8,128)(2,1)}) custom-call(s32[12]{0:T(128)} %reshape.15.refs_0_, bf16[1152,768]{1,0:T(8,128)(2,1)} %bitcast.22, bf16[1152,768]{1,0:T(8,128)(2,1)} %collective-permute-done.2.refs_1_.refs_2_, ...), custom_call_target="tpu_custom_call" | custom-call | flops 18345885696 | bytes 7077888 | tf_op jit(solution)/shard_map/attend/pallas_call | solution.py:275
  176.4 7.6 %all-to-all-start.3 = ((bf16[4,288,768]{2,1,0:T(8,128)(2,1)}), bf16[4,288,768]{2,1,0:T(8,128)(2,1)S(1)}, u32[]{:S(2)}, u32[]{:S(2)}) async-start(bf16[4,288,768]{2,1,0:T(8,128)(2,1)} %gate.11.refs_10_), calls=%async_computation.3 | async-start | bytes 3538944 | tf_op jit(solution)/shard_map/all_to_all | solution.py:344
  186.0 2.4 collective-permute-start.5
  191.7 3.6 %collective-permute-start.14 = (bf16[1152,768]{1,0:T(8,128)(2,1)S(1)}, bf16[1152,768]{1,0:T(8,128)(2,1)}, u32[]{:S(2)}, u32[]{:S(2)}) collective-permute-start(bf16[1152,768]{1,0:T(8,128)(2,1)S(1)} %bitcast.35), channel_id=1, source_target_pairs={{4,0},{8,4},{12,8},{16,12},{20,16},{24,20},{28,24},{5,1},{9,5},{13... | collective-permute-start | bytes 5308424 | tf_op jit(solution)/shard_map/ppermute | solution.py:348
  195.4 27.4 %collective-permute-done.4.refs_6_ = bf16[288,384]{1,0:T(8,128)(2,1)S(1)} collective-permute-done((bf16[288,384]{1,0:T(8,128)(2,1)}, bf16[288,384]{1,0:T(8,128)(2,1)S(1)}, u32[]{:S(2)}, u32[]{:S(2)}) %collective-permute-start.4) | collective-permute-done | bytes 221216 | tf_op jit(solution)/shard_map/ppermute | solution.py:319
  222.8 17.9 %collective-permute-done.5.refs_7_ = bf16[288,384]{1,0:T(8,128)(2,1)S(1)} collective-permute-done((bf16[288,384]{1,0:T(8,128)(2,1)}, bf16[288,384]{1,0:T(8,128)(2,1)S(1)}, u32[]{:S(2)}, u32[]{:S(2)}) %collective-permute-start.5) | collective-permute-done | bytes 221216 | tf_op jit(solution)/shard_map/ppermute | solution.py:319
  240.7 5.4 %collective-permute-start.16 = (bf16[288,384]{1,0:T(8,128)(2,1)}, bf16[288,384]{1,0:T(8,128)(2,1)}, u32[]{:S(2)}, u32[]{:S(2)}) collective-permute-start(bf16[288,384]{1,0:T(8,128)(2,1)} %get-tuple-element.43), channel_id=1, source_target_pairs={{0,2},{1,3},{2,0},{3,1},{4,6},{5,7},{6,4},{7,5},{8,10},{9,11},{10,... | collective-permute-start | bytes 663560 | tf_op jit(solution)/shard_map/ppermute | solution.py:319
  246.1 10.3 %collective-permute-start.17 = (bf16[288,384]{1,0:T(8,128)(2,1)}, bf16[288,384]{1,0:T(8,128)(2,1)}, u32[]{:S(2)}, u32[]{:S(2)}) collective-permute-start(bf16[288,384]{1,0:T(8,128)(2,1)} %get-tuple-element.44), channel_id=1, source_target_pairs={{0,1},{1,2},{2,3},{3,0},{4,5},{5,6},{6,7},{7,4},{8,9},{9,10},{10,1... | collective-permute-start | bytes 663560 | tf_op jit(solution)/shard_map/ppermute | solution.py:319
  256.4 15.2 %attend.5 = (bf16[288,384]{1,0:T(8,128)(2,1)}, bf16[288,384]{1,0:T(8,128)(2,1)}, bf16[288,384]{1,0:T(8,128)(2,1)}, bf16[288,384]{1,0:T(8,128)(2,1)}) custom-call(s32[12]{0:T(128)} %reshape.15.refs_0_, bf16[1152,768]{1,0:T(8,128)(2,1)} %bitcast.28, bf16[1152,768]{1,0:T(8,128)(2,1)} %collective-permute-done.refs_2_, ...), custom_call_target="tpu_custom_call" | custom-call | flops 18345885696 | bytes 7077888 | tf_op jit(solution)/shard_map/attend/pallas_call | solution.py:275
  276.1 3.6 %collective-permute-start.22 = (bf16[1152,256]{1,0:T(8,128)(2,1)S(1)}, bf16[1152,256]{1,0:T(8,128)(2,1)S(1)}, u32[]{:S(2)}, u32[]{:S(2)}) collective-permute-start(bf16[1152,256]{1,0:T(8,128)(2,1)S(1)} %slice.4), channel_id=1, source_target_pairs={{4,0},{8,4},{12,8},{16,12},{20,16},{24,20},{28,24},{5,1},{9,5},{13... | collective-permute-start | bytes 1769480 | tf_op jit(solution)/shard_map/ppermute | solution.py:348
  279.8 15.2 %attend.6 = (bf16[288,384]{1,0:T(8,128)(2,1)}, bf16[288,384]{1,0:T(8,128)(2,1)}, bf16[288,384]{1,0:T(8,128)(2,1)}, bf16[288,384]{1,0:T(8,128)(2,1)}) custom-call(s32[12]{0:T(128)} %reshape.15.refs_0_, bf16[1152,768]{1,0:T(8,128)(2,1)} %bitcast.33, bf16[1152,768]{1,0:T(8,128)(2,1)} %collective-permute-done.13.refs_2_, ...), custom_call_target="tpu_custom_call" | custom-call | flops 18345885696 | bytes 7077888 | tf_op jit(solution)/shard_map/attend/pallas_call | solution.py:275
  299.3 3.0 collective-permute-done.18.refs_5_
  302.3 17.2 %collective-permute-start.12 = (bf16[288,384]{1,0:T(8,128)(2,1)S(1)}, bf16[288,384]{1,0:T(8,128)(2,1)S(1)}, u32[]{:S(2)}, u32[]{:S(2)}) collective-permute-start(bf16[288,384]{1,0:T(8,128)(2,1)S(1)} %copy-done.8), channel_id=1, source_target_pairs={{0,1},{1,2},{2,3},{3,0},{4,5},{5,6},{6,7},{7,4},{8,9},{9,10},{10,1... | collective-permute-start | bytes 663560 | tf_op jit(solution)/shard_map/ppermute | solution.py:319
  319.7 2.4 collective-permute-start.10
  322.1 9.1 %attend.7 = (bf16[288,128]{1,0:T(8,128)(2,1)}, bf16[288,128]{1,0:T(8,128)(2,1)}, bf16[288,128]{1,0:T(8,128)(2,1)}, bf16[288,128]{1,0:T(8,128)(2,1)}) custom-call(s32[12]{0:T(128)} %reshape.15.refs_0_, bf16[1152,768]{1,0:T(8,128)(2,1)} %bitcast.18, bf16[1152,256]{1,0:T(8,128)(2,1)} %copy-done.20, bf16[1152,256]{1,0:T(8,128)(2,1)} %copy-done.21, ...), custom_call_target="tpu_custom_call" | custom-call | flops 6115295232 | bytes 2359296 | tf_op jit(solution)/shard_map/attend/pallas_call | solution.py:275
  335.9 4.8 %collective-permute-done.24.refs_10_ = bf16[288,128]{1,0:T(8,128)(2,1)S(1)} collective-permute-done((bf16[288,128]{1,0:T(8,128)(2,1)}, bf16[288,128]{1,0:T(8,128)(2,1)S(1)}, u32[]{:S(2)}, u32[]{:S(2)}) %collective-permute-start.24) | collective-permute-done | bytes 73760 | tf_op jit(solution)/shard_map/ppermute | solution.py:319
  341.3 2.5 place.3
  (106 shorter events, 37.8 us)
Async XLA Ops:
  2.4 46.1 %all-to-all-start = ((bf16[4,288,768]{2,1,0:T(8,128)(2,1)}), bf16[4,288,768]{2,1,0:T(8,128)(2,1)S(1)}, u32[]{:S(2)}, u32[]{:S(2)}) async-start(bf16[4,288,768]{2,1,0:T(8,128)(2,1)} %pack.4.refs_2_.refs_1_), calls=%async_computation | async-start | bytes 3538944 | tf_op jit(solution)/shard_map/all_to_all | solution.py:344
  49.7 47.6 %all-to-all-start.1 = ((bf16[4,288,768]{2,1,0:T(8,128)(2,1)}), bf16[4,288,768]{2,1,0:T(8,128)(2,1)S(1)}, u32[]{:S(2)}, u32[]{:S(2)}) async-start(bf16[4,288,768]{2,1,0:T(8,128)(2,1)} %gate.8), calls=%async_computation.1 | async-start | bytes 3538944 | tf_op jit(solution)/shard_map/all_to_all | solution.py:344
  53.4 23.9 %collective-permute-start.2 = (bf16[1152,768]{1,0:T(8,128)(2,1)S(1)}, bf16[1152,768]{1,0:T(8,128)(2,1)}, u32[]{:S(2)}, u32[]{:S(2)}) collective-permute-start(bf16[1152,768]{1,0:T(8,128)(2,1)S(1)} %bitcast.23), channel_id=1, source_target_pairs={{0,4},{4,8},{8,12},{12,16},{16,20},{20,24},{24,28},{1,5},{5,9},{9,... | collective-permute-start | bytes 5308424 | tf_op jit(solution)/shard_map/ppermute | solution.py:348
  55.3 39.9 %collective-permute-start.3 = (bf16[1152,768]{1,0:T(8,128)(2,1)S(1)}, bf16[1152,768]{1,0:T(8,128)(2,1)}, u32[]{:S(2)}, u32[]{:S(2)}) collective-permute-start(bf16[1152,768]{1,0:T(8,128)(2,1)S(1)} %bitcast.24), channel_id=1, source_target_pairs={{4,0},{8,4},{12,8},{16,12},{20,16},{24,20},{28,24},{5,1},{9,5},{13... | collective-permute-start | bytes 5308424 | tf_op jit(solution)/shard_map/ppermute | solution.py:348
  98.5 76.6 %all-to-all-start.2 = ((bf16[4,288,768]{2,1,0:T(8,128)(2,1)}), bf16[4,288,768]{2,1,0:T(8,128)(2,1)S(1)}, u32[]{:S(2)}, u32[]{:S(2)}) async-start(bf16[4,288,768]{2,1,0:T(8,128)(2,1)} %gate.9.refs_10_), calls=%async_computation.2 | async-start | bytes 3538944 | tf_op jit(solution)/shard_map/all_to_all | solution.py:344
  105.7 36.2 %collective-permute-start.7 = (bf16[288,384]{1,0:T(8,128)(2,1)}, bf16[288,384]{1,0:T(8,128)(2,1)}, u32[]{:S(2)}, u32[]{:S(2)}) collective-permute-start(bf16[288,384]{1,0:T(8,128)(2,1)} %get-tuple-element.34), channel_id=1, source_target_pairs={{0,1},{1,2},{2,3},{3,0},{4,5},{5,6},{6,7},{7,4},{8,9},{9,10},{10,1... | collective-permute-start | bytes 663560 | tf_op jit(solution)/shard_map/ppermute | solution.py:319
  107.8 52.1 %collective-permute-start.8 = (bf16[288,384]{1,0:T(8,128)(2,1)}, bf16[288,384]{1,0:T(8,128)(2,1)}, u32[]{:S(2)}, u32[]{:S(2)}) collective-permute-start(bf16[288,384]{1,0:T(8,128)(2,1)} %get-tuple-element.35), channel_id=1, source_target_pairs={{0,2},{1,3},{2,0},{3,1},{4,6},{5,7},{6,4},{7,5},{8,10},{9,11},{10,... | collective-permute-start | bytes 663560 | tf_op jit(solution)/shard_map/ppermute | solution.py:319
  110.1 49.7 %collective-permute-start.9 = (bf16[288,384]{1,0:T(8,128)(2,1)}, bf16[288,384]{1,0:T(8,128)(2,1)}, u32[]{:S(2)}, u32[]{:S(2)}) collective-permute-start(bf16[288,384]{1,0:T(8,128)(2,1)} %get-tuple-element.36), channel_id=1, source_target_pairs={{0,3},{1,0},{2,1},{3,2},{4,7},{5,4},{6,5},{7,6},{8,11},{9,8},{10,9... | collective-permute-start | bytes 663560 | tf_op jit(solution)/shard_map/ppermute | solution.py:319
  111.6 64.7 %collective-permute-start = (bf16[1152,768]{1,0:T(8,128)(2,1)S(1)}, bf16[1152,768]{1,0:T(8,128)(2,1)}, u32[]{:S(2)}, u32[]{:S(2)}) collective-permute-start(bf16[1152,768]{1,0:T(8,128)(2,1)S(1)} %bitcast.29), channel_id=1, source_target_pairs={{0,4},{4,8},{8,12},{12,16},{16,20},{20,24},{24,28},{1,5},{5,9},{9,... | collective-permute-start | bytes 5308424 | tf_op jit(solution)/shard_map/ppermute | solution.py:348
  114.0 62.3 %collective-permute-start.1 = (bf16[1152,768]{1,0:T(8,128)(2,1)S(1)}, bf16[1152,768]{1,0:T(8,128)(2,1)}, u32[]{:S(2)}, u32[]{:S(2)}) collective-permute-start(bf16[1152,768]{1,0:T(8,128)(2,1)S(1)} %bitcast.30), channel_id=1, source_target_pairs={{4,0},{8,4},{12,8},{16,12},{20,16},{24,20},{28,24},{5,1},{9,5},{13... | collective-permute-start | bytes 5308424 | tf_op jit(solution)/shard_map/ppermute | solution.py:348
  176.4 95.3 %all-to-all-start.3 = ((bf16[4,288,768]{2,1,0:T(8,128)(2,1)}), bf16[4,288,768]{2,1,0:T(8,128)(2,1)S(1)}, u32[]{:S(2)}, u32[]{:S(2)}) async-start(bf16[4,288,768]{2,1,0:T(8,128)(2,1)} %gate.11.refs_10_), calls=%async_computation.3 | async-start | bytes 3538944 | tf_op jit(solution)/shard_map/all_to_all | solution.py:344
  184.0 38.8 %collective-permute-start.4 = (bf16[288,384]{1,0:T(8,128)(2,1)}, bf16[288,384]{1,0:T(8,128)(2,1)S(1)}, u32[]{:S(2)}, u32[]{:S(2)}) collective-permute-start(bf16[288,384]{1,0:T(8,128)(2,1)} %get-tuple-element.30), channel_id=1, source_target_pairs={{0,1},{1,2},{2,3},{3,0},{4,5},{5,6},{6,7},{7,4},{8,9},{9,10},{10,1... | collective-permute-start | bytes 663560 | tf_op jit(solution)/shard_map/ppermute | solution.py:319
  186.0 54.7 %collective-permute-start.5 = (bf16[288,384]{1,0:T(8,128)(2,1)}, bf16[288,384]{1,0:T(8,128)(2,1)S(1)}, u32[]{:S(2)}, u32[]{:S(2)}) collective-permute-start(bf16[288,384]{1,0:T(8,128)(2,1)} %get-tuple-element.31), channel_id=1, source_target_pairs={{0,2},{1,3},{2,0},{3,1},{4,6},{5,7},{6,4},{7,5},{8,10},{9,11},{10,... | collective-permute-start | bytes 663560 | tf_op jit(solution)/shard_map/ppermute | solution.py:319
  188.4 57.7 %collective-permute-start.6 = (bf16[288,384]{1,0:T(8,128)(2,1)}, bf16[288,384]{1,0:T(8,128)(2,1)}, u32[]{:S(2)}, u32[]{:S(2)}) collective-permute-start(bf16[288,384]{1,0:T(8,128)(2,1)} %get-tuple-element.32), channel_id=1, source_target_pairs={{0,3},{1,0},{2,1},{3,2},{4,7},{5,4},{6,5},{7,6},{8,11},{9,8},{10,9... | collective-permute-start | bytes 663560 | tf_op jit(solution)/shard_map/ppermute | solution.py:319
  189.8 89.9 %collective-permute-start.13 = (bf16[1152,768]{1,0:T(8,128)(2,1)S(1)}, bf16[1152,768]{1,0:T(8,128)(2,1)}, u32[]{:S(2)}, u32[]{:S(2)}) collective-permute-start(bf16[1152,768]{1,0:T(8,128)(2,1)S(1)} %bitcast.34), channel_id=1, source_target_pairs={{0,4},{4,8},{8,12},{12,16},{16,20},{20,24},{24,28},{1,5},{5,9},{9,... | collective-permute-start | bytes 5308424 | tf_op jit(solution)/shard_map/ppermute | solution.py:348
  191.7 88.0 %collective-permute-start.14 = (bf16[1152,768]{1,0:T(8,128)(2,1)S(1)}, bf16[1152,768]{1,0:T(8,128)(2,1)}, u32[]{:S(2)}, u32[]{:S(2)}) collective-permute-start(bf16[1152,768]{1,0:T(8,128)(2,1)S(1)} %bitcast.35), channel_id=1, source_target_pairs={{4,0},{8,4},{12,8},{16,12},{20,16},{24,20},{28,24},{5,1},{9,5},{13... | collective-permute-start | bytes 5308424 | tf_op jit(solution)/shard_map/ppermute | solution.py:348
  222.8 33.6 %copy-start.24 = (bf16[288,384]{1,0:T(8,128)(2,1)}, bf16[288,384]{1,0:T(8,128)(2,1)S(1)}, u32[]{:S(2)}) copy-start(bf16[288,384]{1,0:T(8,128)(2,1)S(1)} %collective-permute-done.4.refs_6_) | copy-start | bytes 663556
  222.8 51.2 %collective-permute-start.15 = (bf16[288,384]{1,0:T(8,128)(2,1)}, bf16[288,384]{1,0:T(8,128)(2,1)}, u32[]{:S(2)}, u32[]{:S(2)}) collective-permute-start(bf16[288,384]{1,0:T(8,128)(2,1)} %get-tuple-element.42), channel_id=1, source_target_pairs={{0,3},{1,0},{2,1},{3,2},{4,7},{5,4},{6,5},{7,6},{8,11},{9,8},{10,9... | collective-permute-start | bytes 663560 | tf_op jit(solution)/shard_map/ppermute | solution.py:319
  240.7 35.4 %collective-permute-start.16 = (bf16[288,384]{1,0:T(8,128)(2,1)}, bf16[288,384]{1,0:T(8,128)(2,1)}, u32[]{:S(2)}, u32[]{:S(2)}) collective-permute-start(bf16[288,384]{1,0:T(8,128)(2,1)} %get-tuple-element.43), channel_id=1, source_target_pairs={{0,2},{1,3},{2,0},{3,1},{4,6},{5,7},{6,4},{7,5},{8,10},{9,11},{10,... | collective-permute-start | bytes 663560 | tf_op jit(solution)/shard_map/ppermute | solution.py:319
  246.1 33.6 %collective-permute-start.17 = (bf16[288,384]{1,0:T(8,128)(2,1)}, bf16[288,384]{1,0:T(8,128)(2,1)}, u32[]{:S(2)}, u32[]{:S(2)}) collective-permute-start(bf16[288,384]{1,0:T(8,128)(2,1)} %get-tuple-element.44), channel_id=1, source_target_pairs={{0,1},{1,2},{2,3},{3,0},{4,5},{5,6},{6,7},{7,4},{8,9},{9,10},{10,1... | collective-permute-start | bytes 663560 | tf_op jit(solution)/shard_map/ppermute | solution.py:319
  274.0 45.6 %collective-permute-start.21 = (bf16[1152,256]{1,0:T(8,128)(2,1)S(1)}, bf16[1152,256]{1,0:T(8,128)(2,1)S(1)}, u32[]{:S(2)}, u32[]{:S(2)}) collective-permute-start(bf16[1152,256]{1,0:T(8,128)(2,1)S(1)} %slice.4), channel_id=1, source_target_pairs={{0,4},{4,8},{8,12},{12,16},{16,20},{20,24},{24,28},{1,5},{5,9},{9,... | collective-permute-start | bytes 1769480 | tf_op jit(solution)/shard_map/ppermute | solution.py:348
  276.1 43.6 %collective-permute-start.22 = (bf16[1152,256]{1,0:T(8,128)(2,1)S(1)}, bf16[1152,256]{1,0:T(8,128)(2,1)S(1)}, u32[]{:S(2)}, u32[]{:S(2)}) collective-permute-start(bf16[1152,256]{1,0:T(8,128)(2,1)S(1)} %slice.4), channel_id=1, source_target_pairs={{4,0},{8,4},{12,8},{16,12},{20,16},{24,20},{28,24},{5,1},{9,5},{13... | collective-permute-start | bytes 1769480 | tf_op jit(solution)/shard_map/ppermute | solution.py:348
  295.0 7.3 %collective-permute-start.18 = (bf16[288,384]{1,0:T(8,128)(2,1)}, bf16[288,384]{1,0:T(8,128)(2,1)S(1)}, u32[]{:S(2)}, u32[]{:S(2)}) collective-permute-start(bf16[288,384]{1,0:T(8,128)(2,1)} %get-tuple-element.46), channel_id=1, source_target_pairs={{0,3},{1,0},{2,1},{3,2},{4,7},{5,4},{6,5},{7,6},{8,11},{9,8},{10,9... | collective-permute-start | bytes 663560 | tf_op jit(solution)/shard_map/ppermute | solution.py:319
  297.3 34.0 %collective-permute-start.19 = (bf16[288,384]{1,0:T(8,128)(2,1)S(1)}, bf16[288,384]{1,0:T(8,128)(2,1)S(1)}, u32[]{:S(2)}, u32[]{:S(2)}) collective-permute-start(bf16[288,384]{1,0:T(8,128)(2,1)S(1)} %copy-done.23), channel_id=1, source_target_pairs={{0,2},{1,3},{2,0},{3,1},{4,6},{5,7},{6,4},{7,5},{8,10},{9,11},{10,... | collective-permute-start | bytes 663560 | tf_op jit(solution)/shard_map/ppermute | solution.py:319
  298.7 34.6 %collective-permute-start.20 = (bf16[288,384]{1,0:T(8,128)(2,1)S(1)}, bf16[288,384]{1,0:T(8,128)(2,1)S(1)}, u32[]{:S(2)}, u32[]{:S(2)}) collective-permute-start(bf16[288,384]{1,0:T(8,128)(2,1)S(1)} %copy-done.22), channel_id=1, source_target_pairs={{0,1},{1,2},{2,3},{3,0},{4,5},{5,6},{6,7},{7,4},{8,9},{9,10},{10,1... | collective-permute-start | bytes 663560 | tf_op jit(solution)/shard_map/ppermute | solution.py:319
  302.3 28.9 %copy-start.9 = (bf16[288,384]{1,0:T(8,128)(2,1)}, bf16[288,384]{1,0:T(8,128)(2,1)S(1)}, u32[]{:S(2)}) copy-start(bf16[288,384]{1,0:T(8,128)(2,1)S(1)} %collective-permute-done.18.refs_5_) | copy-start | bytes 663556
  302.3 31.0 %collective-permute-start.12 = (bf16[288,384]{1,0:T(8,128)(2,1)S(1)}, bf16[288,384]{1,0:T(8,128)(2,1)S(1)}, u32[]{:S(2)}, u32[]{:S(2)}) collective-permute-start(bf16[288,384]{1,0:T(8,128)(2,1)S(1)} %copy-done.8), channel_id=1, source_target_pairs={{0,1},{1,2},{2,3},{3,0},{4,5},{5,6},{6,7},{7,4},{8,9},{9,10},{10,1... | collective-permute-start | bytes 663560 | tf_op jit(solution)/shard_map/ppermute | solution.py:319
  319.6 15.1 %collective-permute-start.11 = (bf16[288,384]{1,0:T(8,128)(2,1)S(1)}, bf16[288,384]{1,0:T(8,128)(2,1)S(1)}, u32[]{:S(2)}, u32[]{:S(2)}) collective-permute-start(bf16[288,384]{1,0:T(8,128)(2,1)S(1)} %copy-done.7), channel_id=1, source_target_pairs={{0,2},{1,3},{2,0},{3,1},{4,6},{5,7},{6,4},{7,5},{8,10},{9,11},{10,... | collective-permute-start | bytes 663560 | tf_op jit(solution)/shard_map/ppermute | solution.py:319
  319.7 15.0 %collective-permute-start.10 = (bf16[288,384]{1,0:T(8,128)(2,1)}, bf16[288,384]{1,0:T(8,128)(2,1)S(1)}, u32[]{:S(2)}, u32[]{:S(2)}) collective-permute-start(bf16[288,384]{1,0:T(8,128)(2,1)} %gate.13), channel_id=1, source_target_pairs={{0,3},{1,0},{2,1},{3,2},{4,7},{5,4},{6,5},{7,6},{8,11},{9,8},{10,9... | collective-permute-start | bytes 663560 | tf_op jit(solution)/shard_map/ppermute | solution.py:319
  331.2 4.6 %collective-permute-start.23 = (bf16[288,128]{1,0:T(8,128)(2,1)}, bf16[288,128]{1,0:T(8,128)(2,1)S(1)}, u32[]{:S(2)}, u32[]{:S(2)}) collective-permute-start(bf16[288,128]{1,0:T(8,128)(2,1)} %get-tuple-element.50), channel_id=1, source_target_pairs={{0,3},{1,0},{2,1},{3,2},{4,7},{5,4},{6,5},{7,6},{8,11},{9,8},{10,9... | collective-permute-start | bytes 221192 | tf_op jit(solution)/shard_map/ppermute | solution.py:319
  333.3 7.4 %collective-permute-start.24 = (bf16[288,128]{1,0:T(8,128)(2,1)}, bf16[288,128]{1,0:T(8,128)(2,1)S(1)}, u32[]{:S(2)}, u32[]{:S(2)}) collective-permute-start(bf16[288,128]{1,0:T(8,128)(2,1)} %get-tuple-element.51), channel_id=1, source_target_pairs={{0,2},{1,3},{2,0},{3,1},{4,6},{5,7},{6,4},{7,5},{8,10},{9,11},{10,... | collective-permute-start | bytes 221192 | tf_op jit(solution)/shard_map/ppermute | solution.py:319
  333.3 7.4 %collective-permute-start.25 = (bf16[288,128]{1,0:T(8,128)(2,1)}, bf16[288,128]{1,0:T(8,128)(2,1)S(1)}, u32[]{:S(2)}, u32[]{:S(2)}) collective-permute-start(bf16[288,128]{1,0:T(8,128)(2,1)} %get-tuple-element.52), channel_id=1, source_target_pairs={{0,1},{1,2},{2,3},{3,0},{4,5},{5,6},{6,7},{7,4},{8,9},{9,10},{10,1... | collective-permute-start | bytes 221192 | tf_op jit(solution)/shard_map/ppermute | solution.py:319
  (24 other events, 138.6 us)

commit v5 on v2

--- a/solution.py
+++ b/solution.py
@@ -292,7 +292,7 @@
         out_shape=[jax.ShapeDtypeStruct((local_rows, width), jnp.bfloat16)] * groups,
         compiler_params=pltpu.CompilerParams(vmem_limit_bytes=VMEM_LIMIT),
         cost_estimate=pl.CostEstimate(
-            flops=12 * pairs * head_size,
+            flops=16 * pairs * head_size,
             bytes_accessed=16 * slab_rows * width,
             transcendentals=pairs,
         ),
@@ -319,10 +319,9 @@
     sizes = [(group_heads - 1 + i) // parts for i in reversed(range(parts))] + [1]
     count = len(sizes)
     firsts = [sum(sizes[:i]) for i in range(count)]
-    with_permutes = min(2, count - 1)
 
     def packed(i, after):
-        arrays = (key_vectors, value_vectors, queries)[: 3 - (i < with_permutes)]
+        arrays = (key_vectors, value_vectors, queries)[: 2 + (i + 1 == count)]
         start, width = firsts[i] * head_size, sizes[i] * head_size
         return pack(arrays, after, groups, group_width, start, width)
 
@@ -341,22 +340,26 @@
     sent, there, asks, done, early = [packed(0, [])], [], [], [], None
     there.append(arrive(0, []))
     if count > 1:
+        asks.append(asked(0, sent))
         sent.append(gate(packed(1, sent), there[0][:1]))
-    for i in range(with_permutes):
-        asks.append(asked(i, there[i - 1][:1] if i else sent[:1]))
+    if count > 2:
+        asks.append(asked(1, there[0][:1]))
     for i, heads in enumerate(sizes):
         if i + 1 < count:
             there.append(arrive(i + 1, [part[1][0] for part in done[-1:]]))
         if i + 2 < count:
             sent.append(gate(packed(i + 2, there[i][:1]), there[i + 1][:1]))
+            if i:
+                asks.append(asked(i + 1, done[i - 1][1][1:] + sent[i + 2 :]))
         hold = [part[0] for part in there[i + 1 :]] + sent[i + 2 :]
         hold += [part[1][0] for part in done[-1:]]
         hold += [block for part in done[-2:-1] for block in part[1][1:]]
-        hold += [part[0] for part in asks[i + 1 :]]
+        if i == 0:
+            hold += [part[0] for part in asks[1:]]
         if i + 1 == count and count > 2:
             early = place(done[:-1], group_width, total_width)
             hold.append(early)
-        pieces = asks[i] if i < with_permutes else []
+        pieces = asks[i] if i + 1 < count else []
         outs = attend(
             plan, *there[i], keep_mask, pieces, hold, groups, firsts[i], heads, tile_count
         )

time: 337 us -> 330 us (0.979)
  waiting for transfers between devices: 163 us -> 141 us
  starting transfers between devices: 70.9 us -> 90.7 us
    ppermute x18 -> x21, waiting for transfers between devices: 86.3 us -> 69.2 us  [turn(): lax.ppermute(array, 'head', [(i, (i + shift) % groups) for i in range(gro...]
    ppermute x18 -> x21, starting transfers between devices: 34.3 us -> 45.8 us  [turn(): lax.ppermute(array, 'head', [(i, (i + shift) % groups) for i in range(gro...]
    all_to_all x4, starting transfers between devices: 15.7 us -> 22.7 us  [arrive(): lax.all_to_all(sent[i], 'head', split_axis=0, concat_axis=0, tiled=True)]
    all_to_all x4, waiting for transfers between devices: 76.6 us -> 71.3 us  [arrive(): lax.all_to_all(sent[i], 'head', split_axis=0, concat_axis=0, tiled=True)]
    unnamed x55 -> x47, local copies, waits for them, and re-layouts: 10.6 us -> 9.8 us
  transfers between devices with their start and end apart: 30 -> 33, of which waited for: 9 -> 10; matrix products, arithmetic and copies ran while one was open for 1% -> 1% of each run, Pallas kernels for 24% -> 24%
where the time goes in v5:
time: 330 us; the launch traced here: 328 us
  waiting for transfers between devices  141 us (43%)
  starting transfers between devices  90.7 us (27%)
  Pallas kernels  84.9 us (26%)
  local copies, waits for them, and re-layouts  11.6 us (4%)
    all_to_all x4, waiting for transfers between devices, arrive(): lax.all_to_all(sent[i], 'head', split_axis=0, concat_axis=0, tiled=True)  71.3 us
    ppermute x21, waiting for transfers between devices, turn(): lax.ppermute(array, 'head', [(i, (i + shift) % groups) for i in range(gro...  69.2 us
    pallas_call x4, Pallas kernels, attend(): pl.pallas_call(functools.partial(attend_kernel, groups, heads, first_head...  64.8 us
    ppermute x21, starting transfers between devices, turn(): lax.ppermute(array, 'head', [(i, (i + shift) % groups) for i in range(gro...  45.8 us
    all_to_all x4, starting transfers between devices, arrive(): lax.all_to_all(sent[i], 'head', split_axis=0, concat_axis=0, tiled=True)  22.7 us
    ppermute x4, starting transfers between devices, arrive(): lax.ppermute(pairs, 'seq', backward)  14.5 us
    unnamed x47, local copies, waits for them, and re-layouts  9.8 us
    pallas_call x4, Pallas kernels, pack(): pl.pallas_call(kernel, in_specs=[ANY] * (len(arrays) + len(after)), out_s...  9.47 us
  transfers between devices with their start and end apart: 33, of which 10 were waited for; matrix products, arithmetic and copies ran while one was open for 1% of the time, Pallas kernels for 24%

profile of v5, /device:TPU:2, one launch (start us, length us, event | category | flops | bytes accessed | tf_op | source)
XLA Modules:
  0.0 328.4 jit_solution(1030265531945501235)
XLA Ops:
  0.0 2.4 pack.4.refs_2_.refs_1_
  2.4 4.9 %all-to-all-start = ((bf16[4,288,768]{2,1,0:T(8,128)(2,1)}), bf16[4,288,768]{2,1,0:T(8,128)(2,1)S(1)}, u32[]{:S(2)}, u32[]{:S(2)}) async-start(bf16[4,288,768]{2,1,0:T(8,128)(2,1)} %pack.4.refs_2_.refs_1_), calls=%async_computation | async-start | bytes 3538944 | tf_op jit(solution)/shard_map/all_to_all | solution.py:334
  7.3 2.4 pack.6.refs_0_
  9.7 38.7 %all-to-all-done = bf16[4,288,768]{2,1,0:T(8,128)(2,1)S(1)} async-done(((bf16[4,288,768]{2,1,0:T(8,128)(2,1)}), bf16[4,288,768]{2,1,0:T(8,128)(2,1)S(1)}, u32[]{:S(2)}, u32[]{:S(2)}) %all-to-all-start) | async-done | bytes 1769504 | tf_op jit(solution)/shard_map/all_to_all | solution.py:334
  49.7 3.7 %all-to-all-start.1 = ((bf16[4,288,768]{2,1,0:T(8,128)(2,1)}), bf16[4,288,768]{2,1,0:T(8,128)(2,1)S(1)}, u32[]{:S(2)}, u32[]{:S(2)}) async-start(bf16[4,288,768]{2,1,0:T(8,128)(2,1)} %gate.5), calls=%async_computation.1 | async-start | bytes 3538944 | tf_op jit(solution)/shard_map/all_to_all | solution.py:334
  55.3 3.6 %collective-permute-start.1 = (bf16[1152,768]{1,0:T(8,128)(2,1)S(1)}, bf16[1152,768]{1,0:T(8,128)(2,1)}, u32[]{:S(2)}, u32[]{:S(2)}) collective-permute-start(bf16[1152,768]{1,0:T(8,128)(2,1)S(1)} %bitcast.17), channel_id=1, source_target_pairs={{4,0},{8,4},{12,8},{16,12},{20,16},{24,20},{28,24},{5,1},{9,5},{13... | collective-permute-start | bytes 5308424 | tf_op jit(solution)/shard_map/ppermute | solution.py:338
  59.0 2.5 pack.5.refs_0_
  61.5 32.6 %all-to-all-done.1 = bf16[4,288,768]{2,1,0:T(8,128)(2,1)S(1)} async-done(((bf16[4,288,768]{2,1,0:T(8,128)(2,1)}), bf16[4,288,768]{2,1,0:T(8,128)(2,1)S(1)}, u32[]{:S(2)}, u32[]{:S(2)}) %all-to-all-start.1) | async-done | bytes 1769504 | tf_op jit(solution)/shard_map/all_to_all | solution.py:334
  95.2 3.6 %all-to-all-start.2 = ((bf16[4,288,768]{2,1,0:T(8,128)(2,1)}), bf16[4,288,768]{2,1,0:T(8,128)(2,1)S(1)}, u32[]{:S(2)}, u32[]{:S(2)}) async-start(bf16[4,288,768]{2,1,0:T(8,128)(2,1)} %gate.6.refs_10_), calls=%async_computation.2 | async-start | bytes 3538944 | tf_op jit(solution)/shard_map/all_to_all | solution.py:334
  102.9 2.4 collective-permute-start.3
  111.5 26.3 %collective-permute-done.2.refs_6_ = bf16[288,384]{1,0:T(8,128)(2,1)} collective-permute-done((bf16[288,384]{1,0:T(8,128)(2,1)}, bf16[288,384]{1,0:T(8,128)(2,1)}, u32[]{:S(2)}, u32[]{:S(2)}) %collective-permute-start.2) | collective-permute-done | bytes 221216 | tf_op jit(solution)/shard_map/ppermute | solution.py:316
  137.8 16.6 %collective-permute-start.15 = (bf16[288,384]{1,0:T(8,128)(2,1)}, bf16[288,384]{1,0:T(8,128)(2,1)}, u32[]{:S(2)}, u32[]{:S(2)}) collective-permute-start(bf16[288,384]{1,0:T(8,128)(2,1)} %get-tuple-element.46), channel_id=1, source_target_pairs={{0,1},{1,2},{2,3},{3,0},{4,5},{5,6},{6,7},{7,4},{8,9},{9,10},{10,1... | collective-permute-start | bytes 663560 | tf_op jit(solution)/shard_map/ppermute | solution.py:316
  154.4 7.5 %collective-permute-done.3.refs_7_ = bf16[288,384]{1,0:T(8,128)(2,1)} collective-permute-done((bf16[288,384]{1,0:T(8,128)(2,1)}, bf16[288,384]{1,0:T(8,128)(2,1)}, u32[]{:S(2)}, u32[]{:S(2)}) %collective-permute-start.3) | collective-permute-done | bytes 221216 | tf_op jit(solution)/shard_map/ppermute | solution.py:316
  163.9 3.6 %collective-permute-start.14 = (bf16[1152,768]{1,0:T(8,128)(2,1)}, bf16[1152,768]{1,0:T(8,128)(2,1)}, u32[]{:S(2)}, u32[]{:S(2)}) collective-permute-start(bf16[1152,768]{1,0:T(8,128)(2,1)} %bitcast.25), channel_id=1, source_target_pairs={{4,0},{8,4},{12,8},{16,12},{20,16},{24,20},{28,24},{5,1},{9,5},{13... | collective-permute-start | bytes 5308424 | tf_op jit(solution)/shard_map/ppermute | solution.py:338
  167.6 18.2 %attend.4 = (bf16[288,384]{1,0:T(8,128)(2,1)}, bf16[288,384]{1,0:T(8,128)(2,1)}, bf16[288,384]{1,0:T(8,128)(2,1)}, bf16[288,384]{1,0:T(8,128)(2,1)}) custom-call(s32[12]{0:T(128)} %reshape.15.refs_0_, bf16[1152,768]{1,0:T(8,128)(2,1)} %bitcast.15, bf16[1152,768]{1,0:T(8,128)(2,1)} %collective-permute-done.refs_2_, ...), custom_call_target="tpu_custom_call" | custom-call | flops 24461180928 | bytes 7077888 | tf_op jit(solution)/shard_map/attend/pallas_call | solution.py:272
  189.2 10.5 %all-to-all-start.3 = ((bf16[4,288,384]{2,1,0:T(8,128)(2,1)}), bf16[4,288,384]{2,1,0:T(8,128)(2,1)S(1)}, u32[]{:S(2)}, u32[]{:S(2)}) async-start(bf16[4,288,384]{2,1,0:T(8,128)(2,1)} %gate.8.refs_4_.refs_10_), calls=%async_computation.3 | async-start | bytes 1769472 | tf_op jit(solution)/shard_map/all_to_all | solution.py:334
  199.7 3.8 %collective-permute-start.7 = (bf16[288,384]{1,0:T(8,128)(2,1)S(1)}, bf16[288,384]{1,0:T(8,128)(2,1)S(1)}, u32[]{:S(2)}, u32[]{:S(2)}) collective-permute-start(bf16[288,384]{1,0:T(8,128)(2,1)S(1)} %copy-done.22), channel_id=1, source_target_pairs={{0,3},{1,0},{2,1},{3,2},{4,7},{5,4},{6,5},{7,6},{8,11},{9,8},{10,9... | collective-permute-start | bytes 663560 | tf_op jit(solution)/shard_map/ppermute | solution.py:316
  206.6 3.6 %collective-permute-start.6 = (bf16[1152,768]{1,0:T(8,128)(2,1)S(1)}, bf16[1152,768]{1,0:T(8,128)(2,1)}, u32[]{:S(2)}, u32[]{:S(2)}) collective-permute-start(bf16[1152,768]{1,0:T(8,128)(2,1)S(1)} %bitcast.22), channel_id=1, source_target_pairs={{4,0},{8,4},{12,8},{16,12},{20,16},{24,20},{28,24},{5,1},{9,5},{13... | collective-permute-start | bytes 5308424 | tf_op jit(solution)/shard_map/ppermute | solution.py:338
  210.3 18.2 %attend.5 = (bf16[288,384]{1,0:T(8,128)(2,1)}, bf16[288,384]{1,0:T(8,128)(2,1)}, bf16[288,384]{1,0:T(8,128)(2,1)}, bf16[288,384]{1,0:T(8,128)(2,1)}) custom-call(s32[12]{0:T(128)} %reshape.15.refs_0_, bf16[1152,768]{1,0:T(8,128)(2,1)} %bitcast.28, bf16[1152,768]{1,0:T(8,128)(2,1)} %collective-permute-done.13.refs_2_, ...), custom_call_target="tpu_custom_call" | custom-call | flops 24461180928 | bytes 7077888 | tf_op jit(solution)/shard_map/attend/pallas_call | solution.py:272
  228.5 6.3 %collective-permute-start.23 = (bf16[288,384]{1,0:T(8,128)(2,1)}, bf16[288,384]{1,0:T(8,128)(2,1)S(1)}, u32[]{:S(2)}, u32[]{:S(2)}) collective-permute-start(bf16[288,384]{1,0:T(8,128)(2,1)} %get-tuple-element.54), channel_id=1, source_target_pairs={{0,3},{1,0},{2,1},{3,2},{4,7},{5,4},{6,5},{7,6},{8,11},{9,8},{10,9... | collective-permute-start | bytes 663560 | tf_op jit(solution)/shard_map/ppermute | solution.py:316
  234.8 17.1 %collective-permute-done.8.refs_2_.refs_12_ = bf16[288,384]{1,0:T(8,128)(2,1)S(1)} collective-permute-done((bf16[288,384]{1,0:T(8,128)(2,1)}, bf16[288,384]{1,0:T(8,128)(2,1)S(1)}, u32[]{:S(2)}, u32[]{:S(2)}) %collective-permute-start.8) | collective-permute-done | bytes 221216 | tf_op jit(solution)/shard_map/ppermute | solution.py:316
  254.7 2.8 collective-permute-start.10
  257.5 9.8 %collective-permute-done.24.refs_6_.refs_7_ = bf16[288,384]{1,0:T(8,128)(2,1)S(1)} collective-permute-done((bf16[288,384]{1,0:T(8,128)(2,1)}, bf16[288,384]{1,0:T(8,128)(2,1)S(1)}, u32[]{:S(2)}, u32[]{:S(2)}) %collective-permute-start.24) | collective-permute-done | bytes 221216 | tf_op jit(solution)/shard_map/ppermute | solution.py:316
  268.1 2.4 place.2.refs_9_.refs_8_
  274.5 3.6 %collective-permute-start.22 = (bf16[1152,256]{1,0:T(8,128)(2,1)S(1)}, bf16[1152,256]{1,0:T(8,128)(2,1)S(1)}, u32[]{:S(2)}, u32[]{:S(2)}) collective-permute-start(bf16[1152,256]{1,0:T(8,128)(2,1)S(1)} %slice.4), channel_id=1, source_target_pairs={{4,0},{8,4},{12,8},{16,12},{20,16},{24,20},{28,24},{5,1},{9,5},{13... | collective-permute-start | bytes 1769480 | tf_op jit(solution)/shard_map/ppermute | solution.py:338
  278.2 18.3 %attend.6 = (bf16[288,384]{1,0:T(8,128)(2,1)}, bf16[288,384]{1,0:T(8,128)(2,1)}, bf16[288,384]{1,0:T(8,128)(2,1)}, bf16[288,384]{1,0:T(8,128)(2,1)}) custom-call(s32[12]{0:T(128)} %reshape.15.refs_0_, bf16[1152,768]{1,0:T(8,128)(2,1)} %bitcast.20, bf16[1152,768]{1,0:T(8,128)(2,1)} %collective-permute-done.5.refs_2_, ...), custom_call_target="tpu_custom_call" | custom-call | flops 24461180928 | bytes 7077888 | tf_op jit(solution)/shard_map/attend/pallas_call | solution.py:272
  296.4 3.7 %collective-permute-start.18 = (bf16[288,384]{1,0:T(8,128)(2,1)}, bf16[288,384]{1,0:T(8,128)(2,1)S(1)}, u32[]{:S(2)}, u32[]{:S(2)}) collective-permute-start(bf16[288,384]{1,0:T(8,128)(2,1)} %get-tuple-element.51), channel_id=1, source_target_pairs={{0,3},{1,0},{2,1},{3,2},{4,7},{5,4},{6,5},{7,6},{8,11},{9,8},{10,9... | collective-permute-start | bytes 663560 | tf_op jit(solution)/shard_map/ppermute | solution.py:316
  302.4 10.1 %attend.7 = (bf16[288,128]{1,0:T(8,128)(2,1)}, bf16[288,128]{1,0:T(8,128)(2,1)}, bf16[288,128]{1,0:T(8,128)(2,1)}, bf16[288,128]{1,0:T(8,128)(2,1)}) custom-call(s32[12]{0:T(128)} %reshape.15.refs_0_, bf16[1152,384]{1,0:T(8,128)(2,1)} %bitcast.31, bf16[1152,256]{1,0:T(8,128)(2,1)} %copy-done.20, bf16[1152,256]{1,0:T(8,128)(2,1)} %copy-done.21, ...), custom_call_target="tpu_custom_call" | custom-call | flops 8153726976 | bytes 2359296 | tf_op jit(solution)/shard_map/attend/pallas_call | solution.py:272
  312.5 2.7 collective-permute-start.26
  316.2 2.6 collective-permute-done.26.refs_5_
  320.6 4.6 %collective-permute-done.28.refs_7_ = bf16[288,128]{1,0:T(8,128)(2,1)S(1)} collective-permute-done((bf16[288,128]{1,0:T(8,128)(2,1)}, bf16[288,128]{1,0:T(8,128)(2,1)S(1)}, u32[]{:S(2)}, u32[]{:S(2)}) %collective-permute-start.28) | collective-permute-done | bytes 73760 | tf_op jit(solution)/shard_map/ppermute | solution.py:316
  326.1 2.2 place.3
  (104 shorter events, 36.5 us)
Async XLA Ops:
  2.4 46.1 %all-to-all-start = ((bf16[4,288,768]{2,1,0:T(8,128)(2,1)}), bf16[4,288,768]{2,1,0:T(8,128)(2,1)S(1)}, u32[]{:S(2)}, u32[]{:S(2)}) async-start(bf16[4,288,768]{2,1,0:T(8,128)(2,1)} %pack.4.refs_2_.refs_1_), calls=%async_computation | async-start | bytes 3538944 | tf_op jit(solution)/shard_map/all_to_all | solution.py:334
  49.7 44.4 %all-to-all-start.1 = ((bf16[4,288,768]{2,1,0:T(8,128)(2,1)}), bf16[4,288,768]{2,1,0:T(8,128)(2,1)S(1)}, u32[]{:S(2)}, u32[]{:S(2)}) async-start(bf16[4,288,768]{2,1,0:T(8,128)(2,1)} %gate.5), calls=%async_computation.1 | async-start | bytes 3538944 | tf_op jit(solution)/shard_map/all_to_all | solution.py:334
  53.4 108.6 %collective-permute-start = (bf16[1152,768]{1,0:T(8,128)(2,1)S(1)}, bf16[1152,768]{1,0:T(8,128)(2,1)}, u32[]{:S(2)}, u32[]{:S(2)}) collective-permute-start(bf16[1152,768]{1,0:T(8,128)(2,1)S(1)} %bitcast.16), channel_id=1, source_target_pairs={{0,4},{4,8},{8,12},{12,16},{16,20},{20,24},{24,28},{1,5},{5,9},{9,... | collective-permute-start | bytes 5308424 | tf_op jit(solution)/shard_map/ppermute | solution.py:338
  55.3 108.6 %collective-permute-start.1 = (bf16[1152,768]{1,0:T(8,128)(2,1)S(1)}, bf16[1152,768]{1,0:T(8,128)(2,1)}, u32[]{:S(2)}, u32[]{:S(2)}) collective-permute-start(bf16[1152,768]{1,0:T(8,128)(2,1)S(1)} %bitcast.17), channel_id=1, source_target_pairs={{4,0},{8,4},{12,8},{16,12},{20,16},{24,20},{28,24},{5,1},{9,5},{13... | collective-permute-start | bytes 5308424 | tf_op jit(solution)/shard_map/ppermute | solution.py:338
  95.2 92.7 %all-to-all-start.2 = ((bf16[4,288,768]{2,1,0:T(8,128)(2,1)}), bf16[4,288,768]{2,1,0:T(8,128)(2,1)S(1)}, u32[]{:S(2)}, u32[]{:S(2)}) async-start(bf16[4,288,768]{2,1,0:T(8,128)(2,1)} %gate.6.refs_10_), calls=%async_computation.2 | async-start | bytes 3538944 | tf_op jit(solution)/shard_map/all_to_all | solution.py:334
  100.9 36.9 %collective-permute-start.2 = (bf16[288,384]{1,0:T(8,128)(2,1)}, bf16[288,384]{1,0:T(8,128)(2,1)}, u32[]{:S(2)}, u32[]{:S(2)}) collective-permute-start(bf16[288,384]{1,0:T(8,128)(2,1)} %get-tuple-element.34), channel_id=1, source_target_pairs={{0,1},{1,2},{2,3},{3,0},{4,5},{5,6},{6,7},{7,4},{8,9},{9,10},{10,1... | collective-permute-start | bytes 663560 | tf_op jit(solution)/shard_map/ppermute | solution.py:316
  102.9 59.0 %collective-permute-start.3 = (bf16[288,384]{1,0:T(8,128)(2,1)}, bf16[288,384]{1,0:T(8,128)(2,1)}, u32[]{:S(2)}, u32[]{:S(2)}) collective-permute-start(bf16[288,384]{1,0:T(8,128)(2,1)} %get-tuple-element.35), channel_id=1, source_target_pairs={{0,2},{1,3},{2,0},{3,1},{4,6},{5,7},{6,4},{7,5},{8,10},{9,11},{10,... | collective-permute-start | bytes 663560 | tf_op jit(solution)/shard_map/ppermute | solution.py:316
  105.3 56.7 %collective-permute-start.4 = (bf16[288,384]{1,0:T(8,128)(2,1)}, bf16[288,384]{1,0:T(8,128)(2,1)}, u32[]{:S(2)}, u32[]{:S(2)}) collective-permute-start(bf16[288,384]{1,0:T(8,128)(2,1)} %get-tuple-element.36), channel_id=1, source_target_pairs={{0,3},{1,0},{2,1},{3,2},{4,7},{5,4},{6,5},{7,6},{8,11},{9,8},{10,9... | collective-permute-start | bytes 663560 | tf_op jit(solution)/shard_map/ppermute | solution.py:316
  137.8 61.9 %collective-permute-start.15 = (bf16[288,384]{1,0:T(8,128)(2,1)}, bf16[288,384]{1,0:T(8,128)(2,1)}, u32[]{:S(2)}, u32[]{:S(2)}) collective-permute-start(bf16[288,384]{1,0:T(8,128)(2,1)} %get-tuple-element.46), channel_id=1, source_target_pairs={{0,1},{1,2},{2,3},{3,0},{4,5},{5,6},{6,7},{7,4},{8,9},{9,10},{10,1... | collective-permute-start | bytes 663560 | tf_op jit(solution)/shard_map/ppermute | solution.py:316
  162.0 41.6 %collective-permute-start.16 = (bf16[288,384]{1,0:T(8,128)(2,1)}, bf16[288,384]{1,0:T(8,128)(2,1)}, u32[]{:S(2)}, u32[]{:S(2)}) collective-permute-start(bf16[288,384]{1,0:T(8,128)(2,1)} %get-tuple-element.47), channel_id=1, source_target_pairs={{0,2},{1,3},{2,0},{3,1},{4,6},{5,7},{6,4},{7,5},{8,10},{9,11},{10,... | collective-permute-start | bytes 663560 | tf_op jit(solution)/shard_map/ppermute | solution.py:316
  162.0 41.6 %collective-permute-start.17 = (bf16[288,384]{1,0:T(8,128)(2,1)}, bf16[288,384]{1,0:T(8,128)(2,1)}, u32[]{:S(2)}, u32[]{:S(2)}) collective-permute-start(bf16[288,384]{1,0:T(8,128)(2,1)} %get-tuple-element.48), channel_id=1, source_target_pairs={{0,3},{1,0},{2,1},{3,2},{4,7},{5,4},{6,5},{7,6},{8,11},{9,8},{10,9... | collective-permute-start | bytes 663560 | tf_op jit(solution)/shard_map/ppermute | solution.py:316
  162.0 42.7 %collective-permute-start.13 = (bf16[1152,768]{1,0:T(8,128)(2,1)}, bf16[1152,768]{1,0:T(8,128)(2,1)}, u32[]{:S(2)}, u32[]{:S(2)}) collective-permute-start(bf16[1152,768]{1,0:T(8,128)(2,1)} %bitcast.24), channel_id=1, source_target_pairs={{0,4},{4,8},{8,12},{12,16},{16,20},{20,24},{24,28},{1,5},{5,9},{9,... | collective-permute-start | bytes 5308424 | tf_op jit(solution)/shard_map/ppermute | solution.py:338
  163.9 42.7 %collective-permute-start.14 = (bf16[1152,768]{1,0:T(8,128)(2,1)}, bf16[1152,768]{1,0:T(8,128)(2,1)}, u32[]{:S(2)}, u32[]{:S(2)}) collective-permute-start(bf16[1152,768]{1,0:T(8,128)(2,1)} %bitcast.25), channel_id=1, source_target_pairs={{4,0},{8,4},{12,8},{16,12},{20,16},{24,20},{28,24},{5,1},{9,5},{13... | collective-permute-start | bytes 5308424 | tf_op jit(solution)/shard_map/ppermute | solution.py:338
  189.2 81.2 %all-to-all-start.3 = ((bf16[4,288,384]{2,1,0:T(8,128)(2,1)}), bf16[4,288,384]{2,1,0:T(8,128)(2,1)S(1)}, u32[]{:S(2)}, u32[]{:S(2)}) async-start(bf16[4,288,384]{2,1,0:T(8,128)(2,1)} %gate.8.refs_4_.refs_10_), calls=%async_computation.3 | async-start | bytes 1769472 | tf_op jit(solution)/shard_map/all_to_all | solution.py:334
  199.7 28.8 %collective-permute-start.7 = (bf16[288,384]{1,0:T(8,128)(2,1)S(1)}, bf16[288,384]{1,0:T(8,128)(2,1)S(1)}, u32[]{:S(2)}, u32[]{:S(2)}) collective-permute-start(bf16[288,384]{1,0:T(8,128)(2,1)S(1)} %copy-done.22), channel_id=1, source_target_pairs={{0,3},{1,0},{2,1},{3,2},{4,7},{5,4},{6,5},{7,6},{8,11},{9,8},{10,9... | collective-permute-start | bytes 663560 | tf_op jit(solution)/shard_map/ppermute | solution.py:316
  203.5 48.3 %collective-permute-start.8 = (bf16[288,384]{1,0:T(8,128)(2,1)}, bf16[288,384]{1,0:T(8,128)(2,1)S(1)}, u32[]{:S(2)}, u32[]{:S(2)}) collective-permute-start(bf16[288,384]{1,0:T(8,128)(2,1)} %get-tuple-element.40), channel_id=1, source_target_pairs={{0,2},{1,3},{2,0},{3,1},{4,6},{5,7},{6,4},{7,5},{8,10},{9,11},{10,... | collective-permute-start | bytes 663560 | tf_op jit(solution)/shard_map/ppermute | solution.py:316
  203.6 48.3 %collective-permute-start.9 = (bf16[288,384]{1,0:T(8,128)(2,1)}, bf16[288,384]{1,0:T(8,128)(2,1)S(1)}, u32[]{:S(2)}, u32[]{:S(2)}) collective-permute-start(bf16[288,384]{1,0:T(8,128)(2,1)} %get-tuple-element.41), channel_id=1, source_target_pairs={{0,1},{1,2},{2,3},{3,0},{4,5},{5,6},{6,7},{7,4},{8,9},{9,10},{10,1... | collective-permute-start | bytes 663560 | tf_op jit(solution)/shard_map/ppermute | solution.py:316
  204.7 73.5 %collective-permute-start.5 = (bf16[1152,768]{1,0:T(8,128)(2,1)S(1)}, bf16[1152,768]{1,0:T(8,128)(2,1)}, u32[]{:S(2)}, u32[]{:S(2)}) collective-permute-start(bf16[1152,768]{1,0:T(8,128)(2,1)S(1)} %bitcast.21), channel_id=1, source_target_pairs={{0,4},{4,8},{8,12},{12,16},{16,20},{20,24},{24,28},{1,5},{5,9},{9,... | collective-permute-start | bytes 5308424 | tf_op jit(solution)/shard_map/ppermute | solution.py:338
  206.6 71.5 %collective-permute-start.6 = (bf16[1152,768]{1,0:T(8,128)(2,1)S(1)}, bf16[1152,768]{1,0:T(8,128)(2,1)}, u32[]{:S(2)}, u32[]{:S(2)}) collective-permute-start(bf16[1152,768]{1,0:T(8,128)(2,1)S(1)} %bitcast.22), channel_id=1, source_target_pairs={{4,0},{8,4},{12,8},{16,12},{20,16},{24,20},{28,24},{5,1},{9,5},{13... | collective-permute-start | bytes 5308424 | tf_op jit(solution)/shard_map/ppermute | solution.py:338
  228.5 26.2 %collective-permute-start.23 = (bf16[288,384]{1,0:T(8,128)(2,1)}, bf16[288,384]{1,0:T(8,128)(2,1)S(1)}, u32[]{:S(2)}, u32[]{:S(2)}) collective-permute-start(bf16[288,384]{1,0:T(8,128)(2,1)} %get-tuple-element.54), channel_id=1, source_target_pairs={{0,3},{1,0},{2,1},{3,2},{4,7},{5,4},{6,5},{7,6},{8,11},{9,8},{10,9... | collective-permute-start | bytes 663560 | tf_op jit(solution)/shard_map/ppermute | solution.py:316
  251.8 15.4 %collective-permute-start.24 = (bf16[288,384]{1,0:T(8,128)(2,1)}, bf16[288,384]{1,0:T(8,128)(2,1)S(1)}, u32[]{:S(2)}, u32[]{:S(2)}) collective-permute-start(bf16[288,384]{1,0:T(8,128)(2,1)} %get-tuple-element.55), channel_id=1, source_target_pairs={{0,2},{1,3},{2,0},{3,1},{4,6},{5,7},{6,4},{7,5},{8,10},{9,11},{10,... | collective-permute-start | bytes 663560 | tf_op jit(solution)/shard_map/ppermute | solution.py:316
  251.9 15.4 %collective-permute-start.25 = (bf16[288,384]{1,0:T(8,128)(2,1)}, bf16[288,384]{1,0:T(8,128)(2,1)S(1)}, u32[]{:S(2)}, u32[]{:S(2)}) collective-permute-start(bf16[288,384]{1,0:T(8,128)(2,1)} %get-tuple-element.56), channel_id=1, source_target_pairs={{0,1},{1,2},{2,3},{3,0},{4,5},{5,6},{6,7},{7,4},{8,9},{9,10},{10,1... | collective-permute-start | bytes 663560 | tf_op jit(solution)/shard_map/ppermute | solution.py:316
  254.7 17.8 %collective-permute-start.10 = (bf16[288,384]{1,0:T(8,128)(2,1)}, bf16[288,384]{1,0:T(8,128)(2,1)}, u32[]{:S(2)}, u32[]{:S(2)}) collective-permute-start(bf16[288,384]{1,0:T(8,128)(2,1)} %get-tuple-element.43), channel_id=1, source_target_pairs={{0,1},{1,2},{2,3},{3,0},{4,5},{5,6},{6,7},{7,4},{8,9},{9,10},{10,1... | collective-permute-start | bytes 663560 | tf_op jit(solution)/shard_map/ppermute | solution.py:316
  267.3 7.3 %collective-permute-start.11 = (bf16[288,384]{1,0:T(8,128)(2,1)}, bf16[288,384]{1,0:T(8,128)(2,1)}, u32[]{:S(2)}, u32[]{:S(2)}) collective-permute-start(bf16[288,384]{1,0:T(8,128)(2,1)} %get-tuple-element.44), channel_id=1, source_target_pairs={{0,2},{1,3},{2,0},{3,1},{4,6},{5,7},{6,4},{7,5},{8,10},{9,11},{10,... | collective-permute-start | bytes 663560 | tf_op jit(solution)/shard_map/ppermute | solution.py:316
  267.3 10.8 %collective-permute-start.12 = (bf16[288,384]{1,0:T(8,128)(2,1)}, bf16[288,384]{1,0:T(8,128)(2,1)}, u32[]{:S(2)}, u32[]{:S(2)}) collective-permute-start(bf16[288,384]{1,0:T(8,128)(2,1)} %get-tuple-element.45), channel_id=1, source_target_pairs={{0,3},{1,0},{2,1},{3,2},{4,7},{5,4},{6,5},{7,6},{8,11},{9,8},{10,9... | collective-permute-start | bytes 663560 | tf_op jit(solution)/shard_map/ppermute | solution.py:316
  272.5 28.8 %collective-permute-start.21 = (bf16[1152,256]{1,0:T(8,128)(2,1)S(1)}, bf16[1152,256]{1,0:T(8,128)(2,1)S(1)}, u32[]{:S(2)}, u32[]{:S(2)}) collective-permute-start(bf16[1152,256]{1,0:T(8,128)(2,1)S(1)} %slice.4), channel_id=1, source_target_pairs={{0,4},{4,8},{8,12},{12,16},{16,20},{20,24},{24,28},{1,5},{5,9},{9,... | collective-permute-start | bytes 1769480 | tf_op jit(solution)/shard_map/ppermute | solution.py:338
  274.5 26.8 %collective-permute-start.22 = (bf16[1152,256]{1,0:T(8,128)(2,1)S(1)}, bf16[1152,256]{1,0:T(8,128)(2,1)S(1)}, u32[]{:S(2)}, u32[]{:S(2)}) collective-permute-start(bf16[1152,256]{1,0:T(8,128)(2,1)S(1)} %slice.4), channel_id=1, source_target_pairs={{4,0},{8,4},{12,8},{16,12},{20,16},{24,20},{28,24},{5,1},{9,5},{13... | collective-permute-start | bytes 1769480 | tf_op jit(solution)/shard_map/ppermute | solution.py:338
  296.4 28.8 %collective-permute-start.18 = (bf16[288,384]{1,0:T(8,128)(2,1)}, bf16[288,384]{1,0:T(8,128)(2,1)S(1)}, u32[]{:S(2)}, u32[]{:S(2)}) collective-permute-start(bf16[288,384]{1,0:T(8,128)(2,1)} %get-tuple-element.51), channel_id=1, source_target_pairs={{0,3},{1,0},{2,1},{3,2},{4,7},{5,4},{6,5},{7,6},{8,11},{9,8},{10,9... | collective-permute-start | bytes 663560 | tf_op jit(solution)/shard_map/ppermute | solution.py:316
  300.1 25.1 %collective-permute-start.19 = (bf16[288,384]{1,0:T(8,128)(2,1)}, bf16[288,384]{1,0:T(8,128)(2,1)S(1)}, u32[]{:S(2)}, u32[]{:S(2)}) collective-permute-start(bf16[288,384]{1,0:T(8,128)(2,1)} %get-tuple-element.52), channel_id=1, source_target_pairs={{0,2},{1,3},{2,0},{3,1},{4,6},{5,7},{6,4},{7,5},{8,10},{9,11},{10,... | collective-permute-start | bytes 663560 | tf_op jit(solution)/shard_map/ppermute | solution.py:316
  300.1 25.1 %collective-permute-start.20 = (bf16[288,384]{1,0:T(8,128)(2,1)}, bf16[288,384]{1,0:T(8,128)(2,1)S(1)}, u32[]{:S(2)}, u32[]{:S(2)}) collective-permute-start(bf16[288,384]{1,0:T(8,128)(2,1)} %get-tuple-element.53), channel_id=1, source_target_pairs={{0,1},{1,2},{2,3},{3,0},{4,5},{5,6},{6,7},{7,4},{8,9},{9,10},{10,1... | collective-permute-start | bytes 663560 | tf_op jit(solution)/shard_map/ppermute | solution.py:316
  312.5 6.4 %collective-permute-start.26 = (bf16[288,128]{1,0:T(8,128)(2,1)}, bf16[288,128]{1,0:T(8,128)(2,1)S(1)}, u32[]{:S(2)}, u32[]{:S(2)}) collective-permute-start(bf16[288,128]{1,0:T(8,128)(2,1)} %get-tuple-element.58), channel_id=1, source_target_pairs={{0,3},{1,0},{2,1},{3,2},{4,7},{5,4},{6,5},{7,6},{8,11},{9,8},{10,9... | collective-permute-start | bytes 221192 | tf_op jit(solution)/shard_map/ppermute | solution.py:316
  318.9 6.4 %collective-permute-start.28 = (bf16[288,128]{1,0:T(8,128)(2,1)}, bf16[288,128]{1,0:T(8,128)(2,1)S(1)}, u32[]{:S(2)}, u32[]{:S(2)}) collective-permute-start(bf16[288,128]{1,0:T(8,128)(2,1)} %get-tuple-element.60), channel_id=1, source_target_pairs={{0,1},{1,2},{2,3},{3,0},{4,5},{5,6},{6,7},{7,4},{8,9},{9,10},{10,1... | collective-permute-start | bytes 221192 | tf_op jit(solution)/shard_map/ppermute | solution.py:316
  (24 other events, 110.6 us)

commit v6 on v5

--- a/solution.py
+++ b/solution.py
@@ -321,7 +321,7 @@
     firsts = [sum(sizes[:i]) for i in range(count)]
 
     def packed(i, after):
-        arrays = (key_vectors, value_vectors, queries)[: 2 + (i + 1 == count)]
+        arrays = (key_vectors, value_vectors)
         start, width = firsts[i] * head_size, sizes[i] * head_size
         return pack(arrays, after, groups, group_width, start, width)
 
@@ -330,38 +330,31 @@
         blocks = pack_turned(queries, after, groups, group_width, start, width)
         return [blocks[0]] + [turn(blocks[shift], shift) for shift in range(1, groups)]
 
-    def arrive(i, after):
-        own = lax.all_to_all(sent[i], "head", split_axis=0, concat_axis=0, tiled=True)
+    def arrive(parts, after):
+        own = lax.all_to_all(parts, "head", split_axis=0, concat_axis=0, tiled=True)
         own = gate(own, after) if after else own
         own = own.reshape(-1, own.shape[2])
-        pairs = own[:, : 2 * sizes[i] * head_size]
-        return own, lax.ppermute(pairs, "seq", onward), lax.ppermute(pairs, "seq", backward)
-
-    sent, there, asks, done, early = [packed(0, [])], [], [], [], None
-    there.append(arrive(0, []))
+        return own, lax.ppermute(own, "seq", onward), lax.ppermute(own, "seq", backward)
+
+    sent = [packed(0, [])]
+    there, asks, done, early = [arrive(sent[0], [])], [asked(0, sent)], [], None
     if count > 1:
-        asks.append(asked(0, sent))
         sent.append(gate(packed(1, sent), there[0][:1]))
-    if count > 2:
         asks.append(asked(1, there[0][:1]))
     for i, heads in enumerate(sizes):
         if i + 1 < count:
-            there.append(arrive(i + 1, [part[1][0] for part in done[-1:]]))
+            there.append(arrive(sent[i + 1], [part[1][0] for part in done[-1:]]))
         if i + 2 < count:
             sent.append(gate(packed(i + 2, there[i][:1]), there[i + 1][:1]))
-            if i:
-                asks.append(asked(i + 1, done[i - 1][1][1:] + sent[i + 2 :]))
-        hold = [part[0] for part in there[i + 1 :]] + sent[i + 2 :]
+            asks.append(asked(i + 2, there[i + 1][:1]))
+        hold = [part[0] for part in there[i + 1 :] + asks[i + 2 :]] + sent[i + 2 :]
         hold += [part[1][0] for part in done[-1:]]
         hold += [block for part in done[-2:-1] for block in part[1][1:]]
-        if i == 0:
-            hold += [part[0] for part in asks[1:]]
         if i + 1 == count and count > 2:
             early = place(done[:-1], group_width, total_width)
             hold.append(early)
-        pieces = asks[i] if i + 1 < count else []
         outs = attend(
-            plan, *there[i], keep_mask, pieces, hold, groups, firsts[i], heads, tile_count
+            plan, *there[i], keep_mask, asks[i], hold, groups, firsts[i], heads, tile_count
         )
         back = [outs[0]] + [turn(outs[shift], groups - shift) for shift in range(1, groups)]
         done.append((firsts[i] * head_size, back))

time: 330 us -> 335 us (1.015)
  the two profiles are of different devices: /device:TPU:2 before, /device:TPU:4 now
where the time goes in v6:
time: 335 us; the launch traced here: 332 us
  waiting for transfers between devices  128 us (38%)
  starting transfers between devices  103 us (31%)
  Pallas kernels  89.6 us (27%)
  local copies, waits for them, and re-layouts  9.68 us (3%)
    all_to_all x4, waiting for transfers between devices, arrive(): own = lax.all_to_all(parts, 'head', split_axis=0, concat_axis=0, tiled=True)  70.4 us
    pallas_call x4, Pallas kernels, attend(): pl.pallas_call(functools.partial(attend_kernel, groups, heads, first_head...  68 us
    ppermute x24, waiting for transfers between devices, turn(): lax.ppermute(array, 'head', [(i, (i + shift) % groups) for i in range(gro...  58 us
    ppermute x24, starting transfers between devices, turn(): lax.ppermute(array, 'head', [(i, (i + shift) % groups) for i in range(gro...  54.7 us
    all_to_all x4, starting transfers between devices, arrive(): own = lax.all_to_all(parts, 'head', split_axis=0, concat_axis=0, tiled=True)  22.7 us
    ppermute x4, starting transfers between devices, arrive(): lax.ppermute(own, 'seq', backward)  18.2 us
    pallas_call x4, Pallas kernels, pack(): pl.pallas_call(kernel, in_specs=[ANY] * (len(arrays) + len(after)), out_s...  9.23 us
    unnamed x57, local copies, waits for them, and re-layouts  8.97 us
  transfers between devices with their start and end apart: 36, of which 11 were waited for; matrix products, arithmetic and copies ran while one was open for 1% of the time, Pallas kernels for 26%

profile of v6, /device:TPU:4, one launch (start us, length us, event | category | flops | bytes accessed | tf_op | source)
XLA Modules:
  0.0 331.7 jit_solution(16195620343274612181)
XLA Ops:
  0.0 2.4 pack.4.refs_2_.refs_1_
  2.4 4.9 %all-to-all-start = ((bf16[4,288,768]{2,1,0:T(8,128)(2,1)}), bf16[4,288,768]{2,1,0:T(8,128)(2,1)S(1)}, u32[]{:S(2)}, u32[]{:S(2)}) async-start(bf16[4,288,768]{2,1,0:T(8,128)(2,1)} %pack.4.refs_2_.refs_1_), calls=%async_computation | async-start | bytes 3538944 | tf_op jit(solution)/shard_map/all_to_all | solution.py:334
  7.3 2.4 pack.6.refs_0_
  9.7 38.7 %all-to-all-done = bf16[4,288,768]{2,1,0:T(8,128)(2,1)S(1)} async-done(((bf16[4,288,768]{2,1,0:T(8,128)(2,1)}), bf16[4,288,768]{2,1,0:T(8,128)(2,1)S(1)}, u32[]{:S(2)}, u32[]{:S(2)}) %all-to-all-start) | async-done | bytes 1769504 | tf_op jit(solution)/shard_map/all_to_all | solution.py:334
  49.7 3.7 %all-to-all-start.1 = ((bf16[4,288,768]{2,1,0:T(8,128)(2,1)}), bf16[4,288,768]{2,1,0:T(8,128)(2,1)S(1)}, u32[]{:S(2)}, u32[]{:S(2)}) async-start(bf16[4,288,768]{2,1,0:T(8,128)(2,1)} %gate.5), calls=%async_computation.1 | async-start | bytes 3538944 | tf_op jit(solution)/shard_map/all_to_all | solution.py:334
  55.3 4.5 %collective-permute-start.1 = (bf16[1152,768]{1,0:T(8,128)(2,1)S(1)}, bf16[1152,768]{1,0:T(8,128)(2,1)}, u32[]{:S(2)}, u32[]{:S(2)}) collective-permute-start(bf16[1152,768]{1,0:T(8,128)(2,1)S(1)} %bitcast.23), channel_id=1, source_target_pairs={{4,0},{8,4},{12,8},{16,12},{20,16},{24,20},{28,24},{5,1},{9,5},{13... | collective-permute-start | bytes 5308424 | tf_op jit(solution)/shard_map/ppermute | solution.py:337
  59.9 2.5 pack.5.refs_0_
  62.4 31.7 %all-to-all-done.1 = bf16[4,288,768]{2,1,0:T(8,128)(2,1)S(1)} async-done(((bf16[4,288,768]{2,1,0:T(8,128)(2,1)}), bf16[4,288,768]{2,1,0:T(8,128)(2,1)S(1)}, u32[]{:S(2)}, u32[]{:S(2)}) %all-to-all-start.1) | async-done | bytes 1769504 | tf_op jit(solution)/shard_map/all_to_all | solution.py:334
  95.3 3.6 %all-to-all-start.2 = ((bf16[4,288,768]{2,1,0:T(8,128)(2,1)}), bf16[4,288,768]{2,1,0:T(8,128)(2,1)S(1)}, u32[]{:S(2)}, u32[]{:S(2)}) async-start(bf16[4,288,768]{2,1,0:T(8,128)(2,1)} %gate.6.refs_11_), calls=%async_computation.2 | async-start | bytes 3538944 | tf_op jit(solution)/shard_map/all_to_all | solution.py:334
  98.9 2.1 pack_turned.4
  103.0 2.4 collective-permute-start.3
  113.6 24.3 %collective-permute-done.2.refs_6_ = bf16[288,384]{1,0:T(8,128)(2,1)} collective-permute-done((bf16[288,384]{1,0:T(8,128)(2,1)}, bf16[288,384]{1,0:T(8,128)(2,1)}, u32[]{:S(2)}, u32[]{:S(2)}) %collective-permute-start.2) | collective-permute-done | bytes 221216 | tf_op jit(solution)/shard_map/ppermute | solution.py:316
  137.9 16.6 %collective-permute-start.12 = (bf16[288,384]{1,0:T(8,128)(2,1)}, bf16[288,384]{1,0:T(8,128)(2,1)}, u32[]{:S(2)}, u32[]{:S(2)}) collective-permute-start(bf16[288,384]{1,0:T(8,128)(2,1)} %get-tuple-element.47), channel_id=1, source_target_pairs={{0,1},{1,2},{2,3},{3,0},{4,5},{5,6},{6,7},{7,4},{8,9},{9,10},{10,1... | collective-permute-start | bytes 663560 | tf_op jit(solution)/shard_map/ppermute | solution.py:316
  154.5 7.6 %collective-permute-done.3.refs_7_ = bf16[288,384]{1,0:T(8,128)(2,1)} collective-permute-done((bf16[288,384]{1,0:T(8,128)(2,1)}, bf16[288,384]{1,0:T(8,128)(2,1)}, u32[]{:S(2)}, u32[]{:S(2)}) %collective-permute-start.3) | collective-permute-done | bytes 221216 | tf_op jit(solution)/shard_map/ppermute | solution.py:316
  164.1 4.5 %collective-permute-start.11 = (bf16[1152,768]{1,0:T(8,128)(2,1)}, bf16[1152,768]{1,0:T(8,128)(2,1)}, u32[]{:S(2)}, u32[]{:S(2)}) collective-permute-start(bf16[1152,768]{1,0:T(8,128)(2,1)} %bitcast.27), channel_id=1, source_target_pairs={{4,0},{8,4},{12,8},{16,12},{20,16},{24,20},{28,24},{5,1},{9,5},{13... | collective-permute-start | bytes 5308424 | tf_op jit(solution)/shard_map/ppermute | solution.py:337
  168.6 19.2 %attend.4 = (bf16[288,384]{1,0:T(8,128)(2,1)}, bf16[288,384]{1,0:T(8,128)(2,1)}, bf16[288,384]{1,0:T(8,128)(2,1)}, bf16[288,384]{1,0:T(8,128)(2,1)}) custom-call(s32[12]{0:T(128)} %reshape.15.refs_0_, bf16[1152,768]{1,0:T(8,128)(2,1)} %bitcast.21, bf16[1152,768]{1,0:T(8,128)(2,1)} %collective-permute-done.refs_2_, ...), custom_call_target="tpu_custom_call" | custom-call | flops 24461180928 | bytes 7077888 | tf_op jit(solution)/shard_map/attend/pallas_call | solution.py:272
  192.7 10.5 %all-to-all-start.3 = ((bf16[4,288,256]{2,1,0:T(8,128)(2,1)}), bf16[4,288,256]{2,1,0:T(8,128)(2,1)S(1)}, u32[]{:S(2)}, u32[]{:S(2)}) async-start(bf16[4,288,256]{2,1,0:T(8,128)(2,1)} %gate.8.refs_11_), calls=%async_computation.3 | async-start | bytes 1179648 | tf_op jit(solution)/shard_map/all_to_all | solution.py:334
  203.2 3.8 %collective-permute-start.15 = (bf16[288,384]{1,0:T(8,128)(2,1)S(1)}, bf16[288,384]{1,0:T(8,128)(2,1)S(1)}, u32[]{:S(2)}, u32[]{:S(2)}) collective-permute-start(bf16[288,384]{1,0:T(8,128)(2,1)S(1)} %copy-done.23), channel_id=1, source_target_pairs={{0,3},{1,0},{2,1},{3,2},{4,7},{5,4},{6,5},{7,6},{8,11},{9,8},{10,9... | collective-permute-start | bytes 663560 | tf_op jit(solution)/shard_map/ppermute | solution.py:316
  210.1 4.5 %collective-permute-start.6 = (bf16[1152,768]{1,0:T(8,128)(2,1)S(1)}, bf16[1152,768]{1,0:T(8,128)(2,1)}, u32[]{:S(2)}, u32[]{:S(2)}) collective-permute-start(bf16[1152,768]{1,0:T(8,128)(2,1)S(1)} %bitcast.17), channel_id=1, source_target_pairs={{4,0},{8,4},{12,8},{16,12},{20,16},{24,20},{28,24},{5,1},{9,5},{13... | collective-permute-start | bytes 5308424 | tf_op jit(solution)/shard_map/ppermute | solution.py:337
  214.7 19.2 %attend.5 = (bf16[288,384]{1,0:T(8,128)(2,1)}, bf16[288,384]{1,0:T(8,128)(2,1)}, bf16[288,384]{1,0:T(8,128)(2,1)}, bf16[288,384]{1,0:T(8,128)(2,1)}) custom-call(s32[12]{0:T(128)} %reshape.15.refs_0_, bf16[1152,768]{1,0:T(8,128)(2,1)} %bitcast.30, bf16[1152,768]{1,0:T(8,128)(2,1)} %collective-permute-done.10.refs_2_, ...), custom_call_target="tpu_custom_call" | custom-call | flops 24461180928 | bytes 7077888 | tf_op jit(solution)/shard_map/attend/pallas_call | solution.py:272
  233.9 3.5 %collective-permute-start.26 = (bf16[288,384]{1,0:T(8,128)(2,1)}, bf16[288,384]{1,0:T(8,128)(2,1)S(1)}, u32[]{:S(2)}, u32[]{:S(2)}) collective-permute-start(bf16[288,384]{1,0:T(8,128)(2,1)} %get-tuple-element.62), channel_id=1, source_target_pairs={{0,3},{1,0},{2,1},{3,2},{4,7},{5,4},{6,5},{7,6},{8,11},{9,8},{10,9... | collective-permute-start | bytes 663560 | tf_op jit(solution)/shard_map/ppermute | solution.py:316
  240.5 6.0 %collective-permute-done.26.refs_5_.refs_10_ = bf16[288,384]{1,0:T(8,128)(2,1)S(1)} collective-permute-done((bf16[288,384]{1,0:T(8,128)(2,1)}, bf16[288,384]{1,0:T(8,128)(2,1)S(1)}, u32[]{:S(2)}, u32[]{:S(2)}) %collective-permute-start.26) | collective-permute-done | bytes 221216 | tf_op jit(solution)/shard_map/ppermute | solution.py:316
  246.5 9.7 %collective-permute-start.7 = (bf16[288,384]{1,0:T(8,128)(2,1)}, bf16[288,384]{1,0:T(8,128)(2,1)}, u32[]{:S(2)}, u32[]{:S(2)}) collective-permute-start(bf16[288,384]{1,0:T(8,128)(2,1)} %get-tuple-element.43), channel_id=1, source_target_pairs={{0,1},{1,2},{2,3},{3,0},{4,5},{5,6},{6,7},{7,4},{8,9},{9,10},{10,1... | collective-permute-start | bytes 663560 | tf_op jit(solution)/shard_map/ppermute | solution.py:316
  256.2 9.5 %collective-permute-done.27.refs_6_.refs_11_ = bf16[288,384]{1,0:T(8,128)(2,1)S(1)} collective-permute-done((bf16[288,384]{1,0:T(8,128)(2,1)}, bf16[288,384]{1,0:T(8,128)(2,1)S(1)}, u32[]{:S(2)}, u32[]{:S(2)}) %collective-permute-start.27) | collective-permute-done | bytes 221216 | tf_op jit(solution)/shard_map/ppermute | solution.py:316
  266.5 2.4 place.2.refs_13_.refs_8_
  278.1 4.5 %collective-permute-start.22 = (bf16[1152,256]{1,0:T(8,128)(2,1)}, bf16[1152,256]{1,0:T(8,128)(2,1)S(1)}, u32[]{:S(2)}, u32[]{:S(2)}) collective-permute-start(bf16[1152,256]{1,0:T(8,128)(2,1)} %bitcast.32), channel_id=1, source_target_pairs={{4,0},{8,4},{12,8},{16,12},{20,16},{24,20},{28,24},{5,1},{9,5},{13... | collective-permute-start | bytes 1769480 | tf_op jit(solution)/shard_map/ppermute | solution.py:337
  282.6 19.2 %attend.6 = (bf16[288,384]{1,0:T(8,128)(2,1)}, bf16[288,384]{1,0:T(8,128)(2,1)}, bf16[288,384]{1,0:T(8,128)(2,1)}, bf16[288,384]{1,0:T(8,128)(2,1)}) custom-call(s32[12]{0:T(128)} %reshape.15.refs_0_, bf16[1152,768]{1,0:T(8,128)(2,1)} %bitcast.15, bf16[1152,768]{1,0:T(8,128)(2,1)} %collective-permute-done.5.refs_2_, ...), custom_call_target="tpu_custom_call" | custom-call | flops 24461180928 | bytes 7077888 | tf_op jit(solution)/shard_map/attend/pallas_call | solution.py:272
  306.1 10.4 %attend.7 = (bf16[288,128]{1,0:T(8,128)(2,1)}, bf16[288,128]{1,0:T(8,128)(2,1)}, bf16[288,128]{1,0:T(8,128)(2,1)}, bf16[288,128]{1,0:T(8,128)(2,1)}) custom-call(s32[12]{0:T(128)} %reshape.15.refs_0_, bf16[1152,256]{1,0:T(8,128)(2,1)} %bitcast.34, bf16[1152,256]{1,0:T(8,128)(2,1)} %copy-done.20, bf16[1152,256]{1,0:T(8,128)(2,1)} %copy-done.21, ...), custom_call_target="tpu_custom_call" | custom-call | flops 8153726976 | bytes 2359296 | tf_op jit(solution)/shard_map/attend/pallas_call | solution.py:272
  316.6 2.4 collective-permute-start.29
  319.6 2.5 collective-permute-done.29.refs_5_
  324.5 4.0 %collective-permute-done.31.refs_7_ = bf16[288,128]{1,0:T(8,128)(2,1)S(1)} collective-permute-done((bf16[288,128]{1,0:T(8,128)(2,1)}, bf16[288,128]{1,0:T(8,128)(2,1)S(1)}, u32[]{:S(2)}, u32[]{:S(2)}) %collective-permute-start.31) | collective-permute-done | bytes 73760 | tf_op jit(solution)/shard_map/ppermute | solution.py:316
  329.4 2.2 place.3
  (120 shorter events, 45.4 us)
Async XLA Ops:
  2.4 46.1 %all-to-all-start = ((bf16[4,288,768]{2,1,0:T(8,128)(2,1)}), bf16[4,288,768]{2,1,0:T(8,128)(2,1)S(1)}, u32[]{:S(2)}, u32[]{:S(2)}) async-start(bf16[4,288,768]{2,1,0:T(8,128)(2,1)} %pack.4.refs_2_.refs_1_), calls=%async_computation | async-start | bytes 3538944 | tf_op jit(solution)/shard_map/all_to_all | solution.py:334
  49.7 44.4 %all-to-all-start.1 = ((bf16[4,288,768]{2,1,0:T(8,128)(2,1)}), bf16[4,288,768]{2,1,0:T(8,128)(2,1)S(1)}, u32[]{:S(2)}, u32[]{:S(2)}) async-start(bf16[4,288,768]{2,1,0:T(8,128)(2,1)} %gate.5), calls=%async_computation.1 | async-start | bytes 3538944 | tf_op jit(solution)/shard_map/all_to_all | solution.py:334
  53.4 108.7 %collective-permute-start = (bf16[1152,768]{1,0:T(8,128)(2,1)S(1)}, bf16[1152,768]{1,0:T(8,128)(2,1)}, u32[]{:S(2)}, u32[]{:S(2)}) collective-permute-start(bf16[1152,768]{1,0:T(8,128)(2,1)S(1)} %bitcast.22), channel_id=1, source_target_pairs={{0,4},{4,8},{8,12},{12,16},{16,20},{20,24},{24,28},{1,5},{5,9},{9,... | collective-permute-start | bytes 5308424 | tf_op jit(solution)/shard_map/ppermute | solution.py:337
  55.3 108.7 %collective-permute-start.1 = (bf16[1152,768]{1,0:T(8,128)(2,1)S(1)}, bf16[1152,768]{1,0:T(8,128)(2,1)}, u32[]{:S(2)}, u32[]{:S(2)}) collective-permute-start(bf16[1152,768]{1,0:T(8,128)(2,1)S(1)} %bitcast.23), channel_id=1, source_target_pairs={{4,0},{8,4},{12,8},{16,12},{20,16},{24,20},{28,24},{5,1},{9,5},{13... | collective-permute-start | bytes 5308424 | tf_op jit(solution)/shard_map/ppermute | solution.py:337
  95.3 94.5 %all-to-all-start.2 = ((bf16[4,288,768]{2,1,0:T(8,128)(2,1)}), bf16[4,288,768]{2,1,0:T(8,128)(2,1)S(1)}, u32[]{:S(2)}, u32[]{:S(2)}) async-start(bf16[4,288,768]{2,1,0:T(8,128)(2,1)} %gate.6.refs_11_), calls=%async_computation.2 | async-start | bytes 3538944 | tf_op jit(solution)/shard_map/all_to_all | solution.py:334
  101.0 36.9 %collective-permute-start.2 = (bf16[288,384]{1,0:T(8,128)(2,1)}, bf16[288,384]{1,0:T(8,128)(2,1)}, u32[]{:S(2)}, u32[]{:S(2)}) collective-permute-start(bf16[288,384]{1,0:T(8,128)(2,1)} %get-tuple-element.38), channel_id=1, source_target_pairs={{0,1},{1,2},{2,3},{3,0},{4,5},{5,6},{6,7},{7,4},{8,9},{9,10},{10,1... | collective-permute-start | bytes 663560 | tf_op jit(solution)/shard_map/ppermute | solution.py:316
  103.0 59.1 %collective-permute-start.3 = (bf16[288,384]{1,0:T(8,128)(2,1)}, bf16[288,384]{1,0:T(8,128)(2,1)}, u32[]{:S(2)}, u32[]{:S(2)}) collective-permute-start(bf16[288,384]{1,0:T(8,128)(2,1)} %get-tuple-element.39), channel_id=1, source_target_pairs={{0,2},{1,3},{2,0},{3,1},{4,6},{5,7},{6,4},{7,5},{8,10},{9,11},{10,... | collective-permute-start | bytes 663560 | tf_op jit(solution)/shard_map/ppermute | solution.py:316
  105.4 56.8 %collective-permute-start.4 = (bf16[288,384]{1,0:T(8,128)(2,1)}, bf16[288,384]{1,0:T(8,128)(2,1)}, u32[]{:S(2)}, u32[]{:S(2)}) collective-permute-start(bf16[288,384]{1,0:T(8,128)(2,1)} %get-tuple-element.40), channel_id=1, source_target_pairs={{0,3},{1,0},{2,1},{3,2},{4,7},{5,4},{6,5},{7,6},{8,11},{9,8},{10,9... | collective-permute-start | bytes 663560 | tf_op jit(solution)/shard_map/ppermute | solution.py:316
  137.9 65.4 %collective-permute-start.12 = (bf16[288,384]{1,0:T(8,128)(2,1)}, bf16[288,384]{1,0:T(8,128)(2,1)}, u32[]{:S(2)}, u32[]{:S(2)}) collective-permute-start(bf16[288,384]{1,0:T(8,128)(2,1)} %get-tuple-element.47), channel_id=1, source_target_pairs={{0,1},{1,2},{2,3},{3,0},{4,5},{5,6},{6,7},{7,4},{8,9},{9,10},{10,1... | collective-permute-start | bytes 663560 | tf_op jit(solution)/shard_map/ppermute | solution.py:316
  162.1 45.0 %collective-permute-start.13 = (bf16[288,384]{1,0:T(8,128)(2,1)}, bf16[288,384]{1,0:T(8,128)(2,1)}, u32[]{:S(2)}, u32[]{:S(2)}) collective-permute-start(bf16[288,384]{1,0:T(8,128)(2,1)} %get-tuple-element.48), channel_id=1, source_target_pairs={{0,2},{1,3},{2,0},{3,1},{4,6},{5,7},{6,4},{7,5},{8,10},{9,11},{10,... | collective-permute-start | bytes 663560 | tf_op jit(solution)/shard_map/ppermute | solution.py:316
  162.1 45.0 %collective-permute-start.14 = (bf16[288,384]{1,0:T(8,128)(2,1)}, bf16[288,384]{1,0:T(8,128)(2,1)}, u32[]{:S(2)}, u32[]{:S(2)}) collective-permute-start(bf16[288,384]{1,0:T(8,128)(2,1)} %get-tuple-element.49), channel_id=1, source_target_pairs={{0,3},{1,0},{2,1},{3,2},{4,7},{5,4},{6,5},{7,6},{8,11},{9,8},{10,9... | collective-permute-start | bytes 663560 | tf_op jit(solution)/shard_map/ppermute | solution.py:316
  162.1 46.1 %collective-permute-start.10 = (bf16[1152,768]{1,0:T(8,128)(2,1)}, bf16[1152,768]{1,0:T(8,128)(2,1)}, u32[]{:S(2)}, u32[]{:S(2)}) collective-permute-start(bf16[1152,768]{1,0:T(8,128)(2,1)} %bitcast.26), channel_id=1, source_target_pairs={{0,4},{4,8},{8,12},{12,16},{16,20},{20,24},{24,28},{1,5},{5,9},{9,... | collective-permute-start | bytes 5308424 | tf_op jit(solution)/shard_map/ppermute | solution.py:337
  164.1 46.1 %collective-permute-start.11 = (bf16[1152,768]{1,0:T(8,128)(2,1)}, bf16[1152,768]{1,0:T(8,128)(2,1)}, u32[]{:S(2)}, u32[]{:S(2)}) collective-permute-start(bf16[1152,768]{1,0:T(8,128)(2,1)} %bitcast.27), channel_id=1, source_target_pairs={{4,0},{8,4},{12,8},{16,12},{20,16},{24,20},{28,24},{5,1},{9,5},{13... | collective-permute-start | bytes 5308424 | tf_op jit(solution)/shard_map/ppermute | solution.py:337
  192.7 76.2 %all-to-all-start.3 = ((bf16[4,288,256]{2,1,0:T(8,128)(2,1)}), bf16[4,288,256]{2,1,0:T(8,128)(2,1)S(1)}, u32[]{:S(2)}, u32[]{:S(2)}) async-start(bf16[4,288,256]{2,1,0:T(8,128)(2,1)} %gate.8.refs_11_), calls=%async_computation.3 | async-start | bytes 1179648 | tf_op jit(solution)/shard_map/all_to_all | solution.py:334
  203.2 30.6 %collective-permute-start.15 = (bf16[288,384]{1,0:T(8,128)(2,1)S(1)}, bf16[288,384]{1,0:T(8,128)(2,1)S(1)}, u32[]{:S(2)}, u32[]{:S(2)}) collective-permute-start(bf16[288,384]{1,0:T(8,128)(2,1)S(1)} %copy-done.23), channel_id=1, source_target_pairs={{0,3},{1,0},{2,1},{3,2},{4,7},{5,4},{6,5},{7,6},{8,11},{9,8},{10,9... | collective-permute-start | bytes 663560 | tf_op jit(solution)/shard_map/ppermute | solution.py:316
  207.1 30.4 %collective-permute-start.16 = (bf16[288,384]{1,0:T(8,128)(2,1)S(1)}, bf16[288,384]{1,0:T(8,128)(2,1)S(1)}, u32[]{:S(2)}, u32[]{:S(2)}) collective-permute-start(bf16[288,384]{1,0:T(8,128)(2,1)S(1)} %copy-done.22), channel_id=1, source_target_pairs={{0,2},{1,3},{2,0},{3,1},{4,6},{5,7},{6,4},{7,5},{8,10},{9,11},{10,... | collective-permute-start | bytes 663560 | tf_op jit(solution)/shard_map/ppermute | solution.py:316
  207.1 31.5 %collective-permute-start.17 = (bf16[288,384]{1,0:T(8,128)(2,1)}, bf16[288,384]{1,0:T(8,128)(2,1)S(1)}, u32[]{:S(2)}, u32[]{:S(2)}) collective-permute-start(bf16[288,384]{1,0:T(8,128)(2,1)} %get-tuple-element.54), channel_id=1, source_target_pairs={{0,1},{1,2},{2,3},{3,0},{4,5},{5,6},{6,7},{7,4},{8,9},{9,10},{10,1... | collective-permute-start | bytes 663560 | tf_op jit(solution)/shard_map/ppermute | solution.py:316
  208.2 67.9 %collective-permute-start.5 = (bf16[1152,768]{1,0:T(8,128)(2,1)S(1)}, bf16[1152,768]{1,0:T(8,128)(2,1)}, u32[]{:S(2)}, u32[]{:S(2)}) collective-permute-start(bf16[1152,768]{1,0:T(8,128)(2,1)S(1)} %bitcast.16), channel_id=1, source_target_pairs={{0,4},{4,8},{8,12},{12,16},{16,20},{20,24},{24,28},{1,5},{5,9},{9,... | collective-permute-start | bytes 5308424 | tf_op jit(solution)/shard_map/ppermute | solution.py:337
  210.1 67.9 %collective-permute-start.6 = (bf16[1152,768]{1,0:T(8,128)(2,1)S(1)}, bf16[1152,768]{1,0:T(8,128)(2,1)}, u32[]{:S(2)}, u32[]{:S(2)}) collective-permute-start(bf16[1152,768]{1,0:T(8,128)(2,1)S(1)} %bitcast.17), channel_id=1, source_target_pairs={{4,0},{8,4},{12,8},{16,12},{20,16},{24,20},{28,24},{5,1},{9,5},{13... | collective-permute-start | bytes 5308424 | tf_op jit(solution)/shard_map/ppermute | solution.py:337
  233.9 12.6 %collective-permute-start.26 = (bf16[288,384]{1,0:T(8,128)(2,1)}, bf16[288,384]{1,0:T(8,128)(2,1)S(1)}, u32[]{:S(2)}, u32[]{:S(2)}) collective-permute-start(bf16[288,384]{1,0:T(8,128)(2,1)} %get-tuple-element.62), channel_id=1, source_target_pairs={{0,3},{1,0},{2,1},{3,2},{4,7},{5,4},{6,5},{7,6},{8,11},{9,8},{10,9... | collective-permute-start | bytes 663560 | tf_op jit(solution)/shard_map/ppermute | solution.py:316
  237.5 28.3 %collective-permute-start.27 = (bf16[288,384]{1,0:T(8,128)(2,1)}, bf16[288,384]{1,0:T(8,128)(2,1)S(1)}, u32[]{:S(2)}, u32[]{:S(2)}) collective-permute-start(bf16[288,384]{1,0:T(8,128)(2,1)} %get-tuple-element.63), channel_id=1, source_target_pairs={{0,2},{1,3},{2,0},{3,1},{4,6},{5,7},{6,4},{7,5},{8,10},{9,11},{10,... | collective-permute-start | bytes 663560 | tf_op jit(solution)/shard_map/ppermute | solution.py:316
  238.6 27.1 %collective-permute-start.28 = (bf16[288,384]{1,0:T(8,128)(2,1)}, bf16[288,384]{1,0:T(8,128)(2,1)S(1)}, u32[]{:S(2)}, u32[]{:S(2)}) collective-permute-start(bf16[288,384]{1,0:T(8,128)(2,1)} %get-tuple-element.64), channel_id=1, source_target_pairs={{0,1},{1,2},{2,3},{3,0},{4,5},{5,6},{6,7},{7,4},{8,9},{9,10},{10,1... | collective-permute-start | bytes 663560 | tf_op jit(solution)/shard_map/ppermute | solution.py:316
  246.5 23.3 %collective-permute-start.7 = (bf16[288,384]{1,0:T(8,128)(2,1)}, bf16[288,384]{1,0:T(8,128)(2,1)}, u32[]{:S(2)}, u32[]{:S(2)}) collective-permute-start(bf16[288,384]{1,0:T(8,128)(2,1)} %get-tuple-element.43), channel_id=1, source_target_pairs={{0,1},{1,2},{2,3},{3,0},{4,5},{5,6},{6,7},{7,4},{8,9},{9,10},{10,1... | collective-permute-start | bytes 663560 | tf_op jit(solution)/shard_map/ppermute | solution.py:316
  265.7 8.7 %collective-permute-start.9 = (bf16[288,384]{1,0:T(8,128)(2,1)}, bf16[288,384]{1,0:T(8,128)(2,1)}, u32[]{:S(2)}, u32[]{:S(2)}) collective-permute-start(bf16[288,384]{1,0:T(8,128)(2,1)} %get-tuple-element.45), channel_id=1, source_target_pairs={{0,3},{1,0},{2,1},{3,2},{4,7},{5,4},{6,5},{7,6},{8,11},{9,8},{10,9... | collective-permute-start | bytes 663560 | tf_op jit(solution)/shard_map/ppermute | solution.py:316
  269.7 32.1 %collective-permute-start.23 = (bf16[288,128]{1,0:T(8,128)(2,1)}, bf16[288,128]{1,0:T(8,128)(2,1)S(1)}, u32[]{:S(2)}, u32[]{:S(2)}) collective-permute-start(bf16[288,128]{1,0:T(8,128)(2,1)} %get-tuple-element.59), channel_id=1, source_target_pairs={{0,1},{1,2},{2,3},{3,0},{4,5},{5,6},{6,7},{7,4},{8,9},{9,10},{10,1... | collective-permute-start | bytes 221192 | tf_op jit(solution)/shard_map/ppermute | solution.py:316
  273.0 30.2 %collective-permute-start.24 = (bf16[288,128]{1,0:T(8,128)(2,1)}, bf16[288,128]{1,0:T(8,128)(2,1)S(1)}, u32[]{:S(2)}, u32[]{:S(2)}) collective-permute-start(bf16[288,128]{1,0:T(8,128)(2,1)} %get-tuple-element.60), channel_id=1, source_target_pairs={{0,2},{1,3},{2,0},{3,1},{4,6},{5,7},{6,4},{7,5},{8,10},{9,11},{10,... | collective-permute-start | bytes 221192 | tf_op jit(solution)/shard_map/ppermute | solution.py:316
  274.4 29.3 %collective-permute-start.25 = (bf16[288,128]{1,0:T(8,128)(2,1)S(1)}, bf16[288,128]{1,0:T(8,128)(2,1)S(1)}, u32[]{:S(2)}, u32[]{:S(2)}) collective-permute-start(bf16[288,128]{1,0:T(8,128)(2,1)S(1)} %copy-done.24), channel_id=1, source_target_pairs={{0,3},{1,0},{2,1},{3,2},{4,7},{5,4},{6,5},{7,6},{8,11},{9,8},{10,9... | collective-permute-start | bytes 221192 | tf_op jit(solution)/shard_map/ppermute | solution.py:316
  276.1 29.0 %collective-permute-start.21 = (bf16[1152,256]{1,0:T(8,128)(2,1)}, bf16[1152,256]{1,0:T(8,128)(2,1)S(1)}, u32[]{:S(2)}, u32[]{:S(2)}) collective-permute-start(bf16[1152,256]{1,0:T(8,128)(2,1)} %bitcast.31), channel_id=1, source_target_pairs={{0,4},{4,8},{8,12},{12,16},{16,20},{20,24},{24,28},{1,5},{5,9},{9,... | collective-permute-start | bytes 1769480 | tf_op jit(solution)/shard_map/ppermute | solution.py:337
  278.1 27.0 %collective-permute-start.22 = (bf16[1152,256]{1,0:T(8,128)(2,1)}, bf16[1152,256]{1,0:T(8,128)(2,1)S(1)}, u32[]{:S(2)}, u32[]{:S(2)}) collective-permute-start(bf16[1152,256]{1,0:T(8,128)(2,1)} %bitcast.32), channel_id=1, source_target_pairs={{4,0},{8,4},{12,8},{16,12},{20,16},{24,20},{28,24},{5,1},{9,5},{13... | collective-permute-start | bytes 1769480 | tf_op jit(solution)/shard_map/ppermute | solution.py:337
  301.8 26.6 %collective-permute-start.18 = (bf16[288,384]{1,0:T(8,128)(2,1)}, bf16[288,384]{1,0:T(8,128)(2,1)S(1)}, u32[]{:S(2)}, u32[]{:S(2)}) collective-permute-start(bf16[288,384]{1,0:T(8,128)(2,1)} %get-tuple-element.56), channel_id=1, source_target_pairs={{0,3},{1,0},{2,1},{3,2},{4,7},{5,4},{6,5},{7,6},{8,11},{9,8},{10,9... | collective-permute-start | bytes 663560 | tf_op jit(solution)/shard_map/ppermute | solution.py:316
  303.1 25.4 %collective-permute-start.19 = (bf16[288,384]{1,0:T(8,128)(2,1)}, bf16[288,384]{1,0:T(8,128)(2,1)S(1)}, u32[]{:S(2)}, u32[]{:S(2)}) collective-permute-start(bf16[288,384]{1,0:T(8,128)(2,1)} %get-tuple-element.57), channel_id=1, source_target_pairs={{0,2},{1,3},{2,0},{3,1},{4,6},{5,7},{6,4},{7,5},{8,10},{9,11},{10,... | collective-permute-start | bytes 663560 | tf_op jit(solution)/shard_map/ppermute | solution.py:316
  303.7 24.8 %collective-permute-start.20 = (bf16[288,384]{1,0:T(8,128)(2,1)}, bf16[288,384]{1,0:T(8,128)(2,1)S(1)}, u32[]{:S(2)}, u32[]{:S(2)}) collective-permute-start(bf16[288,384]{1,0:T(8,128)(2,1)} %get-tuple-element.58), channel_id=1, source_target_pairs={{0,1},{1,2},{2,3},{3,0},{4,5},{5,6},{6,7},{7,4},{8,9},{9,10},{10,1... | collective-permute-start | bytes 663560 | tf_op jit(solution)/shard_map/ppermute | solution.py:316
  (32 other events, 227.6 us)
